TPU v7x, 32 devices: a whole 2x2x4 slice. The times are simulated.
32 devices in a mesh: freq: 2 (over x), strip: 16 (over z, y, core).
Axes of the slice: x: 2, y: 2, z: 4, core: 2. Of those that a mesh axis runs over, the one named last changes fastest.
Arguments:
- source_field: float32 [2, 4, 1024, 1024], P(None, 'freq', 'strip'), may hold values from -6 to 6
- receiver_field: float32 [2, 4, 1024, 1024], P(None, 'freq', 'strip'), may hold values from -6 to 6
- velocity: float32 [2, 1024, 1024], P('freq', 'strip'), may hold values from 0.625 to 1.6
- slice_owner: int32 [2], replicated, may hold values from 0 to 1, each once
Outputs:
- depth_image: float32 [2, 1024, 1024], P(None, 'strip', 'freq')
- source_out: float32 [2, 4, 1024, 1024], P(None, 'freq', 'strip')
- receiver_out: float32 [2, 4, 1024, 1024], P(None, 'freq', 'strip')
Inputs may be any that keep to these rules, and one draw needn't show every extreme that they name: A permutation of the 2 velocity slices; depth step d reads slice slice_owner[d], which index slice_owner[d] // 1 of freq holds.
All inputs are finite; a program needn't handle non-finite values.
Results may differ from a plain program's by a relative error of at most 0.00011.
Values sent between devices are 32-bit elements; how exact they have to be, the bound alone decides.
No kernel may reach another device: no remote copies, remote signals or barrier semaphores. Data moves between devices by JAX's collectives and lax.ppermute only.
A program may use at most 128 MiB of HBM per device.

v0:
```python
import math

import jax
import jax.numpy as jnp
from jax import lax
from jax.sharding import PartitionSpec as P

DEPTHS = 2


step_length = 0.15
omega_top = 1.2
stencil_gain = 0.05
stencil_damping = 0.1


def with_halo(cells, sides, width):
    for axis, dim in sides:
        count = lax.axis_size(axis)
        ends = count - 1
        head = lax.slice_in_dim(cells, 0, width, axis=dim)
        tail = lax.slice_in_dim(cells, cells.shape[dim] - width, cells.shape[dim], axis=dim)
        cells = jnp.concatenate(
            [
                lax.ppermute(tail, axis, [(i, (i + 1) % count) for i in range(ends)]),
                cells,
                lax.ppermute(head, axis, [((i + 1) % count, i) for i in range(ends)]),
            ],
            axis=dim,
        )
    return cells


def spread(value, axis, root):
    mine = lax.axis_index(axis) == root
    return lax.psum(jnp.where(mine, value, jnp.zeros_like(value)), axis)


def unit_table(position, period, sign_value):
    phase = position.astype(jnp.float32) * (2.0 * math.pi / period)
    return (jnp.cos(phase), sign_value * jnp.sin(phase))


def tables(length, sign_value):
    big_factor = min(length, 128)
    small_factor = length // big_factor
    big_index = jnp.arange(big_factor, dtype=jnp.int32)
    small_index = jnp.arange(small_factor, dtype=jnp.int32)
    table_big = unit_table(
        big_index[:, None] * big_index[None, :] % big_factor, big_factor, sign_value
    )
    twiddle = unit_table(small_index[:, None] * big_index[None, :] % length, length, sign_value)
    table_small = unit_table(
        small_index[:, None] * small_index[None, :] % small_factor, small_factor, sign_value
    )
    return (big_factor, small_factor, table_big, twiddle, table_small)


def contract(pattern, left_pair, right_pair):

    def single(left_side, right_side):
        return jnp.einsum(
            pattern,
            left_side,
            right_side,
            precision=lax.Precision.HIGHEST,
            preferred_element_type=jnp.float32,
        )

    real_part = single(left_pair[0], right_pair[0]) - single(left_pair[1], right_pair[1])
    imag_part = single(left_pair[0], right_pair[1]) + single(left_pair[1], right_pair[0])
    return (real_part, imag_part)


def complex_times(left_pair, right_pair):
    return (
        left_pair[0] * right_pair[0] - left_pair[1] * right_pair[1],
        left_pair[0] * right_pair[1] + left_pair[1] * right_pair[0],
    )


def transform_last(complex_pair, sign_value):
    length = complex_pair[0].shape[-1]
    leading = complex_pair[0].shape[:-1]
    big_factor, small_factor, table_big, twiddle, table_small = tables(length, sign_value)
    reshaped = tuple(
        (member.reshape(leading + (big_factor, small_factor)) for member in complex_pair)
    )
    sectioned = contract("...ab,ak->...bk", reshaped, table_big)
    sectioned = complex_times(sectioned, twiddle)
    sectioned = contract("...bk,bj->...jk", sectioned, table_small)
    return tuple((member.reshape(leading + (length,)) for member in sectioned))


def transform_rows(complex_pair, sign_value):
    length = complex_pair[0].shape[-2]
    columns = complex_pair[0].shape[-1]
    leading = complex_pair[0].shape[:-2]
    big_factor, small_factor, table_big, twiddle, table_small = tables(length, sign_value)
    reshaped = tuple(
        (member.reshape(leading + (big_factor, small_factor, columns)) for member in complex_pair)
    )
    sectioned = contract("...abl,ak->...bkl", reshaped, table_big)
    sectioned = complex_times(sectioned, (twiddle[0][:, :, None], twiddle[1][:, :, None]))
    sectioned = contract("...bkl,bj->...jkl", sectioned, table_small)
    return tuple((member.reshape(leading + (length, columns)) for member in sectioned))


def centered(position, length):
    shifted = jnp.where(position < length // 2, position, position - length)
    return shifted.astype(jnp.float32) * (2.0 * math.pi / length)


def lateral_shift(complex_pair, transfer):
    spectral = transform_last(complex_pair, -1.0)
    columns_pair = lax.all_to_all(spectral, "strip", split_axis=3, concat_axis=2, tiled=True)
    columns_pair = transform_rows(columns_pair, -1.0)
    columns_pair = complex_times(columns_pair, transfer)
    columns_pair = transform_rows(columns_pair, 1.0)
    rows_pair = lax.all_to_all(columns_pair, "strip", split_axis=2, concat_axis=3, tiled=True)
    return transform_last(rows_pair, 1.0)


def stencil_step(complex_pair, weight, field_signs):
    stacked = jnp.stack([complex_pair[0], complex_pair[1]])
    padded = with_halo(stacked, (("strip", 3),), 1)
    center = padded[:, :, :, 1:-1, :]
    beside = padded[:, :, :, 2:, :] + padded[:, :, :, :-2, :]
    upper = jnp.pad(center[..., 1:], ((0, 0), (0, 0), (0, 0), (0, 0), (0, 1)))
    lower = jnp.pad(center[..., :-1], ((0, 0), (0, 0), (0, 0), (0, 0), (1, 0)))
    laplace_all = beside + upper + lower - 4.0 * center
    real_part = complex_pair[0] + weight * (
        stencil_damping * laplace_all[0] - field_signs * laplace_all[1]
    )
    imag_part = complex_pair[1] + weight * (
        stencil_damping * laplace_all[1] + field_signs * laplace_all[0]
    )
    return (real_part, imag_part)


def fetch_slice(velocity, slot_number):
    slot_count = velocity.shape[0]
    local_slice = lax.dynamic_index_in_dim(velocity, slot_number % slot_count, 0, keepdims=False)
    return spread(local_slice, "freq", slot_number // slot_count)


def local(source_field, receiver_field, velocity, slice_owner):
    freq_local = source_field.shape[1]
    rows_local = source_field.shape[2]
    width_y = source_field.shape[3]
    strip_count = lax.axis_size("strip")
    columns_local = width_y // strip_count
    width_x = rows_local * strip_count
    freq_total = freq_local * lax.axis_size("freq")
    freq_number = lax.axis_index("freq") * freq_local + jnp.arange(freq_local, dtype=jnp.int32)
    angular = (omega_top * (freq_number + 1).astype(jnp.float32) / freq_total)[:, None, None]
    wave_x = centered(jnp.arange(width_x, dtype=jnp.int32), width_x)
    wave_y = centered(
        lax.axis_index("strip") * columns_local + jnp.arange(columns_local, dtype=jnp.int32),
        width_y,
    )
    argument = (
        angular * angular
        - (wave_x[:, None] * wave_x[:, None] + wave_y[None, :] * wave_y[None, :])[None]
    )
    radius = jnp.sqrt(jnp.abs(argument))
    travel = argument >= 0.0
    norm_scale = 1.0 / (width_x * width_y)
    field_signs = jnp.array([-1.0, 1.0], jnp.float32)[:, None, None, None]
    trans_real = (
        jnp.where(travel, jnp.cos(step_length * radius), jnp.exp(-step_length * radius))
        * norm_scale
    )[None]
    trans_imag = (
        field_signs
        * (jnp.where(travel, jnp.sin(step_length * radius), jnp.zeros_like(radius)) * norm_scale)[
            None
        ]
    )
    transfer = (trans_real, trans_imag)
    real_part = jnp.stack([source_field[0], receiver_field[0]])
    imag_part = jnp.stack([source_field[1], receiver_field[1]])
    image_terms = []
    for depth_step in range(DEPTHS):
        speed = fetch_slice(velocity, slice_owner[depth_step])
        real_part, imag_part = lateral_shift((real_part, imag_part), transfer)
        phase = field_signs * (angular * step_length * (1.0 / speed - 1.0)[None])[None]
        cosine = jnp.cos(phase)
        sine = jnp.sin(phase)
        real_part, imag_part = (
            real_part * cosine - imag_part * sine,
            real_part * sine + imag_part * cosine,
        )
        weight = stencil_gain * (speed * speed - 1.0)[None] * angular / omega_top
        real_part, imag_part = stencil_step((real_part, imag_part), weight, field_signs)
        image_term = jnp.sum(real_part[0] * real_part[1] + imag_part[0] * imag_part[1], axis=0)
        image_terms.append(image_term)
    depth_image = lax.psum_scatter(jnp.stack(image_terms), "freq", scatter_dimension=2, tiled=True)
    source_out = jnp.stack([real_part[0], imag_part[0]])
    receiver_out = jnp.stack([real_part[1], imag_part[1]])
    return (depth_image, source_out, receiver_out)


def solution(mesh):
    return jax.shard_map(
        local,
        mesh=mesh,
        in_specs=(
            P(None, "freq", "strip", None),
            P(None, "freq", "strip", None),
            P("freq", "strip", None),
            P(),
        ),
        out_specs=(
            P(None, "strip", "freq"),
            P(None, "freq", "strip", None),
            P(None, "freq", "strip", None),
        ),
        check_vma=False,
    )
```

profile of v0, /device:TPU:0, one launch (start us, length us, event | category | flops | bytes accessed | tf_op | source)
XLA Modules:
  0.0 544.5 jit_solution(13190275868086972005)
XLA Ops:
  25.5 4.2 reshape.511
  29.7 7.4 %all-to-all-start = ((f32[16,1,16384]{2,1,0:T(1,128)}), f32[16,1,16384]{2,1,0:T(1,128)}, u32[]{:S(2)}, u32[]{:S(2)}) async-start(f32[16,1,16384]{2,1,0:T(1,128)} %reshape.511), calls=%async_computation | async-start | bytes 2097152 | tf_op jit(solution)/shard_map/all_to_all | solution.py:116
  42.5 3.2 reshape.513
  45.6 14.5 %all-to-all-done = f32[16,1,16384]{2,1,0:T(1,128)} async-done(((f32[16,1,16384]{2,1,0:T(1,128)}), f32[16,1,16384]{2,1,0:T(1,128)}, u32[]{:S(2)}, u32[]{:S(2)}) %all-to-all-start) | async-done | bytes 1048608 | tf_op jit(solution)/shard_map/all_to_all | solution.py:116
  60.2 7.2 %all-to-all-start.1 = ((f32[16,1,16384]{2,1,0:T(1,128)}), f32[16,1,16384]{2,1,0:T(1,128)}, u32[]{:S(2)}, u32[]{:S(2)}) async-start(f32[16,1,16384]{2,1,0:T(1,128)} %reshape.513), calls=%async_computation.1 | async-start | bytes 2097152 | tf_op jit(solution)/shard_map/all_to_all | solution.py:116
  70.2 5.3 reduce.2
  75.5 2.7 reshape.512
  78.3 3.2 copy.352
  90.3 5.3 reduce.3
  95.6 2.7 reshape.514
  98.3 2.9 copy.355
  116.0 3.7 fusion.52
  119.7 3.2 copy.276
  137.8 3.2 reshape.515
  141.0 7.0 %all-to-all-start.2 = ((f32[16,1,16384]{2,1,0:T(1,128)}), f32[16,1,16384]{2,1,0:T(1,128)}, u32[]{:S(2)}, u32[]{:S(2)}) async-start(f32[16,1,16384]{2,1,0:T(1,128)} %reshape.515), calls=%async_computation.2 | async-start | bytes 2097152 | tf_op jit(solution)/shard_map/all_to_all | solution.py:120
  157.6 3.2 reshape.517
  160.8 10.3 %all-to-all-done.2 = f32[16,1,16384]{2,1,0:T(1,128)} async-done(((f32[16,1,16384]{2,1,0:T(1,128)}), f32[16,1,16384]{2,1,0:T(1,128)}, u32[]{:S(2)}, u32[]{:S(2)}) %all-to-all-start.2) | async-done | bytes 1048608 | tf_op jit(solution)/shard_map/all_to_all | solution.py:120
  171.0 6.9 %all-to-all-start.3 = ((f32[16,1,16384]{2,1,0:T(1,128)}), f32[16,1,16384]{2,1,0:T(1,128)}, u32[]{:S(2)}, u32[]{:S(2)}) async-start(f32[16,1,16384]{2,1,0:T(1,128)} %reshape.517), calls=%async_computation.3 | async-start | bytes 2097152 | tf_op jit(solution)/shard_map/all_to_all | solution.py:120
  178.0 3.9 all-reduce.7.cloned.1.call-done
  187.7 5.3 reduce.4
  193.0 2.7 reshape.516
  195.7 2.9 copy.358
  205.3 5.3 reduce.5
  210.6 2.7 reshape.518
  213.3 3.0 copy.361
  232.0 3.2 fusion.46
  237.7 5.2 fusion.68
  244.3 3.2 collective-permute-start.1
  247.5 2.8 fusion.4
  254.2 3.1 copy.297
  257.4 3.3 copy.299
  260.7 3.1 fusion.7
  273.0 7.6 %fusion.67 = (f32[2,2,64,128,8]{3,4,2,1,0:T(8,128)S(1)}, f32[2,2,64,128,8]{3,4,2,1,0:T(8,128)S(1)}) fusion(f32[2,2,64,128,8]{3,4,2,1,0:T(8,128)} %copy.297, f32[2,2,64,128,8]{3,4,2,1,0:T(8,128)} %copy.299, f32[2,2,64,128,8]{3,4,2,1,0:T(8,128)} %copy.303, f32[2,2,64,128,8]{3,4,2,1,0:T(8,128)} %copy.305, f32[2,64,128,8]{2,3,1,0:T(8,128)} %multiply_multiply_fusion.5, ...), kind=kLoop, calls=%fused_computation.139 | loop fusion | flops 4456448 | bytes 7340040 | tf_op jit(solution)/shard_map/add | solution.py:135
  288.6 2.8 copy.362
  291.4 4.3 reshape.519
  295.7 6.3 %all-to-all-start.4 = ((f32[16,1,16384]{2,1,0:T(1,128)}), f32[16,1,16384]{2,1,0:T(1,128)}, u32[]{:S(2)}, u32[]{:S(2)}) async-start(f32[16,1,16384]{2,1,0:T(1,128)} %reshape.519), calls=%async_computation.4 | async-start | bytes 2097152 | tf_op jit(solution)/shard_map/all_to_all | solution.py:116
  307.3 3.2 reshape.521
  310.5 14.5 %all-to-all-done.4 = f32[16,1,16384]{2,1,0:T(1,128)} async-done(((f32[16,1,16384]{2,1,0:T(1,128)}), f32[16,1,16384]{2,1,0:T(1,128)}, u32[]{:S(2)}, u32[]{:S(2)}) %all-to-all-start.4) | async-done | bytes 1048608 | tf_op jit(solution)/shard_map/all_to_all | solution.py:116
  325.0 7.1 %all-to-all-start.5 = ((f32[16,1,16384]{2,1,0:T(1,128)}), f32[16,1,16384]{2,1,0:T(1,128)}, u32[]{:S(2)}, u32[]{:S(2)}) async-start(f32[16,1,16384]{2,1,0:T(1,128)} %reshape.521), calls=%async_computation.5 | async-start | bytes 2097152 | tf_op jit(solution)/shard_map/all_to_all | solution.py:116
  332.2 5.3 reduce.6
  337.5 2.7 reshape.520
  340.2 2.8 copy.364
  349.7 5.4 %all-to-all-done.5 = f32[16,1,16384]{2,1,0:T(1,128)} async-done(((f32[16,1,16384]{2,1,0:T(1,128)}), f32[16,1,16384]{2,1,0:T(1,128)}, u32[]{:S(2)}, u32[]{:S(2)}) %all-to-all-start.5) | async-done | bytes 1048608 | tf_op jit(solution)/shard_map/all_to_all | solution.py:116
  355.1 5.3 reduce.7
  363.2 3.2 copy.367
  381.1 3.7 fusion.40
  384.8 3.2 copy.326
  401.5 4.3 reshape.523
  405.8 7.3 %all-to-all-start.6 = ((f32[16,1,16384]{2,1,0:T(1,128)}), f32[16,1,16384]{2,1,0:T(1,128)}, u32[]{:S(2)}, u32[]{:S(2)}) async-start(f32[16,1,16384]{2,1,0:T(1,128)} %reshape.523), calls=%async_computation.6 | async-start | bytes 2097152 | tf_op jit(solution)/shard_map/all_to_all | solution.py:120
  419.3 3.2 reshape.525
  422.5 13.5 %all-to-all-done.6 = f32[16,1,16384]{2,1,0:T(1,128)} async-done(((f32[16,1,16384]{2,1,0:T(1,128)}), f32[16,1,16384]{2,1,0:T(1,128)}, u32[]{:S(2)}, u32[]{:S(2)}) %all-to-all-start.6) | async-done | bytes 1048608 | tf_op jit(solution)/shard_map/all_to_all | solution.py:120
  436.0 6.9 %all-to-all-start.7 = ((f32[16,1,16384]{2,1,0:T(1,128)}), f32[16,1,16384]{2,1,0:T(1,128)}, u32[]{:S(2)}, u32[]{:S(2)}) async-start(f32[16,1,16384]{2,1,0:T(1,128)} %reshape.525), calls=%async_computation.7 | async-start | bytes 2097152 | tf_op jit(solution)/shard_map/all_to_all | solution.py:120
  446.5 4.3 reduce.8
  452.3 3.2 copy.370
  462.2 3.7 all-to-all-done.7
  466.0 4.3 reduce.9
  471.8 2.9 copy.373
  484.9 3.3 fusion.34
  490.6 5.3 fusion.58
  497.3 3.1 collective-permute-start.3
  500.4 2.8 fusion
  505.9 2.9 fusion.3
  510.1 9.0 %fusion.71 = (f32[2,2,64,1024]{3,2,1,0:T(8,128)S(1)}, f32[2,2,64,1024]{3,2,1,0:T(8,128)S(1)}, f32[2,2,64,1024]{3,2,1,0:T(8,128)S(1)}, f32[2,2,64,1024]{3,2,1,0:T(8,128)S(1)}) fusion(f32[2,2,64,1024]{3,2,1,0:T(8,128)S(1)} %copy-done.23, f32[2,2,64,1024]{3,2,1,0:T(8,128)S(1)} %copy-done.22, f32[2,64,1024]{2,1,0:T(8,128)S(1)} %copy-done.35, ...), kind=kLoop, calls=%fused_computation.143 | loop fusion | flops 8912896 | bytes 14680072 | tf_op jit(solution)/shard_map/add | solution.py:132
  522.5 15.0 %reduce-scatter.2.cloned.1.call-done = f32[2,64,512]{2,1,0:T(8,128)} async-done(((f32[2,64,1024]{2,1,0:T(8,128)}), f32[2,64,512]{2,1,0:T(8,128)}) %reduce-scatter.2.cloned.1.call-update) | async-done | bytes 262160 | tf_op jit(solution)/shard_map/reduce_scatter | solution.py:198
  (233 shorter events, 208.9 us)
Async XLA Ops:
  7.2 1.5 copy-start.37
  11.2 3.4 copy-start.34
  18.9 1.2 copy-start.32
  29.7 30.4 %all-to-all-start = ((f32[16,1,16384]{2,1,0:T(1,128)}), f32[16,1,16384]{2,1,0:T(1,128)}, u32[]{:S(2)}, u32[]{:S(2)}) async-start(f32[16,1,16384]{2,1,0:T(1,128)} %reshape.511), calls=%async_computation | async-start | bytes 2097152 | tf_op jit(solution)/shard_map/all_to_all | solution.py:116
  60.2 30.2 %all-to-all-start.1 = ((f32[16,1,16384]{2,1,0:T(1,128)}), f32[16,1,16384]{2,1,0:T(1,128)}, u32[]{:S(2)}, u32[]{:S(2)}) async-start(f32[16,1,16384]{2,1,0:T(1,128)} %reshape.513), calls=%async_computation.1 | async-start | bytes 2097152 | tf_op jit(solution)/shard_map/all_to_all | solution.py:116
  101.3 2.3 copy-start.30
  103.6 1.3 copy-start.26
  122.9 2.2 copy-start.40
  130.6 1.0 copy-start.15
  130.6 2.5 copy-start.11
  137.8 10.7 %copy-start.41 = (s32[2]{0:T(128)S(1)}, s32[2]{0:T(128)}, u32[]{:S(2)}) copy-start(s32[2]{0:T(128)} %param.8) | copy-start | bytes 28
  137.8 12.6 %copy-start.39 = (f32[1,64,1024]{2,1,0:T(8,128)S(1)}, f32[1,64,1024]{2,1,0:T(8,128)}, u32[]{:S(2)}) copy-start(f32[1,64,1024]{2,1,0:T(8,128)} %param.7) | copy-start | bytes 786436
  141.0 10.3 %copy-start.16 = (f32[2,2,8,128,64]{3,4,2,1,0:T(8,128)S(1)}, f32[2,2,8,128,64]{3,4,2,1,0:T(8,128)}, u32[]{:S(2)}) copy-start(f32[2,2,8,128,64]{3,4,2,1,0:T(8,128)} %copy-done.15) | copy-start | bytes 3145732
  141.0 30.1 %all-to-all-start.2 = ((f32[16,1,16384]{2,1,0:T(1,128)}), f32[16,1,16384]{2,1,0:T(1,128)}, u32[]{:S(2)}, u32[]{:S(2)}) async-start(f32[16,1,16384]{2,1,0:T(1,128)} %reshape.515), calls=%async_computation.2 | async-start | bytes 2097152 | tf_op jit(solution)/shard_map/all_to_all | solution.py:120
  148.0 4.8 copy-start.12
  148.1 33.8 %all-reduce.7.cloned.1.call-start = ((), (), s32[]{:S(2)}) async-start(), calls=%async_computation.10 | async-start | bytes 1048576 | tf_op jit(solution)/shard_map/psum | solution.py:36
  171.0 34.2 %all-to-all-start.3 = ((f32[16,1,16384]{2,1,0:T(1,128)}), f32[16,1,16384]{2,1,0:T(1,128)}, u32[]{:S(2)}, u32[]{:S(2)}) async-start(f32[16,1,16384]{2,1,0:T(1,128)} %reshape.517), calls=%async_computation.3 | async-start | bytes 2097152 | tf_op jit(solution)/shard_map/all_to_all | solution.py:120
  178.0 7.6 %copy-start.42 = (f32[2]{0:T(128)}, f32[2]{0:T(128)S(1)}, u32[]{:S(2)}) copy-start(f32[2]{0:T(128)S(1)} %get-tuple-element.63) | copy-start | bytes 28
  218.5 1.0 copy-start.10
  219.5 2.5 copy-start.28
  235.2 2.5 copy-start.20
  235.2 2.5 copy-start.33
  242.9 4.6 copy-start.6
  242.9 4.6 copy-start.8
  243.0 17.7 %collective-permute-start = (f32[2,2,2,1,1024]{4,3,2,1,0:T(1,128)S(1)}, f32[2,2,2,1,1024]{4,3,2,1,0:T(1,128)S(1)}, u32[]{:S(2)}, u32[]{:S(2)}) collective-permute-start(f32[2,2,2,1,1024]{4,3,2,1,0:T(1,128)S(1)} %get-tuple-element.31), channel_id=1, source_target_pairs={{1,0},{2,1},{3,2},{4,3},{5,4},{6,5},{7,6},{8,7},{9,8},{10,9},{11,1... | collective-permute-start | bytes 98312 | tf_op jit(solution)/shard_map/ppermute | solution.py:27
  244.3 6.0 %copy-start.2 = (f32[2,2,64,8,128]{4,3,2,1,0:T(8,128)S(1)}, f32[2,2,64,8,128]{4,3,2,1,0:T(8,128)}, u32[]{:S(2)}) copy-start(f32[2,2,64,8,128]{4,3,2,1,0:T(8,128)} %fusion.47) | copy-start | bytes 3145732
  244.3 16.4 %collective-permute-start.1 = (f32[2,2,2,1,1024]{4,3,2,1,0:T(1,128)S(1)}, f32[2,2,2,1,1024]{4,3,2,1,0:T(1,128)S(1)}, u32[]{:S(2)}, u32[]{:S(2)}) collective-permute-start(f32[2,2,2,1,1024]{4,3,2,1,0:T(1,128)S(1)} %get-tuple-element.32), channel_id=1, source_target_pairs={{0,1},{1,2},{2,3},{3,4},{4,5},{5,6},{6,7},{7,8},{8,9},{9,10},{10,1... | collective-permute-start | bytes 98312 | tf_op jit(solution)/shard_map/ppermute | solution.py:25
  250.2 2.0 copy-start.4
  257.4 3.3 copy-start.7
  257.4 3.3 copy-start.9
  263.9 2.1 copy-start
  295.7 29.3 %all-to-all-start.4 = ((f32[16,1,16384]{2,1,0:T(1,128)}), f32[16,1,16384]{2,1,0:T(1,128)}, u32[]{:S(2)}, u32[]{:S(2)}) async-start(f32[16,1,16384]{2,1,0:T(1,128)} %reshape.519), calls=%async_computation.4 | async-start | bytes 2097152 | tf_op jit(solution)/shard_map/all_to_all | solution.py:116
  325.0 30.1 %all-to-all-start.5 = ((f32[16,1,16384]{2,1,0:T(1,128)}), f32[16,1,16384]{2,1,0:T(1,128)}, u32[]{:S(2)}, u32[]{:S(2)}) async-start(f32[16,1,16384]{2,1,0:T(1,128)} %reshape.521), calls=%async_computation.5 | async-start | bytes 2097152 | tf_op jit(solution)/shard_map/all_to_all | solution.py:116
  366.4 2.3 copy-start.31
  368.7 1.3 copy-start.25
  395.6 1.0 copy-start.17
  395.6 2.5 copy-start.13
  401.5 11.6 %copy-start.18 = (f32[2,2,8,128,64]{3,4,2,1,0:T(8,128)S(1)}, f32[2,2,8,128,64]{3,4,2,1,0:T(8,128)}, u32[]{:S(2)}) copy-start(f32[2,2,8,128,64]{3,4,2,1,0:T(8,128)} %copy-done.17) | copy-start | bytes 3145732
  405.8 8.8 %copy-start.14 = (f32[2,2,8,128,64]{3,4,2,1,0:T(8,128)S(1)}, f32[2,2,8,128,64]{3,4,2,1,0:T(8,128)}, u32[]{:S(2)}) copy-start(f32[2,2,8,128,64]{3,4,2,1,0:T(8,128)} %copy-done.13) | copy-start | bytes 3145732
  405.8 30.2 %all-to-all-start.6 = ((f32[16,1,16384]{2,1,0:T(1,128)}), f32[16,1,16384]{2,1,0:T(1,128)}, u32[]{:S(2)}, u32[]{:S(2)}) async-start(f32[16,1,16384]{2,1,0:T(1,128)} %reshape.523), calls=%async_computation.6 | async-start | bytes 2097152 | tf_op jit(solution)/shard_map/all_to_all | solution.py:120
  419.3 23.7 %copy-start.43 = (f32[2]{0:T(128)S(1)}, f32[2]{0:T(128)}, u32[]{:S(2)}) copy-start(f32[2]{0:T(128)} %copy-done.42) | copy-start | bytes 28
  422.5 20.5 %copy-start.38 = (f32[64,1024]{1,0:T(8,128)S(1)}, f32[64,1024]{1,0:T(8,128)}, u32[]{:S(2)}) copy-start(f32[64,1024]{1,0:T(8,128)} %get-tuple-element.44) | copy-start | bytes 786436
  422.5 21.7 %copy-start.3 = (f32[2,2,64,8,128]{4,3,2,1,0:T(8,128)S(1)}, f32[2,2,64,8,128]{4,3,2,1,0:T(8,128)}, u32[]{:S(2)}) copy-start(f32[2,2,64,8,128]{4,3,2,1,0:T(8,128)} %fusion.47) | copy-start | bytes 3145732
  436.0 29.9 %all-to-all-start.7 = ((f32[16,1,16384]{2,1,0:T(1,128)}), f32[16,1,16384]{2,1,0:T(1,128)}, u32[]{:S(2)}, u32[]{:S(2)}) async-start(f32[16,1,16384]{2,1,0:T(1,128)} %reshape.525), calls=%async_computation.7 | async-start | bytes 2097152 | tf_op jit(solution)/shard_map/all_to_all | solution.py:120
  443.0 2.4 copy-start.5
  443.0 94.5 %reduce-scatter.2.cloned.1.call-start = ((), (), s32[]{:S(2)}) async-start(), calls=%async_computation.9 | async-start | bytes 786432 | tf_op jit(solution)/shard_map/reduce_scatter | solution.py:198
  474.7 2.3 copy-start.29
  477.1 1.2 copy-start.27
  496.0 9.8 %collective-permute-start.2 = (f32[2,2,2,1,1024]{4,3,2,1,0:T(1,128)S(1)}, f32[2,2,2,1,1024]{4,3,2,1,0:T(1,128)S(1)}, u32[]{:S(2)}, u32[]{:S(2)}) collective-permute-start(f32[2,2,2,1,1024]{4,3,2,1,0:T(1,128)S(1)} %get-tuple-element.25), channel_id=1, source_target_pairs={{1,0},{2,1},{3,2},{4,3},{5,4},{6,5},{7,6},{8,7},{9,8},{10,9},{11,1... | collective-permute-start | bytes 98312 | tf_op jit(solution)/shard_map/ppermute | solution.py:27
  497.3 8.5 %collective-permute-start.3 = (f32[2,2,2,1,1024]{4,3,2,1,0:T(1,128)S(1)}, f32[2,2,2,1,1024]{4,3,2,1,0:T(1,128)S(1)}, u32[]{:S(2)}, u32[]{:S(2)}) collective-permute-start(f32[2,2,2,1,1024]{4,3,2,1,0:T(1,128)S(1)} %get-tuple-element.26), channel_id=1, source_target_pairs={{0,1},{1,2},{2,3},{3,4},{4,5},{5,6},{6,7},{7,8},{8,9},{9,10},{10,1... | collective-permute-start | bytes 98312 | tf_op jit(solution)/shard_map/ppermute | solution.py:25
  505.8 3.0 copy-start.1
  505.8 3.0 copy-start.19
  505.8 3.1 copy-start.21
  505.8 3.4 copy-start.22
  505.8 3.7 copy-start.23
  505.8 4.0 copy-start.24
  505.8 4.1 copy-start.35
  505.9 4.3 copy-start.36
Sparse Core Ops, SparseCore 0:
  151.8 30.0 all-reduce.6
  520.5 16.8 reduce-scatter.1
where the time goes:
time: 555 us; the launch traced here: 545 us
  local copies, waits for them, and re-layouts  173 us (31%)
  matrix products  113 us (20%)
  other arithmetic  92.9 us (17%)
  waiting for transfers between devices  83.1 us (15%)
  starting transfers between devices  65.6 us (12%)
  between operations  17 us (3%)
    dot_general x64, matrix products, single(): jnp.einsum(pattern, left_side, right_side, precision=lax.Precision.HIGHES...  113 us
    unnamed x104, local copies, waits for them, and re-layouts  53 us
    all_to_all x4, waiting for transfers between devices, lateral_shift(): lax.all_to_all(spectral, 'strip', split_axis=3, concat_axis=2, tiled=True)  36.7 us
    reshape x14, local copies, waits for them, and re-layouts, transform_last(): return tuple((member.reshape(leading + (length,)) for member in sectioned))  29 us
    all_to_all x4, starting transfers between devices, lateral_shift(): lax.all_to_all(columns_pair, 'strip', split_axis=2, concat_axis=3, tiled=...  28.2 us
    all_to_all x4, starting transfers between devices, lateral_shift(): lax.all_to_all(spectral, 'strip', split_axis=3, concat_axis=2, tiled=True)  28.1 us
    all_to_all x4, waiting for transfers between devices, lateral_shift(): lax.all_to_all(columns_pair, 'strip', split_axis=2, concat_axis=3, tiled=...  27.5 us
    all_to_all x4, other arithmetic, lateral_shift(): lax.all_to_all(spectral, 'strip', split_axis=3, concat_axis=2, tiled=True)  21.2 us
  transfers between devices with their start and end apart: 14, of which 9 were waited for; matrix products, arithmetic and copies ran while one was open for 25% of the time, Pallas kernels for 0%

commit v1 on v0

v1 whole, which is shorter than its diff:
```python
import functools
import math

import jax
import jax.numpy as jnp
import numpy as np
from jax import lax
from jax.experimental import pallas as pl
from jax.experimental.pallas import tpu as pltpu
from jax.sharding import PartitionSpec as P

DEPTHS = 2

step_length = 0.15
omega_top = 1.2
stencil_gain = 0.05
stencil_damping = 0.1

LANES = 128
ROWS = 16
VMEM_LIMIT = 56 * 1024 * 1024
F32 = jnp.float32
BF16 = jnp.bfloat16


def halves(table):
    table = np.asarray(table, np.float32)
    high = table.astype(jnp.bfloat16)
    low = (table - high.astype(np.float32)).astype(jnp.bfloat16)
    return high, low


def point_tables():
    index = np.arange(LANES)
    angle = 2.0 * np.pi * (index[:, None] * index[None, :] % LANES) / LANES
    cosine, sine = np.cos(angle), np.sin(angle)
    forward = np.block([[cosine, -sine], [sine, cosine]])
    return forward, forward.T


def twiddles(radix):
    length = radix * LANES
    angle = 2.0 * np.pi * (np.arange(radix)[:, None] * np.arange(LANES)[None, :]) / length
    return np.stack([np.cos(angle), -np.sin(angle)]).astype(np.float32)


def small_dft(real, imag, sign):
    count = len(real)
    if count == 1:
        return list(real), list(imag)
    even = small_dft(real[0::2], imag[0::2], sign)
    odd = small_dft(real[1::2], imag[1::2], sign)
    half = count // 2
    top_real, top_imag, low_real, low_imag = [], [], [], []
    for k in range(half):
        o_re, o_im = odd[0][k], odd[1][k]
        if k == 0:
            t_re, t_im = o_re, o_im
        elif 4 * k == count:
            t_re, t_im = (-o_im, o_re) if sign > 0 else (o_im, -o_re)
        elif 8 * k == count:
            h = math.sqrt(0.5)
            t_re, t_im = ((o_re - o_im) * h, (o_im + o_re) * h) if sign > 0 else ((o_re + o_im) * h, (o_im - o_re) * h)
        elif 8 * k == 3 * count:
            h = math.sqrt(0.5)
            t_re, t_im = ((-o_re - o_im) * h, (o_re - o_im) * h) if sign > 0 else ((o_im - o_re) * h, (-o_re - o_im) * h)
        else:
            w_re, w_im = math.cos(2 * math.pi * k / count), sign * math.sin(2 * math.pi * k / count)
            t_re, t_im = o_re * w_re - o_im * w_im, o_re * w_im + o_im * w_re
        top_real.append(even[0][k] + t_re)
        top_imag.append(even[1][k] + t_im)
        low_real.append(even[0][k] - t_re)
        low_imag.append(even[1][k] - t_im)
    return top_real + low_real, top_imag + low_imag


def parts(value):
    high = value.astype(BF16)
    return high, (value - high.astype(F32)).astype(BF16)


def dot(left, right):
    return jnp.dot(left, right, preferred_element_type=F32)


def dot_right(high, low, table):
    return dot(high, table[0]) + dot(low, table[0]) + dot(high, table[1])


def dot_left(both, data_high, data_low):
    size = both.shape[0] // 2
    first = dot(both[...], data_high)
    return first[:size] + first[size:] + dot(both[:size], data_low)


def lanes(k, count=1):
    return slice(k * LANES, (k + count) * LANES)


def forward_into(load, row, twist, high, low, index):
    radix = twist.shape[1]
    real, imag = zip(*[load(a) for a in range(radix)])
    real, imag = small_dft(list(real), list(imag), -1)
    for k in range(radix):
        re, im = real[k], imag[k]
        if k:
            c, s = twist[0, k : k + 1, :], twist[1, k : k + 1, :]
            re, im = re * c - im * s, re * s + im * c
        for part, value in ((0, re), (1, im)):
            h, l = parts(value)
            high[index(k) + (row, lanes(part))] = h
            low[index(k) + (row, lanes(part))] = l


def wait_all(copies):
    for copy in copies:
        copy.start()
    for copy in copies:
        copy.wait()


def copier(sems):
    made = []

    def add(source, target):
        made.append(pltpu.make_async_copy(source, target, sems.at[len(made)]))

    return made, add


def first_kernel(ids, source, receiver, table, twist, keep, send, high, low):
    z, core = ids[0], ids[2]
    groups, half = keep.shape[0], keep.shape[1]
    rows = source.shape[2]
    for e in range(groups):
        field = z ^ e
        which, number = lax.rem(field, 2), lax.div(field, 2)

        def chunk(t, carry, e=e, which=which, number=number):
            row = pl.ds(pl.multiple_of(t * ROWS, ROWS), ROWS)

            def load(a):
                return tuple(
                    jnp.where(which == 0, source[part, number, row, lanes(a)], receiver[part, number, row, lanes(a)])
                    for part in (0, 1)
                )

            forward_into(load, row, twist, high, low, lambda k: (e, k))
            return carry

        lax.fori_loop(0, rows // ROWS, chunk, 0)
        for out, start in ((keep, core * half), (send, (1 - core) * half)):
            h = high[e, pl.ds(start, half)].reshape(half * rows, 2 * LANES)
            l = low[e, pl.ds(start, half)].reshape(half * rows, 2 * LANES)
            result = dot_right(h, l, table)
            for part in (0, 1):
                out[e, :, part] = result[:, lanes(part)].reshape(half, rows, LANES)


def first_transform(ids, source, receiver, groups, tab):
    rows, width = source.shape[2:]
    radix = width // LANES
    out = jax.ShapeDtypeStruct((groups, radix // 2, 2, rows, LANES), F32)
    scratch = pltpu.VMEM((groups, radix, rows, 2 * LANES), BF16)
    return pl.pallas_call(
        first_kernel,
        out_shape=(out, out),
        in_specs=[pl.BlockSpec(memory_space=pltpu.SMEM)] + [pl.BlockSpec(memory_space=pltpu.VMEM)] * 4,
        out_specs=(pl.BlockSpec(memory_space=pltpu.VMEM),) * 2,
        scratch_shapes=[scratch, scratch],
        compiler_params=pltpu.CompilerParams(vmem_limit_bytes=VMEM_LIMIT),
        name="first_transform",
    )(ids, source, receiver, tab["right_forward"], tab["twist_y"])


def shift_columns(data, filt_re, filt_im, ahead, back, twist, high, low, line):
    blocks = data.shape[0]
    radix = twist.shape[1]
    for pair in range(0, blocks, 2):

        def fold(t, carry, pair=pair):
            off = pl.multiple_of(t * ROWS, ROWS)
            for kk in (0, 1):
                real = [data[pair + kk, 0, pl.ds(a * LANES + off, ROWS), :] for a in range(radix)]
                imag = [data[pair + kk, 1, pl.ds(a * LANES + off, ROWS), :] for a in range(radix)]
                real, imag = small_dft(real, imag, -1)
                for k in range(radix):
                    re, im = real[k], imag[k]
                    if k:
                        c, s = twist[0, k, pl.ds(off, ROWS), :], twist[1, k, pl.ds(off, ROWS), :]
                        re, im = re * c - im * s, re * s + im * c
                    for part, value in ((0, re), (1, im)):
                        h, l = parts(value)
                        high[k, pl.ds(part * LANES + off, ROWS), lanes(kk)] = h
                        low[k, pl.ds(part * LANES + off, ROWS), lanes(kk)] = l
            return carry

        lax.fori_loop(0, LANES // ROWS, fold, 0)

        def spectral(k, carry, pair=pair):
            value = dot_left(ahead, high[k], low[k])
            re, im = value[:LANES], value[LANES:]
            fr = jnp.concatenate([filt_re[pair, k], filt_re[pair + 1, k]], axis=1)
            fi = jnp.concatenate([filt_im[pair, k], filt_im[pair + 1, k]], axis=1)
            both = jnp.concatenate([re * fr - im * fi, re * fi + im * fr], axis=0)
            h, l = parts(both)
            line[k] = dot_left(back, h, l)
            return carry

        lax.fori_loop(0, radix, spectral, 0, unroll=4)

        def unfold(t, carry, pair=pair):
            off = pl.multiple_of(t * ROWS, ROWS)
            for kk in (0, 1):
                real, imag = [], []
                for k in range(radix):
                    re = line[k, pl.ds(off, ROWS), lanes(kk)]
                    im = line[k, pl.ds(LANES + off, ROWS), lanes(kk)]
                    if k:
                        c, s = twist[0, k, pl.ds(off, ROWS), :], twist[1, k, pl.ds(off, ROWS), :]
                        re, im = re * c + im * s, im * c - re * s
                    real.append(re)
                    imag.append(im)
                real, imag = small_dft(real, imag, 1)
                for a in range(radix):
                    data[pair + kk, 0, pl.ds(a * LANES + off, ROWS), :] = real[a]
                    data[pair + kk, 1, pl.ds(a * LANES + off, ROWS), :] = imag[a]
            return carry

        lax.fori_loop(0, LANES // ROWS, unfold, 0)


def enter_kernel(groups, across, rows, ids, filt_re, filt_im, ahead, back, twist, *refs):
    pieces = refs[: groups * across]
    keep, send, data, high, low, line, edge, sems = refs[groups * across :]
    z, y, core = ids[0], ids[1], ids[2]
    count = groups * across
    copies, add = copier(sems)
    for e in range(groups):
        for r in range(across):
            block = (z ^ e) * across + (y ^ r)
            for h in (0, 1):
                start = pl.multiple_of((2 * block + (core ^ h)) * rows, rows)
                add(pieces[e * across + r].at[h], data.at[:, :, pl.ds(start, rows), :])
    wait_all(copies)
    shift_columns(data, filt_re, filt_im, ahead, back, twist, high, low, line)
    total = data.shape[2]
    for i in range(count):
        for h in (0, 1):
            start = (2 * i + h) * rows
            for side, row in ((0, start - 1), (1, start + rows)):
                if 0 <= row < total:
                    edge[h, :, :, 2 * i + side : 2 * i + side + 1, :] = data[:, :, row : row + 1, :]
                else:
                    edge[h, :, :, 2 * i + side : 2 * i + side + 1, :] = jnp.zeros(data.shape[:2] + (1, LANES), F32)
    copies, add = copier(sems)
    for out, parity in ((keep, core), (send, 1 - core)):
        for i in range(count):
            start = pl.multiple_of((2 * i + parity) * rows, rows)
            add(data.at[:, :, pl.ds(start, rows), :], out.at[:, :, pl.ds(i * rows, rows), :])
        add(edge.at[parity], out.at[:, :, pl.ds(count * rows, 2 * count), :])
    wait_all(copies)


def leave_kernel(groups, across, rows, ids, filt_re, filt_im, ahead, back, twist, mine, other, *refs):
    outs = refs[: 2 * groups]
    data, high, low, line, edge, sems = refs[2 * groups :]
    z, y, core = ids[0], ids[1], ids[2]
    count = groups * across
    copies, add = copier(sems)
    for piece, parity in ((mine, core), (other, 1 - core)):
        for i in range(count):
            start = pl.multiple_of((2 * i + parity) * rows, rows)
            add(piece.at[:, :, pl.ds(i * rows, rows), :], data.at[:, :, pl.ds(start, rows), :])
    wait_all(copies)
    shift_columns(data, filt_re, filt_im, ahead, back, twist, high, low, line)
    blocks, _, total, _ = data.shape
    for b in range(2 * count):
        for side, row in ((0, b * rows - 1), (1, (b + 1) * rows)):
            for k in range(blocks):
                for part in (0, 1):
                    at = (2 * k + part) * 2 + side
                    if 0 <= row < total:
                        edge[b, at : at + 1, :] = data[k, part, row : row + 1, :]
                    else:
                        edge[b, at : at + 1, :] = jnp.zeros((1, LANES), F32)
    copies, add = copier(sems)
    for e in range(groups):
        for h in (0, 1):
            block = 2 * ((z ^ e) * across + y) + (core ^ h)
            start = pl.multiple_of(block * rows, rows)
            out = outs[2 * e + h]
            for k in range(blocks):
                for part in (0, 1):
                    add(data.at[k, part, pl.ds(start, rows), :], out.at[pl.ds((2 * k + part) * rows, rows), :])
            add(edge.at[block], out.at[pl.ds(2 * blocks * rows, 4 * blocks), :])
    wait_all(copies)


def column_scratch(half, total):
    radix = total // LANES
    return [
        pltpu.VMEM((half, 2, total, LANES), F32),
        pltpu.VMEM((radix, 2 * LANES, 2 * LANES), BF16),
        pltpu.VMEM((radix, 2 * LANES, 2 * LANES), BF16),
        pltpu.VMEM((radix, 2 * LANES, 2 * LANES), F32),
    ]


def column_specs():
    return [pl.BlockSpec(memory_space=pltpu.SMEM)] + [pl.BlockSpec(memory_space=pltpu.VMEM)] * 5


def enter_columns(ids, pieces, filt, tab, groups, across):
    _, half, _, rows, _ = pieces[0].shape
    count = groups * across
    total = 2 * count * rows
    out = jax.ShapeDtypeStruct((half, 2, count * rows + 2 * count, LANES), F32)
    return pl.pallas_call(
        functools.partial(enter_kernel, groups, across, rows),
        out_shape=(out, out),
        in_specs=column_specs() + [pl.BlockSpec(memory_space=pl.ANY)] * count,
        out_specs=(pl.BlockSpec(memory_space=pl.ANY),) * 2,
        scratch_shapes=column_scratch(half, total)
        + [pltpu.VMEM((2, half, 2, 2 * count, LANES), F32), pltpu.SemaphoreType.DMA((2 * count + 2,))],
        compiler_params=pltpu.CompilerParams(vmem_limit_bytes=VMEM_LIMIT),
        name="enter_columns",
    )(ids, *filt, tab["left_forward"], tab["left_inverse"], tab["twist_x"], *pieces)


def leave_columns(ids, mine, other, filt, tab, groups, across):
    half, _, own, _ = mine.shape
    count = groups * across
    rows = own // count
    total = 2 * own
    out = jax.ShapeDtypeStruct((2 * half * rows + 4 * half, LANES), F32)
    return pl.pallas_call(
        functools.partial(leave_kernel, groups, across, rows),
        out_shape=(out,) * (2 * groups),
        in_specs=column_specs() + [pl.BlockSpec(memory_space=pl.ANY)] * 2,
        out_specs=(pl.BlockSpec(memory_space=pl.ANY),) * (2 * groups),
        scratch_shapes=column_scratch(half, total)
        + [
            pltpu.VMEM((2 * count, 4 * half, LANES), F32),
            pltpu.SemaphoreType.DMA((max(2 * count, 2 * groups * (2 * half + 1)),)),
        ],
        compiler_params=pltpu.CompilerParams(vmem_limit_bytes=VMEM_LIMIT),
        name="leave_columns",
    )(ids, *filt, tab["left_forward"], tab["left_inverse"], tab["twist_x"], mine, other)


def inverse_rows(load, rows, table, twist, cosine, sine, store):
    radix = twist.shape[1]
    size = next(s for s in (48, 64, 80, 32, 16) if rows % s == 0)

    def chunk(t, carry):
        row = pl.ds(pl.multiple_of(t * size, ROWS), size)
        data = jnp.concatenate(
            [jnp.concatenate([load(k, 0, row), load(k, 1, row)], axis=1) for k in range(radix)], axis=0
        )
        result = dot_right(*parts(data), table)
        real, imag = [], []
        for k in range(radix):
            re = result[k * size : (k + 1) * size, lanes(0)]
            im = result[k * size : (k + 1) * size, lanes(1)]
            if k:
                c, s = twist[0, k : k + 1, :], twist[1, k : k + 1, :]
                re, im = re * c + im * s, im * c - re * s
            real.append(re)
            imag.append(im)
        real, imag = small_dft(real, imag, 1)
        for a in range(radix):
            c, s = cosine(row, lanes(a)), sine(row, lanes(a))
            store(0, row, lanes(a), real[a] * c - imag[a] * s)
            store(1, row, lanes(a), real[a] * s + imag[a] * c)
        return carry

    lax.fori_loop(0, rows // size, chunk, 0)


def laplace(center, above, below):
    rows, width = center.shape
    line = lax.broadcasted_iota(jnp.int32, center.shape, 0)
    place = lax.broadcasted_iota(jnp.int32, center.shape, 1)
    up = jnp.where(line == 0, above, pltpu.roll(center, 1, axis=0))
    down = jnp.where(line == rows - 1, below, pltpu.roll(center, rows - 1, axis=0))
    left = jnp.where(place == 0, 0.0, pltpu.roll(center, 1, axis=1))
    right = jnp.where(place == width - 1, 0.0, pltpu.roll(center, width - 1, axis=1))
    return (up + down) + (left + right) - 4.0 * center


def stencil(field, rows, halo, weight, sign):
    center = [field(part) for part in (0, 1)]
    bent = [laplace(center[part], halo(part, 0), halo(part, 1)) for part in (0, 1)]
    turn = weight * sign
    damp = weight * stencil_damping
    return (
        center[0] + damp * bent[0] - turn * bent[1],
        center[1] + damp * bent[1] + turn * bent[0],
    )


def middle_kernel(groups, across, rows, ids, back, ahead, twist, cosine, sine, weight, mine, other, keep, send, near, far, *scratch):
    data, field, fresh, high, low, sems = scratch
    z, y, core = ids[0], ids[1], ids[2]
    which = lax.rem(z, 2)
    sign = jnp.where(which == 0, -1.0, 1.0).astype(F32)
    half = mine.shape[0]
    count = groups * across
    own = count * rows
    copies, add = copier(sems)
    add(mine, data.at[pl.ds(core * half, half)])
    add(other, data.at[pl.ds((1 - core) * half, half)])
    wait_all(copies)

    def store(part, row, lane, value):
        field[part, row, lane] = value

    inverse_rows(
        lambda k, part, row: data[k, part, row, :],
        own + 2 * count,
        back,
        twist,
        lambda row, lane: cosine[row, lane],
        lambda row, lane: sine[row, lane],
        store,
    )

    def block(i, carry):
        row = pl.ds(pl.multiple_of(i * rows, rows), rows)
        new = stencil(
            lambda part: field[part, row, :],
            rows,
            lambda part, side: field[part, pl.ds(own + 2 * i + side, 1), :],
            weight[row, :],
            sign,
        )
        fresh[0, row, :] = new[0]
        fresh[1, row, :] = new[1]
        return carry

    lax.fori_loop(0, count, block, 0)

    copies, add = copier(sems)
    for out, parity in ((near, which), (far, 1 - which)):
        for t in range(groups // 2):
            start = pl.multiple_of(((parity + 2 * t) * across + y) * rows, rows)
            add(fresh.at[:, pl.ds(start, rows), :], out.at[:, t])
    for copy in copies:
        copy.start()

    def fold(t, carry):
        row = pl.ds(pl.multiple_of(t * ROWS, ROWS), ROWS)
        forward_into(lambda a: (fresh[0, row, lanes(a)], fresh[1, row, lanes(a)]), row, twist, high, low, lambda k: (k,))
        return carry

    lax.fori_loop(0, own // ROWS, fold, 0)
    for out, start in ((keep, core * half), (send, (1 - core) * half)):
        for k in range(half):
            result = dot_right(high[start + k], low[start + k], ahead)
            for part in (0, 1):
                out[k, part] = result[:, lanes(part)]
    for copy in copies:
        copy.wait()


def middle(ids, mine, other, factors, tab, groups, across):
    half, _, tall, _ = mine.shape
    count = groups * across
    own = tall - 2 * count
    rows = own // count
    radix = 2 * half
    width = radix * LANES
    out = jax.ShapeDtypeStruct((half, 2, own, LANES), F32)
    image = jax.ShapeDtypeStruct((2, groups // 2, rows, width), F32)
    vmem, hbm = pl.BlockSpec(memory_space=pltpu.VMEM), pl.BlockSpec(memory_space=pl.ANY)
    return pl.pallas_call(
        functools.partial(middle_kernel, groups, across, rows),
        out_shape=(out, out, image, image),
        in_specs=[pl.BlockSpec(memory_space=pltpu.SMEM)] + [vmem] * 6 + [hbm] * 2,
        out_specs=(vmem, vmem, hbm, hbm),
        scratch_shapes=[
            pltpu.VMEM((radix, 2, tall, LANES), F32),
            pltpu.VMEM((2, tall, width), F32),
            pltpu.VMEM((2, own, width), F32),
            pltpu.VMEM((radix, own, 2 * LANES), BF16),
            pltpu.VMEM((radix, own, 2 * LANES), BF16),
            pltpu.SemaphoreType.DMA((max(2, groups),)),
        ],
        compiler_params=pltpu.CompilerParams(vmem_limit_bytes=VMEM_LIMIT),
        name="middle",
    )(ids, tab["right_inverse"], tab["right_forward"], tab["twist_y"], *factors, mine, other)


def last_kernel(groups, rows, ids, back, twist, cosine, sine, weight, *refs):
    pieces = refs[: 2 * groups]
    source, receiver, image, data, field, halo, sems = refs[2 * groups :]
    z, core = ids[0], ids[2]
    half = data.shape[1] // 2
    copies, add = copier(sems)
    for e in range(groups):
        for h in (0, 1):
            piece = pieces[2 * e + h]
            for k in range(half):
                for part in (0, 1):
                    add(
                        piece.at[pl.ds((2 * k + part) * rows, rows), :],
                        data.at[z ^ e, (core ^ h) * half + k, part, pl.ds(0, rows), :],
                    )
            add(piece.at[pl.ds(2 * half * rows, 4 * half), :], halo.at[z ^ e, core ^ h])
    wait_all(copies)
    for g in range(groups):
        for h in (0, 1):
            for k in range(half):
                for part in (0, 1):
                    at = (2 * k + part) * 2
                    data[g, h * half + k, part, pl.ds(rows, 2), :] = halo[g, h, at : at + 2, :]
    total = jnp.zeros(image.shape, F32)
    for number in range(groups // 2):
        new = []
        for which, out in ((0, source), (1, receiver)):
            sign = 2.0 * which - 1.0

            def store(part, row, lane, value):
                field[part, row, lane] = value

            inverse_rows(
                lambda k, part, row: data[2 * number + which, k, part, row, :],
                rows + ROWS,
                back,
                twist,
                lambda row, lane: cosine[number, row, lane],
                lambda row, lane: sine[number, row, lane] * sign,
                store,
            )
            result = stencil(
                lambda part: field[part, pl.ds(0, rows), :],
                rows,
                lambda part, side: field[part, pl.ds(rows + side, 1), :],
                weight[number, pl.ds(0, rows), :],
                sign,
            )
            out[0, number] = result[0]
            out[1, number] = result[1]
        total = total + source[0, number] * receiver[0, number] + source[1, number] * receiver[1, number]
    image[...] = total


def last(ids, pieces, factors, tab, groups, rows):
    width = factors[0].shape[-1]
    radix = width // LANES
    half = radix // 2
    out = jax.ShapeDtypeStruct((2, groups // 2, rows, width), F32)
    vmem, hbm = pl.BlockSpec(memory_space=pltpu.VMEM), pl.BlockSpec(memory_space=pl.ANY)
    return pl.pallas_call(
        functools.partial(last_kernel, groups, rows),
        out_shape=(out, out, jax.ShapeDtypeStruct((rows, width), F32)),
        in_specs=[pl.BlockSpec(memory_space=pltpu.SMEM)] + [vmem] * 5 + [hbm] * (2 * groups),
        out_specs=(vmem, vmem, vmem),
        scratch_shapes=[
            pltpu.VMEM((groups, radix, 2, rows + ROWS, LANES), F32),
            pltpu.VMEM((2, rows + ROWS, width), F32),
            pltpu.VMEM((groups, 2, 4 * half, LANES), F32),
            pltpu.SemaphoreType.DMA((2 * groups * (2 * half + 1),)),
        ],
        compiler_params=pltpu.CompilerParams(vmem_limit_bytes=VMEM_LIMIT),
        name="last",
    )(ids, tab["right_inverse"], tab["twist_y"], *factors, *pieces)


def centered(position, length):
    shifted = jnp.where(position < length // 2, position, position - length)
    return shifted.astype(F32) * (2.0 * math.pi / length)


def column_filter(angular, sign, height, width, first_block, blocks):
    radix_x, radix_y = height // LANES, width // LANES
    inner = jnp.arange(LANES, dtype=jnp.int32)
    wave_x = centered(jnp.arange(radix_x, dtype=jnp.int32)[:, None] + radix_x * inner[None, :], height)
    wave_y = centered(first_block + jnp.arange(blocks, dtype=jnp.int32)[:, None] + radix_y * inner[None, :], width)
    wave_x = wave_x[None, :, :, None]
    wave_y = wave_y[:, None, None, :]
    argument = angular * angular - (wave_x * wave_x + wave_y * wave_y)
    radius = jnp.sqrt(jnp.abs(argument))
    travel = argument >= 0.0
    scale = 1.0 / (height * width)
    real = jnp.where(travel, jnp.cos(step_length * radius), jnp.exp(-step_length * radius)) * scale
    imag = sign * jnp.where(travel, jnp.sin(step_length * radius), 0.0) * scale
    return real, imag


def correction(speed, angular):
    phase = angular * step_length * (1.0 / speed - 1.0)
    return jnp.cos(phase), jnp.sin(phase), stencil_gain * (speed * speed - 1.0) * angular / omega_top


def local(source_field, receiver_field, velocity, slice_owner):
    freq_local, rows, width = source_field.shape[1:]
    strips = lax.axis_size("strip")
    planes = lax.axis_size("freq")
    height = rows * strips
    groups = 2 * freq_local
    members = strips // groups
    across = members // 2
    count = groups * across
    radix = width // LANES
    half = radix // 2
    freq_total = freq_local * planes
    me = lax.axis_index("strip")
    plane = lax.axis_index("freq")
    z, y, core = me // members, (me // 2) % across, me % 2
    ids = jnp.stack([z, y, core]).astype(jnp.int32)

    def swap(value, bit):
        return lax.ppermute(value, "strip", [(i, i ^ bit) for i in range(strips)])

    def swap_z(value, e):
        return swap(value, e * members)

    def swap_y(value, r):
        return swap(value, 2 * r)

    def swap_core(value):
        return swap(value, 1)

    def ahead_plane(value, k):
        return lax.ppermute(value, "freq", [(i, (i + k) % planes) for i in range(planes)])

    forward, inverse = point_tables()
    stack = lambda table: jnp.asarray(np.stack(halves(table)))
    both = lambda table: jnp.asarray(np.concatenate(halves(table)))
    tab = {
        "right_forward": stack(forward),
        "right_inverse": stack(inverse),
        "left_forward": both(forward.T),
        "left_inverse": both(inverse.T),
        "twist_y": jnp.asarray(twiddles(radix)),
        "twist_x": jnp.broadcast_to(
            jnp.asarray(twiddles(height // LANES))[..., None], (2, height // LANES, LANES, LANES)
        ),
    }

    slots = velocity.shape[0]
    shelf = jnp.stack([velocity] + [ahead_plane(velocity, k) for k in range(1, planes)])

    def own_slice(depth):
        number = slice_owner[depth]
        return lax.dynamic_slice(
            shelf,
            ((plane - number // slots) % planes, number % slots, 0, 0),
            (1, 1, rows, width),
        )[0, 0]

    speeds = [own_slice(depth) for depth in range(DEPTHS)]
    mid_speed = lax.all_gather(
        speeds[0],
        "strip",
        axis_index_groups=[[i for i in range(strips) if i % 2 == c] for c in (0, 1)],
    )
    edges = lax.all_gather(jnp.stack([jnp.stack([s[0], s[-1]]) for s in speeds]), "strip")
    one = jnp.ones((1, width), F32)
    above = [jnp.concatenate([one, edges[:-1, d, 1]]) for d in range(DEPTHS)]
    below = [jnp.concatenate([edges[1:, d, 0], one]) for d in range(DEPTHS)]

    keep, send = first_transform(ids, source_field, receiver_field, groups, tab)
    recv = swap_core(send)
    pieces = []
    for e in range(groups):
        message = jnp.stack([keep[e], recv[e]])
        pieces.append(swap_z(message, e) if e else message)
    full = []
    for e in range(groups):
        full.append(pieces[e])
        for r in range(1, across):
            full.append(swap_y(pieces[e], r))

    angular = omega_top * (plane * freq_local + z // 2 + 1).astype(F32) / freq_total
    sign = jnp.where(z % 2 == 0, -1.0, 1.0).astype(F32)
    filt = column_filter(angular, sign, height, width, core * half, half)

    mine, give = enter_columns(ids, full, filt, tab, groups, across)
    other = swap_core(give)
    beside = jnp.stack([above[0], below[0]], axis=1).reshape(count, 2, 2, width)
    beside = lax.dynamic_index_in_dim(beside, core, 1, keepdims=False).reshape(2 * count, width)
    tall = jnp.concatenate([mid_speed.reshape(count * rows, width), beside])
    cosine, sine, weight = correction(tall, angular)
    mine, give, near, far = middle(ids, mine, other, (cosine, sign * sine, weight), tab, groups, across)

    other = swap_core(give)
    outs = leave_columns(ids, mine, other, filt, tab, groups, across)
    arrived = []
    for e in range(groups):
        kept, given = outs[2 * e], outs[2 * e + 1]
        if e:
            given, kept = swap_z(given, e), swap_z(kept, e)
        arrived += [kept, swap_core(given)]

    across_freq = swap_z(far, 1)
    image = near[0] * across_freq[0] + near[1] * across_freq[1]

    def spread(value):
        wide = width // planes
        part = lambda k: lax.dynamic_slice_in_dim(value, ((plane + k) % planes) * wide, wide, axis=value.ndim - 1)
        total = part(0)
        for k in range(1, planes):
            total = total + ahead_plane(part(k), k)
        return total

    image = spread(image)
    first_image = lax.dynamic_index_in_dim(image, z // 2, 0, keepdims=False)
    for d in range(1, groups // 2):
        piece = lax.dynamic_index_in_dim(image, (z // 2) ^ d, 0, keepdims=False)
        first_image = first_image + swap_z(piece, 2 * d)

    numbers = jnp.arange(freq_local, dtype=jnp.int32) + plane * freq_local
    angulars = (omega_top * (numbers + 1).astype(F32) / freq_total)[:, None, None]
    ends = [lax.dynamic_index_in_dim(side[1], me, 0) for side in (above, below)]
    spare = jnp.ones((ROWS - 2, width), F32)
    tall = jnp.concatenate([speeds[1]] + ends + [spare])
    source_out, receiver_out, last_image = last(ids, arrived, correction(tall[None], angulars), tab, groups, rows)
    depth_image = jnp.stack([first_image, spread(last_image)])
    return (depth_image, source_out, receiver_out)


def solution(mesh):
    return jax.shard_map(
        local,
        mesh=mesh,
        in_specs=(
            P(None, "freq", "strip", None),
            P(None, "freq", "strip", None),
            P("freq", "strip", None),
            P(),
        ),
        out_specs=(
            P(None, "strip", "freq"),
            P(None, "freq", "strip", None),
            P(None, "freq", "strip", None),
        ),
        check_vma=False,
    )
```

time: 555 us -> 296 us (0.53); the launches traced: 545 us -> 292 us
  local copies, waits for them, and re-layouts: 173 us -> 8.18 us
  matrix products: 113 us -> 0 us
  Pallas kernels: 0 us -> 62.3 us
  other arithmetic: 92.9 us -> 32 us
  waiting for transfers between devices: 83.1 us -> 130 us
  starting transfers between devices: 65.6 us -> 21.2 us
  blocking collectives: 0 us -> 21.7 us
    ppermute x4 -> x25, waiting for transfers between devices: 0.01 us -> 130 us  [the longest x22 121 us: swap(): return lax.ppermute(value, 'strip', [(i, i ^ bit) for i in range(strips)])]
    dot_general x64 -> x0, matrix products: 113 us -> none  [single(): jnp.einsum(pattern, left_side, right_side, precision=lax.Precision.HIGHES...]
    reshape x32 -> x1, local copies, waits for them, and re-layouts: 67.1 us -> 0.05 us  [local(): lax.dynamic_index_in_dim(beside, core, 1, keepdims=False)]
    all_to_all x8 -> x0, waiting for transfers between devices: 64.2 us -> none  [the longest x4 36.7 us: lateral_shift(): lax.all_to_all(spectral, 'strip', split_axis=3, concat_axis=2, tiled=True)]
    pallas_call x0 -> x5, Pallas kernels: none -> 62.3 us  [the longest x1 18.9 us: middle(): pl.pallas_call(functools.partial(middle_kernel, groups, across, rows), ou...]
    all_to_all x8 -> x0, starting transfers between devices: 56.2 us -> none  [the longest x4 28.2 us: lateral_shift(): lax.all_to_all(columns_pair, 'strip', split_axis=2, concat_axis=3, tiled=...]
    unnamed x104 -> x49, local copies, waits for them, and re-layouts: 53 us -> 3.74 us
    all_to_all x8 -> x0, other arithmetic: 40.4 us -> none  [the longest x4 21.2 us: lateral_shift(): lax.all_to_all(spectral, 'strip', split_axis=3, concat_axis=2, tiled=True)]
  transfers between devices with their start and end apart: 14 -> 26, of which waited for: 9 -> 11; matrix products, arithmetic and copies ran while one was open for 25% -> 12% of each run, Pallas kernels for 0% -> 13%
where the time goes in v1:
time: 296 us; the launch traced here: 292 us
  waiting for transfers between devices  130 us (44%)
  Pallas kernels  62.3 us (21%)
  other arithmetic  32 us (11%)
  blocking collectives  21.7 us (7%)
  starting transfers between devices  21.2 us (7%)
  between operations  15.9 us (5%)
  local copies, waits for them, and re-layouts  8.18 us (3%)
    ppermute x22, waiting for transfers between devices, swap(): return lax.ppermute(value, 'strip', [(i, i ^ bit) for i in range(strips)])  121 us
    all_gather x1, blocking collectives, local(): lax.all_gather(jnp.stack([jnp.stack([s[0], s[-1]]) for s in speeds]), 'st...  21.7 us
    pallas_call x1, Pallas kernels, middle(): pl.pallas_call(functools.partial(middle_kernel, groups, across, rows), ou...  18.9 us
    ppermute x22, starting transfers between devices, swap(): return lax.ppermute(value, 'strip', [(i, i ^ bit) for i in range(strips)])  16.5 us
    pallas_call x1, Pallas kernels, enter_columns(): pl.pallas_call(functools.partial(enter_kernel, groups, across, rows), out...  15.2 us
    pallas_call x1, Pallas kernels, leave_columns(): pl.pallas_call(functools.partial(leave_kernel, groups, across, rows), out...  15 us
    div x2, other arithmetic, correction(): stencil_gain * (speed * speed - 1.0) * angular / omega_top  13.4 us
    mul x1, other arithmetic, column_filter(): imag = sign * jnp.where(travel, jnp.sin(step_length * radius), 0.0) * scale  10.2 us
  transfers between devices with their start and end apart: 26, of which 11 were waited for; matrix products, arithmetic and copies ran while one was open for 12% of the time, Pallas kernels for 13%

profile of v1, /device:TPU:0, one launch (start us, length us, event | category | flops | bytes accessed | tf_op | source)
XLA Modules:
  0.0 291.7 jit_solution(330979178463677622)
XLA Ops:
  7.2 0.0 all-gather.4.cloned.1.call-start
  7.3 0.6 pad_add_fusion.ids
  7.8 5.3 %first_transform.1 = (f32[4,4,2,64,128]{4,3,2,1,0:T(8,128)}, f32[4,4,2,64,128]{4,3,2,1,0:T(8,128)}) custom-call(s32[3]{0:T(128)} %pad_add_fusion.ids, f32[2,2,64,1024]{3,2,1,0:T(8,128)} %source.1, f32[2,2,64,1024]{3,2,1,0:T(8,128)} %receiver.1, bf16[2,256,256]{2,1,0:T(8,128)(2,1)} %constant.206.clone.table.ahead, f32[2,8,128]{2,1,0:T(8,128)} %constant.210.clone.twist), custom_call_target="tpu_custom_call" | custom-call | tf_op jit(solution)/shard_map/first_transform/pallas_call | solution.py:165
  13.1 0.5 collective-permute-start.1
  13.6 2.6 collective-permute-start
  16.1 0.6 fusion.17
  18.1 5.0 %collective-permute-done = f32[1,64,1024]{2,1,0:T(8,128)S(1)} collective-permute-done((f32[1,64,1024]{2,1,0:T(8,128)S(1)}, f32[1,64,1024]{2,1,0:T(8,128)S(1)}, u32[]{:S(2)}, u32[]{:S(2)}) %collective-permute-start) | collective-permute-done | bytes 262176 | tf_op jit(solution)/shard_map/ppermute | solution.py:627
  23.1 0.8 fusion.4
  23.9 0.1 fusion.14
  24.0 0.1 fusion.15
  24.2 1.9 collective-permute-start.3
  26.1 2.7 collective-permute-start.5
  28.8 0.1 collective-permute-start.7
  29.0 1.8 collective-permute-start.2
  30.8 25.5 %collective-permute-done.3.refs_2_ = f32[2,4,2,64,128]{4,3,2,1,0:T(8,128)S(1)} collective-permute-done((f32[2,4,2,64,128]{4,3,2,1,0:T(8,128)S(1)}, f32[2,4,2,64,128]{4,3,2,1,0:T(8,128)S(1)}, u32[]{:S(2)}, u32[]{:S(2)}) %collective-permute-start.3) | collective-permute-done | bytes 524320 | tf_op jit(solution)/shard_map/ppermute | solution.py:615
  56.2 1.6 collective-permute-start.4
  57.8 15.0 %collective-permute-done.5.refs_4_ = f32[2,4,2,64,128]{4,3,2,1,0:T(8,128)S(1)} collective-permute-done((f32[2,4,2,64,128]{4,3,2,1,0:T(8,128)S(1)}, f32[2,4,2,64,128]{4,3,2,1,0:T(8,128)S(1)}, u32[]{:S(2)}, u32[]{:S(2)}) %collective-permute-start.5) | collective-permute-done | bytes 524320 | tf_op jit(solution)/shard_map/ppermute | solution.py:615
  72.8 1.5 collective-permute-start.6
  74.4 0.5 collective-permute-start.8
  74.9 0.1 fusion.13
  75.0 10.2 %multiply_multiply_fusion.1 = (f32[4,8,128,128]{3,2,1,0:T(8,128)}, f32[4,8,128,128]{3,2,1,0:T(8,128)}) fusion(f32[]{:T(128)S(6)} %select_n.124, f32[4,128]{1,0:T(4,128)S(1)} %fusion.13, f32[8,128]{1,0:T(8,128)S(1)} %fusion.10, f32[]{:T(128)S(6)} %mul.195), kind=kLoop, calls=%fused_computation.4 | loop fusion | flops 5767168 | bytes 4200456 | tf_op jit(solution)/shard_map/mul | solution.py:588
  85.2 8.8 %collective-permute-done.6.refs_5_ = f32[2,4,2,64,128]{4,3,2,1,0:T(8,128)S(1)} collective-permute-done((f32[2,4,2,64,128]{4,3,2,1,0:T(8,128)S(1)}, f32[2,4,2,64,128]{4,3,2,1,0:T(8,128)S(1)}, u32[]{:S(2)}, u32[]{:S(2)}) %collective-permute-start.6) | collective-permute-done | bytes 524320 | tf_op jit(solution)/shard_map/ppermute | solution.py:615
  94.0 8.8 %collective-permute-done.8.refs_7_ = f32[2,4,2,64,128]{4,3,2,1,0:T(8,128)S(1)} collective-permute-done((f32[2,4,2,64,128]{4,3,2,1,0:T(8,128)S(1)}, f32[2,4,2,64,128]{4,3,2,1,0:T(8,128)S(1)}, u32[]{:S(2)}, u32[]{:S(2)}) %collective-permute-start.8) | collective-permute-done | bytes 524320 | tf_op jit(solution)/shard_map/ppermute | solution.py:615
  102.8 1.3 broadcast_in_dim.5.twist
  104.1 15.2 %enter_columns.1 = (f32[4,2,528,128]{3,2,1,0:T(8,128)}, f32[4,2,528,128]{3,2,1,0:T(8,128)}) custom-call(s32[3]{0:T(128)} %pad_add_fusion.ids, f32[4,8,128,128]{3,2,1,0:T(8,128)} %get-tuple-element.67.filt_re, f32[4,8,128,128]{3,2,1,0:T(8,128)} %get-tuple-element.66.filt_im, bf16[512,256]{1,0:T(8,128)(2,1)} %constant.208.clone.ahead, ...), custom_call_target="tpu_custom_call" | custom-call | tf_op jit(solution)/shard_map/enter_columns/pallas_call | solution.py:319
  119.3 0.1 collective-permute-start.9
  119.4 0.8 slice_bitcast_fusion.3
  120.3 21.7 %all-gather.1 = f32[32,2,1024]{2,1,0:T(2,128)S(1)} all-gather(f32[2,2,1024]{2,1,0:T(2,128)S(1)} %pad_maximum_fusion.6), channel_id=3, replica_groups=mesh['freq'=2,'strip'=16] {'strip'}, dimensions={0}, use_global_device_ids=true | all-gather | bytes 278528 | tf_op jit(solution)/shard_map/all_gather | solution.py:660
  142.0 0.2 fusion.16
  142.3 0.1 copy.17
  142.4 0.1 copy.18
  142.5 0.1 fusion.7
  142.7 12.5 %multiply_multiply_fusion = (f32[528,1024]{1,0:T(8,128)}, f32[528,1024]{1,0:T(8,128)}, f32[528,1024]{1,0:T(8,128)}) fusion(f32[16,1024]{1,0:T(8,128)S(1)} %reshape.171, f32[512,1024]{1,0:T(8,128)} %bitcast.48, f32[]{:T(128)S(6)} %mul.191, f32[]{:T(128)S(6)} %mul.185, f32[]{:T(128)S(6)} %select_n.124), kind=kLoop, calls=%fused_computation.1 | loop fusion | flops 4866048 | bytes 8650764 | tf_op jit(solution)/shard_map/div | solution.py:594
  155.1 1.4 copy-done
  156.5 18.9 %middle.1 = (f32[4,2,512,128]{3,2,1,0:T(8,128)}, f32[4,2,512,128]{3,2,1,0:T(8,128)}, f32[2,2,64,1024]{3,2,1,0:T(8,128)}, f32[2,2,64,1024]{3,2,1,0:T(8,128)}) custom-call(s32[3]{0:T(128)} %pad_add_fusion.ids, bf16[2,256,256]{2,1,0:T(8,128)(2,1)} %constant.207.clone.back, bf16[2,256,256]{2,1,0:T(8,128)(2,1)} %constant.206.clone.table.ahead, ...), custom_call_target="tpu_custom_call" | custom-call | tf_op jit(solution)/shard_map/middle/pallas_call | solution.py:477
  175.4 0.4 collective-permute-start.13
  175.8 0.1 pad.9.clone
  176.0 25.3 %collective-permute-done.10 = f32[2,2,64,1024]{3,2,1,0:T(8,128)S(1)} collective-permute-done((f32[2,2,64,1024]{3,2,1,0:T(8,128)}, f32[2,2,64,1024]{3,2,1,0:T(8,128)S(1)}, u32[]{:S(2)}, u32[]{:S(2)}) %collective-permute-start.10) | collective-permute-done | bytes 1048608 | tf_op jit(solution)/shard_map/ppermute | solution.py:615
  201.2 1.4 fusion.2
  202.6 1.5 collective-permute-start.11
  204.2 1.3 copy-done.1
  205.5 15.0 %leave_columns.1 = (f32[528,128]{1,0:T(8,128)}, f32[528,128]{1,0:T(8,128)}, f32[528,128]{1,0:T(8,128)}, f32[528,128]{1,0:T(8,128)}, f32[528,128]{1,0:T(8,128)}, ...) custom-call(s32[3]{0:T(128)} %pad_add_fusion.ids, f32[4,8,128,128]{3,2,1,0:T(8,128)} %get-tuple-element.67.filt_re, ...), custom_call_target="tpu_custom_call" | custom-call | tf_op jit(solution)/shard_map/leave_columns/pallas_call | solution.py:337
  220.5 0.3 collective-permute-start.16
  220.9 0.1 add_multiply_fusion.1
  221.0 0.1 collective-permute-start.19
  221.1 4.1 %collective-permute-start.22 = (f32[528,128]{1,0:T(8,128)}, f32[528,128]{1,0:T(8,128)S(1)}, u32[]{:S(2)}, u32[]{:S(2)}) collective-permute-start(f32[528,128]{1,0:T(8,128)} %get-tuple-element.37), channel_id=1, source_target_pairs={{0,12},{1,13},{2,14},{3,15},{4,8},{5,9},{6,10},{7,11},{8,4},{9,5},... | collective-permute-start | bytes 811016 | tf_op jit(solution)/shard_map/ppermute | solution.py:615
  225.2 3.5 %multiply_sine_fusion = (f32[2,80,1024]{2,1,0:T(8,128)}, f32[2,80,1024]{2,1,0:T(8,128)}) fusion(f32[80,1024]{1,0:T(8,128)S(1)} %get-tuple-element.57, f32[2]{0:T(128)S(1)} %convert_multiply_fusion.1), kind=kLoop, calls=%fused_computation.10 | loop fusion | flops 163840 | bytes 1638408 | tf_op jit(solution)/shard_map/sin | solution.py:594
  228.7 4.3 %collective-permute-done.16 = f32[528,128]{1,0:T(8,128)S(1)} collective-permute-done((f32[528,128]{1,0:T(8,128)}, f32[528,128]{1,0:T(8,128)S(1)}, u32[]{:S(2)}, u32[]{:S(2)}) %collective-permute-start.16) | collective-permute-done | bytes 270368 | tf_op jit(solution)/shard_map/ppermute | solution.py:615
  233.0 10.9 %collective-permute-done.19 = f32[528,128]{1,0:T(8,128)S(1)} collective-permute-done((f32[528,128]{1,0:T(8,128)}, f32[528,128]{1,0:T(8,128)S(1)}, u32[]{:S(2)}, u32[]{:S(2)}) %collective-permute-start.19) | collective-permute-done | bytes 270368 | tf_op jit(solution)/shard_map/ppermute | solution.py:615
  243.9 0.5 collective-permute-start.21
  244.4 0.5 collective-permute-start.20
  244.9 0.7 collective-permute-done.15.refs_2_
  245.6 21.7 %collective-permute-done.18.refs_4_ = f32[528,128]{1,0:T(8,128)S(1)} collective-permute-done((f32[528,128]{1,0:T(8,128)S(1)}, f32[528,128]{1,0:T(8,128)S(1)}, u32[]{:S(2)}, u32[]{:S(2)}) %collective-permute-start.18) | collective-permute-done | bytes 270368 | tf_op jit(solution)/shard_map/ppermute | solution.py:615
  267.3 1.0 multiply_multiply_fusion.2.weight
  268.4 0.6 copy-done.14
  269.1 0.1 copy-done.15
  269.2 0.1 copy-done.16
  269.2 0.1 copy-done.17
  269.3 7.9 %last.1 = (f32[2,2,64,1024]{3,2,1,0:T(8,128)}, f32[2,2,64,1024]{3,2,1,0:T(8,128)}, f32[64,1024]{1,0:T(8,128)}) custom-call(s32[3]{0:T(128)} %pad_add_fusion.ids, bf16[2,256,256]{2,1,0:T(8,128)(2,1)} %constant.207.clone.back, f32[2,8,128]{2,1,0:T(8,128)} %constant.210.clone.twist, f32[2,80,1024]{2,1,0:T(8,128)} %get-tuple-element.55.cosine, ...), custom_call_target="tpu_custom_call" | custom-call | tf_op jit(solution)/shard_map/last/pallas_call | solution.py:555
  277.3 0.9 constant_dynamic-slice_fusion
  278.2 0.7 collective-permute-start.24
  278.9 4.3 %collective-permute-done.24 = f32[64,512]{1,0:T(8,128)S(1)} collective-permute-done((f32[64,512]{1,0:T(8,128)S(1)}, f32[64,512]{1,0:T(8,128)S(1)}, u32[]{:S(2)}, u32[]{:S(2)}) %collective-permute-start.24) | collective-permute-done | bytes 131104 | tf_op jit(solution)/shard_map/ppermute | solution.py:627
  283.2 0.9 add_bitcast_fusion
  284.2 0.7 pad_maximum_fusion.5
  (90 shorter events, 0.7 us)
Async XLA Ops:
  7.2 6.4 %copy-start.18 = (f32[1,64,1024]{2,1,0:T(8,128)S(1)}, f32[1,64,1024]{2,1,0:T(8,128)}, u32[]{:S(2)}) copy-start(f32[1,64,1024]{2,1,0:T(8,128)} %param.12) | copy-start | bytes 786436
  7.2 9.0 %copy-start.20 = (s32[2]{0:T(128)S(1)}, s32[2]{0:T(128)}, u32[]{:S(2)}) copy-start(s32[2]{0:T(128)} %param.13) | copy-start | bytes 28
  7.2 135.5 %all-gather.4.cloned.1.call-start = ((), (), s32[]{:S(2)}) async-start(), calls=%async_computation | async-start | bytes 2359296 | tf_op jit(solution)/shard_map/all_gather | solution.py:655
  13.1 10.7 %copy-start.3 = (f32[4,4,2,64,128]{4,3,2,1,0:T(8,128)S(1)}, f32[4,4,2,64,128]{4,3,2,1,0:T(8,128)}, u32[]{:S(2)}) copy-start(f32[4,4,2,64,128]{4,3,2,1,0:T(8,128)} %get-tuple-element.22) | copy-start | bytes 3145732
  13.1 10.9 %collective-permute-start.1 = (f32[4,4,2,64,128]{4,3,2,1,0:T(8,128)}, f32[4,4,2,64,128]{4,3,2,1,0:T(8,128)S(1)}, u32[]{:S(2)}, u32[]{:S(2)}) collective-permute-start(f32[4,4,2,64,128]{4,3,2,1,0:T(8,128)} %get-tuple-element.23), channel_id=1, source_target_pairs={{0,1},{1,0},{2,3},{3,2},{4,5},{5,4},{6,7},{7,6},{8,9},{9,8},{10,11... | collective-permute-start | bytes 3145736 | tf_op jit(solution)/shard_map/ppermute | solution.py:615
  13.6 9.5 %collective-permute-start = (f32[1,64,1024]{2,1,0:T(8,128)S(1)}, f32[1,64,1024]{2,1,0:T(8,128)S(1)}, u32[]{:S(2)}, u32[]{:S(2)}) collective-permute-start(f32[1,64,1024]{2,1,0:T(8,128)S(1)} %copy-done.18), channel_id=1, source_target_pairs={{0,16},{16,0},{1,17},{17,1},{2,18},{18,2},{3,19},{19,3},{4,20},{20... | collective-permute-start | bytes 786440 | tf_op jit(solution)/shard_map/ppermute | solution.py:627
  24.2 32.0 %collective-permute-start.3 = (f32[2,4,2,64,128]{4,3,2,1,0:T(8,128)S(1)}, f32[2,4,2,64,128]{4,3,2,1,0:T(8,128)S(1)}, u32[]{:S(2)}, u32[]{:S(2)}) collective-permute-start(f32[2,4,2,64,128]{4,3,2,1,0:T(8,128)S(1)} %pad_maximum_fusion.2), channel_id=1, source_target_pairs={{0,4},{1,5},{2,6},{3,7},{4,0},{5,1},{6,2},{7,3},{8,12},{9,13},{10,... | collective-permute-start | bytes 1572872 | tf_op jit(solution)/shard_map/ppermute | solution.py:615
  26.1 46.7 %collective-permute-start.5 = (f32[2,4,2,64,128]{4,3,2,1,0:T(8,128)S(1)}, f32[2,4,2,64,128]{4,3,2,1,0:T(8,128)S(1)}, u32[]{:S(2)}, u32[]{:S(2)}) collective-permute-start(f32[2,4,2,64,128]{4,3,2,1,0:T(8,128)S(1)} %pad_maximum_fusion.3), channel_id=1, source_target_pairs={{0,8},{1,9},{2,10},{3,11},{4,12},{5,13},{6,14},{7,15},{8,0},{9,1},... | collective-permute-start | bytes 1572872 | tf_op jit(solution)/shard_map/ppermute | solution.py:615
  28.8 45.6 %collective-permute-start.7 = (f32[2,4,2,64,128]{4,3,2,1,0:T(8,128)S(1)}, f32[2,4,2,64,128]{4,3,2,1,0:T(8,128)S(1)}, u32[]{:S(2)}, u32[]{:S(2)}) collective-permute-start(f32[2,4,2,64,128]{4,3,2,1,0:T(8,128)S(1)} %pad_maximum_fusion.4), channel_id=1, source_target_pairs={{0,12},{1,13},{2,14},{3,15},{4,8},{5,9},{6,10},{7,11},{8,4},{9,5},... | collective-permute-start | bytes 1572872 | tf_op jit(solution)/shard_map/ppermute | solution.py:615
  29.0 56.2 %copy-start.2 = (f32[2,4,2,64,128]{4,3,2,1,0:T(8,128)}, f32[2,4,2,64,128]{4,3,2,1,0:T(8,128)S(1)}, u32[]{:S(2)}) copy-start(f32[2,4,2,64,128]{4,3,2,1,0:T(8,128)S(1)} %pad_maximum_fusion.1.refs_0_) | copy-start | bytes 1572868
  29.0 56.2 %collective-permute-start.2 = (f32[2,4,2,64,128]{4,3,2,1,0:T(8,128)S(1)}, f32[2,4,2,64,128]{4,3,2,1,0:T(8,128)S(1)}, u32[]{:S(2)}, u32[]{:S(2)}) collective-permute-start(f32[2,4,2,64,128]{4,3,2,1,0:T(8,128)S(1)} %pad_maximum_fusion.1.refs_0_), channel_id=1, source_target_pairs={{0,2},{1,3},{2,0},{3,1},{4,6},{5,7},{6,4},{7,5},{8,10},{9,11},{10,... | collective-permute-start | bytes 1572872 | tf_op jit(solution)/shard_map/ppermute | solution.py:615
  56.2 28.9 %copy-start.4 = (f32[2,4,2,64,128]{4,3,2,1,0:T(8,128)}, f32[2,4,2,64,128]{4,3,2,1,0:T(8,128)S(1)}, u32[]{:S(2)}) copy-start(f32[2,4,2,64,128]{4,3,2,1,0:T(8,128)S(1)} %collective-permute-done.3.refs_2_) | copy-start | bytes 1572868
  56.2 29.0 %collective-permute-start.4 = (f32[2,4,2,64,128]{4,3,2,1,0:T(8,128)S(1)}, f32[2,4,2,64,128]{4,3,2,1,0:T(8,128)S(1)}, u32[]{:S(2)}, u32[]{:S(2)}) collective-permute-start(f32[2,4,2,64,128]{4,3,2,1,0:T(8,128)S(1)} %collective-permute-done.3.refs_2_), channel_id=1, source_target_pairs={{0,2},{1,3},{2,0},{3,1},{4,6},{5,7},{6,4},{7,5},{8,10},{9,11},{10,... | collective-permute-start | bytes 1572872 | tf_op jit(solution)/shard_map/ppermute | solution.py:615
  72.8 12.3 %copy-start.5 = (f32[2,4,2,64,128]{4,3,2,1,0:T(8,128)}, f32[2,4,2,64,128]{4,3,2,1,0:T(8,128)S(1)}, u32[]{:S(2)}) copy-start(f32[2,4,2,64,128]{4,3,2,1,0:T(8,128)S(1)} %collective-permute-done.5.refs_4_) | copy-start | bytes 1572868
  72.8 21.2 %collective-permute-start.6 = (f32[2,4,2,64,128]{4,3,2,1,0:T(8,128)S(1)}, f32[2,4,2,64,128]{4,3,2,1,0:T(8,128)S(1)}, u32[]{:S(2)}, u32[]{:S(2)}) collective-permute-start(f32[2,4,2,64,128]{4,3,2,1,0:T(8,128)S(1)} %collective-permute-done.5.refs_4_), channel_id=1, source_target_pairs={{0,2},{1,3},{2,0},{3,1},{4,6},{5,7},{6,4},{7,5},{8,10},{9,11},{10,... | collective-permute-start | bytes 1572872 | tf_op jit(solution)/shard_map/ppermute | solution.py:615
  74.4 10.8 %copy-start.6 = (f32[2,4,2,64,128]{4,3,2,1,0:T(8,128)}, f32[2,4,2,64,128]{4,3,2,1,0:T(8,128)S(1)}, u32[]{:S(2)}) copy-start(f32[2,4,2,64,128]{4,3,2,1,0:T(8,128)S(1)} %collective-permute-done.7.refs_6_) | copy-start | bytes 1572868
  74.4 28.4 %collective-permute-start.8 = (f32[2,4,2,64,128]{4,3,2,1,0:T(8,128)S(1)}, f32[2,4,2,64,128]{4,3,2,1,0:T(8,128)S(1)}, u32[]{:S(2)}, u32[]{:S(2)}) collective-permute-start(f32[2,4,2,64,128]{4,3,2,1,0:T(8,128)S(1)} %collective-permute-done.7.refs_6_), channel_id=1, source_target_pairs={{0,2},{1,3},{2,0},{3,1},{4,6},{5,7},{6,4},{7,5},{8,10},{9,11},{10,... | collective-permute-start | bytes 1572872 | tf_op jit(solution)/shard_map/ppermute | solution.py:615
  75.0 27.9 %copy-start.19 = (f32[2,8,128]{2,1,0:T(8,128)S(1)}, f32[2,8,128]{2,1,0:T(8,128)}, u32[]{:S(2)}) copy-start(f32[2,8,128]{2,1,0:T(8,128)} %constant.210.clone.twist) | copy-start | bytes 24580
  85.2 18.9 %copy-start.7 = (f32[2,4,2,64,128]{4,3,2,1,0:T(8,128)}, f32[2,4,2,64,128]{4,3,2,1,0:T(8,128)S(1)}, u32[]{:S(2)}) copy-start(f32[2,4,2,64,128]{4,3,2,1,0:T(8,128)S(1)} %collective-permute-done.2.refs_1_) | copy-start | bytes 1572868
  85.2 18.9 %copy-start.8 = (f32[2,4,2,64,128]{4,3,2,1,0:T(8,128)}, f32[2,4,2,64,128]{4,3,2,1,0:T(8,128)S(1)}, u32[]{:S(2)}) copy-start(f32[2,4,2,64,128]{4,3,2,1,0:T(8,128)S(1)} %collective-permute-done.4.refs_3_) | copy-start | bytes 1572868
  94.0 10.1 %copy-start.9 = (f32[2,4,2,64,128]{4,3,2,1,0:T(8,128)}, f32[2,4,2,64,128]{4,3,2,1,0:T(8,128)S(1)}, u32[]{:S(2)}) copy-start(f32[2,4,2,64,128]{4,3,2,1,0:T(8,128)S(1)} %collective-permute-done.6.refs_5_) | copy-start | bytes 1572868
  102.8 1.3 copy-start.10
  119.3 35.8 %collective-permute-start.9 = (f32[4,2,528,128]{3,2,1,0:T(8,128)}, f32[4,2,528,128]{3,2,1,0:T(8,128)S(1)}, u32[]{:S(2)}, u32[]{:S(2)}) collective-permute-start(f32[4,2,528,128]{3,2,1,0:T(8,128)} %get-tuple-element.25), channel_id=1, source_target_pairs={{0,1},{1,0},{2,3},{3,2},{4,5},{5,4},{6,7},{7,6},{8,9},{9,8},{10,11... | collective-permute-start | bytes 6488072 | tf_op jit(solution)/shard_map/ppermute | solution.py:615
  155.1 1.4 copy-start
  175.4 28.8 %collective-permute-start.13 = (f32[4,2,512,128]{3,2,1,0:T(8,128)}, f32[4,2,512,128]{3,2,1,0:T(8,128)S(1)}, u32[]{:S(2)}, u32[]{:S(2)}) collective-permute-start(f32[4,2,512,128]{3,2,1,0:T(8,128)} %get-tuple-element.29), channel_id=1, source_target_pairs={{0,1},{1,0},{2,3},{3,2},{4,5},{5,4},{6,7},{7,6},{8,9},{9,8},{10,11... | collective-permute-start | bytes 6291464 | tf_op jit(solution)/shard_map/ppermute | solution.py:615
  175.8 25.4 %collective-permute-start.10 = (f32[2,2,64,1024]{3,2,1,0:T(8,128)}, f32[2,2,64,1024]{3,2,1,0:T(8,128)S(1)}, u32[]{:S(2)}, u32[]{:S(2)}) collective-permute-start(f32[2,2,64,1024]{3,2,1,0:T(8,128)} %get-tuple-element.27), channel_id=1, source_target_pairs={{0,4},{1,5},{2,6},{3,7},{4,0},{5,1},{6,2},{7,3},{8,12},{9,13},{10,... | collective-permute-start | bytes 3145736 | tf_op jit(solution)/shard_map/ppermute | solution.py:615
  202.6 22.5 %collective-permute-start.11 = (f32[2,64,512]{2,1,0:T(8,128)S(1)}, f32[2,64,512]{2,1,0:T(8,128)S(1)}, u32[]{:S(2)}, u32[]{:S(2)}) collective-permute-start(f32[2,64,512]{2,1,0:T(8,128)S(1)} %dynamic-slice_bitcast_fusion), channel_id=1, source_target_pairs={{0,16},{16,0},{1,17},{17,1},{2,18},{18,2},{3,19},{19,3},{4,20},{20... | collective-permute-start | bytes 786440 | tf_op jit(solution)/shard_map/ppermute | solution.py:627
  204.2 1.3 copy-start.1
  220.5 12.4 %copy-start.22 = (f32[528,128]{1,0:T(8,128)S(1)}, f32[528,128]{1,0:T(8,128)}, u32[]{:S(2)}) copy-start(f32[528,128]{1,0:T(8,128)} %get-tuple-element.34) | copy-start | bytes 811012
  220.5 23.4 %copy-start.21 = (f32[528,128]{1,0:T(8,128)S(1)}, f32[528,128]{1,0:T(8,128)}, u32[]{:S(2)}) copy-start(f32[528,128]{1,0:T(8,128)} %get-tuple-element.36) | copy-start | bytes 811012
  220.5 12.4 %collective-permute-start.16 = (f32[528,128]{1,0:T(8,128)}, f32[528,128]{1,0:T(8,128)S(1)}, u32[]{:S(2)}, u32[]{:S(2)}) collective-permute-start(f32[528,128]{1,0:T(8,128)} %get-tuple-element.33), channel_id=1, source_target_pairs={{0,4},{1,5},{2,6},{3,7},{4,0},{5,1},{6,2},{7,3},{8,12},{9,13},{10,... | collective-permute-start | bytes 811016 | tf_op jit(solution)/shard_map/ppermute | solution.py:615
  221.0 22.9 %collective-permute-start.19 = (f32[528,128]{1,0:T(8,128)}, f32[528,128]{1,0:T(8,128)S(1)}, u32[]{:S(2)}, u32[]{:S(2)}) collective-permute-start(f32[528,128]{1,0:T(8,128)} %get-tuple-element.35), channel_id=1, source_target_pairs={{0,8},{1,9},{2,10},{3,11},{4,12},{5,13},{6,14},{7,15},{8,0},{9,1},... | collective-permute-start | bytes 811016 | tf_op jit(solution)/shard_map/ppermute | solution.py:615
  221.1 23.3 %collective-permute-start.22 = (f32[528,128]{1,0:T(8,128)}, f32[528,128]{1,0:T(8,128)S(1)}, u32[]{:S(2)}, u32[]{:S(2)}) collective-permute-start(f32[528,128]{1,0:T(8,128)} %get-tuple-element.37), channel_id=1, source_target_pairs={{0,12},{1,13},{2,14},{3,15},{4,8},{5,9},{6,10},{7,11},{8,4},{9,5},... | collective-permute-start | bytes 811016 | tf_op jit(solution)/shard_map/ppermute | solution.py:615
  225.2 19.2 %collective-permute-start.14 = (f32[528,128]{1,0:T(8,128)}, f32[528,128]{1,0:T(8,128)S(1)}, u32[]{:S(2)}, u32[]{:S(2)}) collective-permute-start(f32[528,128]{1,0:T(8,128)} %get-tuple-element.31), channel_id=1, source_target_pairs={{0,1},{1,0},{2,3},{3,2},{4,5},{5,4},{6,7},{7,6},{8,9},{9,8},{10,11... | collective-permute-start | bytes 811016 | tf_op jit(solution)/shard_map/ppermute | solution.py:615
  225.2 20.4 %collective-permute-start.15 = (f32[528,128]{1,0:T(8,128)}, f32[528,128]{1,0:T(8,128)S(1)}, u32[]{:S(2)}, u32[]{:S(2)}) collective-permute-start(f32[528,128]{1,0:T(8,128)} %get-tuple-element.32), channel_id=1, source_target_pairs={{0,4},{1,5},{2,6},{3,7},{4,0},{5,1},{6,2},{7,3},{8,12},{9,13},{10,... | collective-permute-start | bytes 811016 | tf_op jit(solution)/shard_map/ppermute | solution.py:615
  232.9 34.4 %collective-permute-start.18 = (f32[528,128]{1,0:T(8,128)S(1)}, f32[528,128]{1,0:T(8,128)S(1)}, u32[]{:S(2)}, u32[]{:S(2)}) collective-permute-start(f32[528,128]{1,0:T(8,128)S(1)} %copy-done.22), channel_id=1, source_target_pairs={{0,8},{1,9},{2,10},{3,11},{4,12},{5,13},{6,14},{7,15},{8,0},{9,1},... | collective-permute-start | bytes 811016 | tf_op jit(solution)/shard_map/ppermute | solution.py:615
  243.9 24.5 %collective-permute-start.21 = (f32[528,128]{1,0:T(8,128)S(1)}, f32[528,128]{1,0:T(8,128)S(1)}, u32[]{:S(2)}, u32[]{:S(2)}) collective-permute-start(f32[528,128]{1,0:T(8,128)S(1)} %copy-done.21), channel_id=1, source_target_pairs={{0,12},{1,13},{2,14},{3,15},{4,8},{5,9},{6,10},{7,11},{8,4},{9,5},... | collective-permute-start | bytes 811016 | tf_op jit(solution)/shard_map/ppermute | solution.py:615
  244.4 23.9 %collective-permute-start.17 = (f32[528,128]{1,0:T(8,128)S(1)}, f32[528,128]{1,0:T(8,128)S(1)}, u32[]{:S(2)}, u32[]{:S(2)}) collective-permute-start(f32[528,128]{1,0:T(8,128)S(1)} %collective-permute-done.16), channel_id=1, source_target_pairs={{0,1},{1,0},{2,3},{3,2},{4,5},{5,4},{6,7},{7,6},{8,9},{9,8},{10,11... | collective-permute-start | bytes 811016 | tf_op jit(solution)/shard_map/ppermute | solution.py:615
  244.4 24.0 %copy-start.11 = (f32[528,128]{1,0:T(8,128)}, f32[528,128]{1,0:T(8,128)S(1)}, u32[]{:S(2)}) copy-start(f32[528,128]{1,0:T(8,128)S(1)} %collective-permute-done.14.refs_1_) | copy-start | bytes 811012
  244.4 23.9 %collective-permute-start.20 = (f32[528,128]{1,0:T(8,128)S(1)}, f32[528,128]{1,0:T(8,128)S(1)}, u32[]{:S(2)}, u32[]{:S(2)}) collective-permute-start(f32[528,128]{1,0:T(8,128)S(1)} %collective-permute-done.19), channel_id=1, source_target_pairs={{0,1},{1,0},{2,3},{3,2},{4,5},{5,4},{6,7},{7,6},{8,9},{9,8},{10,11... | collective-permute-start | bytes 811016 | tf_op jit(solution)/shard_map/ppermute | solution.py:615
  245.6 22.8 %copy-start.12 = (f32[528,128]{1,0:T(8,128)}, f32[528,128]{1,0:T(8,128)S(1)}, u32[]{:S(2)}) copy-start(f32[528,128]{1,0:T(8,128)S(1)} %collective-permute-done.15.refs_2_) | copy-start | bytes 811012
  245.6 22.8 %collective-permute-start.23 = (f32[528,128]{1,0:T(8,128)S(1)}, f32[528,128]{1,0:T(8,128)S(1)}, u32[]{:S(2)}, u32[]{:S(2)}) collective-permute-start(f32[528,128]{1,0:T(8,128)S(1)} %collective-permute-done.22), channel_id=1, source_target_pairs={{0,1},{1,0},{2,3},{3,2},{4,5},{5,4},{6,7},{7,6},{8,9},{9,8},{10,11... | collective-permute-start | bytes 811016 | tf_op jit(solution)/shard_map/ppermute | solution.py:615
  267.3 1.1 copy-start.13
  267.3 11.5 %collective-permute-start.12 = (f32[64,512]{1,0:T(8,128)S(1)}, f32[64,512]{1,0:T(8,128)S(1)}, u32[]{:S(2)}, u32[]{:S(2)}) collective-permute-start(f32[64,512]{1,0:T(8,128)S(1)} %dynamic-slice_bitcast_fusion.1), channel_id=1, source_target_pairs={{0,8},{1,9},{2,10},{3,11},{4,12},{5,13},{6,14},{7,15},{8,0},{9,1},... | collective-permute-start | bytes 393224 | tf_op jit(solution)/shard_map/ppermute | solution.py:615
  268.3 0.7 copy-start.14
  268.3 0.8 copy-start.15
  268.4 0.9 copy-start.16
  268.4 0.9 copy-start.17
  278.2 5.0 %collective-permute-start.24 = (f32[64,512]{1,0:T(8,128)S(1)}, f32[64,512]{1,0:T(8,128)S(1)}, u32[]{:S(2)}, u32[]{:S(2)}) collective-permute-start(f32[64,512]{1,0:T(8,128)S(1)} %constant_dynamic-slice_fusion), channel_id=1, source_target_pairs={{0,16},{16,0},{1,17},{17,1},{2,18},{18,2},{3,19},{19,3},{4,20},{20... | collective-permute-start | bytes 393224 | tf_op jit(solution)/shard_map/ppermute | solution.py:627
Sparse Core Ops, SparseCore 0:
  24.0 81.4 all-gather.3

commit v2 on v0

v2 whole, which is shorter than its diff:
```python
import functools
import math

import jax
import jax.numpy as jnp
import numpy as np
from jax import lax
from jax.experimental import pallas as pl
from jax.experimental.pallas import tpu as pltpu
from jax.sharding import PartitionSpec as P

DEPTHS = 2

step_length = 0.15
omega_top = 1.2
stencil_gain = 0.05
stencil_damping = 0.1

LANES = 128
ROWS = 16
VMEM_LIMIT = 56 * 1024 * 1024
ANY = pl.BlockSpec(memory_space=pl.ANY)
VMEM = pl.BlockSpec(memory_space=pltpu.VMEM)
SMEM = pl.BlockSpec(memory_space=pltpu.SMEM)
F32 = jnp.float32
BF16 = jnp.bfloat16


def halves(table):
    table = np.asarray(table, np.float32)
    high = table.astype(jnp.bfloat16)
    low = (table - high.astype(np.float32)).astype(jnp.bfloat16)
    return high, low


def point_tables():
    index = np.arange(LANES)
    angle = 2.0 * np.pi * (index[:, None] * index[None, :] % LANES) / LANES
    cosine, sine = np.cos(angle), np.sin(angle)
    forward = np.block([[cosine, -sine], [sine, cosine]])
    return forward, forward.T


def twiddles(radix):
    length = radix * LANES
    angle = 2.0 * np.pi * (np.arange(radix)[:, None] * np.arange(LANES)[None, :]) / length
    return np.stack([np.cos(angle), -np.sin(angle)]).astype(np.float32)


def small_dft(real, imag, sign):
    count = len(real)
    if count == 1:
        return list(real), list(imag)
    even = small_dft(real[0::2], imag[0::2], sign)
    odd = small_dft(real[1::2], imag[1::2], sign)
    half = count // 2
    top_real, top_imag, low_real, low_imag = [], [], [], []
    for k in range(half):
        o_re, o_im = odd[0][k], odd[1][k]
        if k == 0:
            t_re, t_im = o_re, o_im
        elif 4 * k == count:
            t_re, t_im = (-o_im, o_re) if sign > 0 else (o_im, -o_re)
        elif 8 * k == count:
            h = math.sqrt(0.5)
            t_re, t_im = ((o_re - o_im) * h, (o_im + o_re) * h) if sign > 0 else ((o_re + o_im) * h, (o_im - o_re) * h)
        elif 8 * k == 3 * count:
            h = math.sqrt(0.5)
            t_re, t_im = ((-o_re - o_im) * h, (o_re - o_im) * h) if sign > 0 else ((o_im - o_re) * h, (-o_re - o_im) * h)
        else:
            w_re, w_im = math.cos(2 * math.pi * k / count), sign * math.sin(2 * math.pi * k / count)
            t_re, t_im = o_re * w_re - o_im * w_im, o_re * w_im + o_im * w_re
        top_real.append(even[0][k] + t_re)
        top_imag.append(even[1][k] + t_im)
        low_real.append(even[0][k] - t_re)
        low_imag.append(even[1][k] - t_im)
    return top_real + low_real, top_imag + low_imag


def parts(value):
    high = value.astype(BF16)
    return high, (value - high.astype(F32)).astype(BF16)


def dot(left, right):
    return jnp.dot(left, right, preferred_element_type=F32)


def dot_right(high, low, table):
    return dot(high, table[0]) + dot(low, table[0]) + dot(high, table[1])


def dot_left(both, data_high, data_low):
    size = both.shape[0] // 2
    first = dot(both[...], data_high)
    return first[:size] + first[size:] + dot(both[:size], data_low)


def lanes(k, count=1):
    return slice(k * LANES, (k + count) * LANES)


def turned(re, im, twist, k, row, back):
    if k == 0:
        return re, im
    c, s = twist[0, k, row, :], twist[1, k, row, :]
    if back:
        return re * c + im * s, im * c - re * s
    return re * c - im * s, re * s + im * c


def forward_into(load, row, twist, high, low, index):
    radix = twist.shape[1]
    real, imag = zip(*[load(a) for a in range(radix)])
    real, imag = small_dft(list(real), list(imag), -1)
    for k in range(radix):
        pair = turned(real[k], imag[k], twist, k, slice(0, 1), False)
        for part in (0, 1):
            h, l = parts(pair[part])
            high[index(k) + (row, lanes(part))] = h
            low[index(k) + (row, lanes(part))] = l


def inverse_tiles(load, size, table, twist):
    radix = twist.shape[1]
    data = jnp.concatenate([jnp.concatenate([load(k, 0), load(k, 1)], axis=1) for k in range(radix)], axis=0)
    result = dot_right(*parts(data), table)
    real, imag = [], []
    for k in range(radix):
        row = slice(k * size, (k + 1) * size)
        re, im = turned(result[row, lanes(0)], result[row, lanes(1)], twist, k, slice(0, 1), True)
        real.append(re)
        imag.append(im)
    return small_dft(real, imag, 1)


class Copies:
    def __init__(self, sems):
        self.sems, self.used = sems, 0

    def __call__(self, *pairs):
        made = []
        for source, target in pairs:
            made.append(pltpu.make_async_copy(source, target, self.sems.at[self.used]))
            self.used += 1
        for copy in made:
            copy.start()
        return made


def done(copies):
    for copy in copies:
        copy.wait()


def call(kernel, name, out_shape, in_specs, out_specs, scratch, flops, moved, args):
    return pl.pallas_call(
        kernel,
        out_shape=out_shape,
        in_specs=in_specs,
        out_specs=out_specs,
        scratch_shapes=scratch,
        compiler_params=pltpu.CompilerParams(vmem_limit_bytes=VMEM_LIMIT),
        cost_estimate=pl.CostEstimate(flops=flops, bytes_accessed=moved, transcendentals=0),
        name=name,
    )(*args)


def first_kernel(offsets, final, ids, source, receiver, table, twist, *refs):
    high, low, given, out, sems = refs[-5:]
    messages = refs[:-5]
    z, core = ids[0], ids[2]
    radix = twist.shape[1]
    half = radix // 2
    rows = source.shape[2]
    for e, offset in enumerate(offsets):
        field = z ^ offset
        which, number = lax.rem(field, 2), lax.div(field, 2)
        for kind, ref in ((0, source), (1, receiver)):

            @pl.when(which == kind)
            def start(e=e, ref=ref, number=number):
                pltpu.make_async_copy(ref.at[:, number], given.at[e], sems.at[e]).start()

    leaving, used = [], len(offsets)
    place = 0
    for e, offset in enumerate(offsets):
        pltpu.make_async_copy(source.at[:, 0], given.at[e], sems.at[e]).wait()

        def chunk(t, carry, e=e):
            row = pl.ds(pl.multiple_of(t * ROWS, ROWS), ROWS)
            forward_into(
                lambda a: (given[e, 0, row, lanes(a)], given[e, 1, row, lanes(a)]), row, twist, high, low, lambda k: (e, k)
            )
            return carry

        lax.fori_loop(0, rows // ROWS, chunk, 0)
        for slot, start in ((0, core * half), (1, (1 - core) * half)):
            h = high[e, pl.ds(start, half)].reshape(half * rows, 2 * LANES)
            l = low[e, pl.ds(start, half)].reshape(half * rows, 2 * LANES)
            result = dot_right(h, l, table)
            for k in range(half):
                for part in (0, 1):
                    at = (slot * half + k) * 2 + part
                    out[e, at * rows : (at + 1) * rows, :] = result[k * rows : (k + 1) * rows, lanes(part)]
        moves = []
        if offset == final:
            for p in range(half // 2):
                for slot in (0, 1):
                    moves.append(
                        (
                            out.at[e, pl.ds((slot * half + 2 * p) * 2 * rows, 4 * rows)],
                            messages[place].at[pl.ds(slot * 4 * rows, 4 * rows)],
                        )
                    )
                place += 1
        else:
            moves.append((out.at[e], messages[place]))
            place += 1
        for source_part, target in moves:
            copy = pltpu.make_async_copy(source_part, target, sems.at[used])
            copy.start()
            leaving.append(copy)
            used += 1
    done(leaving)


def first_transform(ids, source, receiver, offsets, final, tab):
    rows, width = source.shape[2:]
    radix = width // LANES
    tall = 2 * radix * rows
    shapes = []
    for offset in offsets:
        if offset == final:
            shapes += [jax.ShapeDtypeStruct((8 * rows, LANES), F32)] * (radix // 4)
        else:
            shapes.append(jax.ShapeDtypeStruct((tall, LANES), F32))
    count = len(offsets)
    return call(
        functools.partial(first_kernel, offsets, final),
        "first_transform",
        tuple(shapes),
        [SMEM, ANY, ANY, VMEM, VMEM],
        (ANY,) * len(shapes),
        [
            pltpu.VMEM((count, radix, rows, 2 * LANES), BF16),
            pltpu.VMEM((count, radix, rows, 2 * LANES), BF16),
            pltpu.VMEM((count, 2, rows, width), F32),
            pltpu.VMEM((count, tall, LANES), F32),
            pltpu.SemaphoreType.DMA((count + 2 * len(shapes),)),
        ],
        count * 1000000000,
        count * 1000000,
        (ids, source, receiver, tab["right_forward"], tab["twist_y"]),
    )


def shift_pair(pair, rows, data, filt_re, filt_im, ahead, back, twist, high, low, line):
    radix = twist.shape[1]
    per = rows // ROWS

    def spot(k, part, a, t):
        index = a * (LANES // ROWS) + t
        block, inner = lax.div(index, per), lax.rem(index, per)
        start = pl.multiple_of((2 * k + part) * rows + inner * ROWS, ROWS)
        return lax.div(block, 2), lax.rem(block, 2), pl.ds(start, ROWS)

    def fold(t, carry):
        off = pl.multiple_of(t * ROWS, ROWS)
        row = pl.ds(off, ROWS)
        for kk in (0, 1):
            real, imag = ([data[spot(pair + kk, part, a, t)] for a in range(radix)] for part in (0, 1))
            real, imag = small_dft(real, imag, -1)
            for k in range(radix):
                turn_pair = turned(real[k], imag[k], twist, k, row, False)
                for part in (0, 1):
                    h, l = parts(turn_pair[part])
                    high[k, pl.ds(part * LANES + off, ROWS), lanes(kk)] = h
                    low[k, pl.ds(part * LANES + off, ROWS), lanes(kk)] = l
        return carry

    lax.fori_loop(0, LANES // ROWS, fold, 0)

    def spectral(k, carry):
        value = dot_left(ahead, high[k], low[k])
        re, im = value[:LANES], value[LANES:]
        fr = jnp.concatenate([filt_re[pair, k], filt_re[pair + 1, k]], axis=1)
        fi = jnp.concatenate([filt_im[pair, k], filt_im[pair + 1, k]], axis=1)
        both = jnp.concatenate([re * fr - im * fi, re * fi + im * fr], axis=0)
        h, l = parts(both)
        line[k] = dot_left(back, h, l)
        return carry

    lax.fori_loop(0, radix, spectral, 0, unroll=4)

    def unfold(t, carry):
        off = pl.multiple_of(t * ROWS, ROWS)
        row = pl.ds(off, ROWS)
        for kk in (0, 1):
            real, imag = [], []
            for k in range(radix):
                re = line[k, pl.ds(off, ROWS), lanes(kk)]
                im = line[k, pl.ds(LANES + off, ROWS), lanes(kk)]
                re, im = turned(re, im, twist, k, row, True)
                real.append(re)
                imag.append(im)
            both = small_dft(real, imag, 1)
            for part in (0, 1):
                for a in range(radix):
                    data[spot(pair + kk, part, a, t)] = both[part][a]
        return carry

    lax.fori_loop(0, LANES // ROWS, unfold, 0)


def outer_rows(rows, half, data):
    count = data.shape[0]
    for b in range(2 * count):
        for k in range(half):
            for part in (0, 1):
                base = (2 * k + part) * rows
                at = 2 * half * rows + (2 * k + part) * 2
                for side, beside, row in ((0, b - 1, base + rows - 1), (1, b + 1, base)):
                    if 0 <= beside < 2 * count:
                        value = data[beside // 2, beside % 2, row : row + 1, :]
                    else:
                        value = jnp.zeros((1, LANES), F32)
                    data[b // 2, b % 2, at + side : at + side + 1, :] = value


def enter_kernel(groups, across, rows, ids, filt_re, filt_im, ahead, back, twist, *refs):
    keep, send, data, fre, fim, tw, high, low, line, sems = refs[-10:]
    pieces = refs[:-10]
    z, y, core = ids[0], ids[1], ids[2]
    half = fre.shape[0]
    pairs = half // 2
    copies = Copies(sems)
    first = copies((twist, tw))
    arrivals = []
    for p in range(pairs):
        moves = []
        at = 0
        for e in range(groups):
            split = e == groups - 1
            for r in range(across):
                block = (z ^ e) * across + (y ^ r)
                for h in (0, 1):
                    piece = pieces[at + (p if split else 0)]
                    at += pairs if split else 1
                    start = h * 4 * rows if split else (h * half + 2 * p) * 2 * rows
                    moves.append(
                        (
                            piece.at[pl.ds(start, 4 * rows)],
                            data.at[block, core ^ h, pl.ds(4 * p * rows, 4 * rows)],
                        )
                    )
        moves += [(a.at[pl.ds(2 * p, 2)], b.at[pl.ds(2 * p, 2)]) for a, b in ((filt_re, fre), (filt_im, fim))]
        arrivals.append(copies(*moves))
    done(first)
    leaving = []
    for p in range(pairs):
        done(arrivals[p])
        shift_pair(2 * p, rows, data, fre, fim, ahead, back, tw, high, low, line)
        lot = pl.ds(4 * p * rows, 4 * rows)
        leaving += copies(*[(data.at[:, par, lot], out.at[:, lot]) for out, par in ((send, 1 - core), (keep, core))])
    outer_rows(rows, half, data)
    lot = pl.ds(2 * half * rows, 4 * half)
    leaving += copies(*[(data.at[:, par, lot], out.at[:, lot]) for out, par in ((send, 1 - core), (keep, core))])
    done(leaving)


def leave_kernel(groups, across, rows, ids, filt_re, filt_im, ahead, back, twist, mine, other, *refs):
    data, fre, fim, tw, high, low, line, sems = refs[-8:]
    outs = refs[:-8]
    z, y, core = ids[0], ids[1], ids[2]
    half = fre.shape[0]
    pairs = half // 2
    copies = Copies(sems)
    first = copies((twist, tw))
    arrivals = []
    for p in range(pairs):
        lot = pl.ds(4 * p * rows, 4 * rows)
        moves = [(mine.at[:, lot], data.at[:, core, lot]), (other.at[:, lot], data.at[:, 1 - core, lot])]
        moves += [(a.at[pl.ds(2 * p, 2)], b.at[pl.ds(2 * p, 2)]) for a, b in ((filt_re, fre), (filt_im, fim))]
        arrivals.append(copies(*moves))
    done(first)
    for p in range(pairs):
        done(arrivals[p])
        shift_pair(2 * p, rows, data, fre, fim, ahead, back, tw, high, low, line)
    outer_rows(rows, half, data)
    moves = []
    for e in range(groups):
        for h in (0, 1):
            moves.append((data.at[(z ^ e) * across + y, core ^ h], outs[2 * e + h]))
    done(copies(*moves))


def column_scratch(half, count, rows, copies):
    radix = 2 * count * rows // LANES
    return [
        pltpu.VMEM((count, 2, 2 * half * rows + 4 * half, LANES), F32),
        pltpu.VMEM((half, radix, LANES, LANES), F32),
        pltpu.VMEM((half, radix, LANES, LANES), F32),
        pltpu.VMEM((2, radix, LANES, LANES), F32),
        pltpu.VMEM((radix, 2 * LANES, 2 * LANES), BF16),
        pltpu.VMEM((radix, 2 * LANES, 2 * LANES), BF16),
        pltpu.VMEM((radix, 2 * LANES, 2 * LANES), F32),
        pltpu.SemaphoreType.DMA((copies,)),
    ]


def enter_columns(ids, pieces, filt, tab, groups, across, rows, half):
    count = groups * across
    out = jax.ShapeDtypeStruct((count, 2 * half * rows + 4 * half, LANES), F32)
    pairs = half // 2
    return call(
        functools.partial(enter_kernel, groups, across, rows),
        "enter_columns",
        (out, out),
        [SMEM, ANY, ANY, VMEM, VMEM, ANY] + [ANY] * len(pieces),
        (ANY, ANY),
        column_scratch(half, count, rows, 1 + pairs * (2 * count + 4) + 2),
        8000000000,
        8000000,
        (ids, *filt, tab["left_forward"], tab["left_inverse"], tab["twist_x"], *pieces),
    )


def leave_columns(ids, mine, other, filt, tab, groups, across, rows, half):
    count = groups * across
    out = jax.ShapeDtypeStruct((2 * half * rows + 4 * half, LANES), F32)
    return call(
        functools.partial(leave_kernel, groups, across, rows),
        "leave_columns",
        (out,) * (2 * groups),
        [SMEM, ANY, ANY, VMEM, VMEM, ANY, ANY, ANY],
        (ANY,) * (2 * groups),
        column_scratch(half, count, rows, 1 + 2 * half + 2 * groups),
        8000000000,
        8000000,
        (ids, *filt, tab["left_forward"], tab["left_inverse"], tab["twist_x"], mine, other),
    )


def turn(square):
    cosine, ratio = 1.0, 1.0
    for n in (4, 3, 2, 1):
        cosine = 1.0 - cosine * square * (1.0 / ((2 * n - 1) * (2 * n)))
        ratio = 1.0 - ratio * square * (1.0 / ((2 * n) * (2 * n + 1)))
    return cosine, ratio


def correction(speed, angular, sign):
    phase = (sign * step_length) * angular * (1.0 / speed - 1.0)
    cosine, ratio = turn(phase * phase)
    return cosine, ratio * phase, stencil_gain * (speed * speed - 1.0) * angular / omega_top


def stencil(field, halo, weight, sign, store):
    radix, weigh = weight
    shape = field(0, 0).shape
    line = lax.broadcasted_iota(jnp.int32, shape, 0)
    place = lax.broadcasted_iota(jnp.int32, shape, 1)
    top, bottom = line == 0, line == shape[0] - 1
    left, right = place == 0, place == LANES - 1
    zero = jnp.zeros(shape, F32)
    before = [zero, zero]
    for a in range(radix):
        center, bent = [], []
        for part in (0, 1):
            value = field(part, a)
            ahead = pltpu.roll(value, 1, axis=1)
            west = jnp.where(left, before[part], ahead)
            before[part] = ahead
            follow = pltpu.roll(field(part, a + 1), LANES - 1, axis=1) if a + 1 < radix else zero
            east = jnp.where(right, follow, pltpu.roll(value, LANES - 1, axis=1))
            north = jnp.where(top, halo(part, 0, a), pltpu.roll(value, 1, axis=0))
            south = jnp.where(bottom, halo(part, 1, a), pltpu.roll(value, shape[0] - 1, axis=0))
            center.append(value)
            bent.append((north + south) + (west + east) - 4.0 * value)
        heavy = weigh(a)
        twist, damp = heavy * sign, heavy * stencil_damping
        store(0, a, center[0] + damp * bent[0] - twist * bent[1])
        store(1, a, center[1] + damp * bent[1] + twist * bent[0])


def middle_kernel(groups, across, rows, ids, back, ahead, twist, halo_cos, halo_sin, cosine, sine, weight, mine, other, *refs):
    keep, send, near, far, data, halo, cos, sin, wei, field, edge, fresh, high, low, out, block_sems, sems = refs
    z, y, core = ids[0], ids[1], ids[2]
    which = lax.rem(z, 2)
    sign = jnp.where(which == 0, -1.0, 1.0).astype(F32)
    count = groups * across
    radix = twist.shape[1]
    half = radix // 2
    own, outer = pl.ds(0, 2 * half * rows), pl.ds(2 * half * rows, 4 * half)
    copies = Copies(sems)
    first = copies((mine.at[:, outer], halo.at[core]), (other.at[:, outer], halo.at[1 - core]))

    def arrivals(i):
        pairs = (
            (mine.at[i, own], data.at[core, i]),
            (other.at[i, own], data.at[1 - core, i]),
            (cosine.at[i], cos.at[i]),
            (sine.at[i], sin.at[i]),
            (weight.at[i], wei.at[i]),
        )
        return [pltpu.make_async_copy(a, b, block_sems.at[i, n]) for n, (a, b) in enumerate(pairs)]

    def launch(i, carry):
        for copy in arrivals(i):
            copy.start()
        return carry

    lax.fori_loop(0, count, launch, 0)
    done(first)

    def halo_rows(k, part):
        at = (2 * (k % half) + part) * 2
        return jnp.concatenate([halo[k // half, i, at : at + 2, :] for i in range(count)], axis=0)

    real, imag = inverse_tiles(halo_rows, 2 * count, back, twist)
    for a in range(radix):
        c, s = halo_cos[a], halo_sin[a]
        edge[0, a] = real[a] * c - imag[a] * s
        edge[1, a] = real[a] * s + imag[a] * c

    def departures(i):
        pairs = ((out.at[1, i], send.at[i]), (out.at[0, i], keep.at[i]))
        return [pltpu.make_async_copy(a, b, block_sems.at[i, n]) for n, (a, b) in enumerate(pairs)]

    def block(i, carry):
        done(arrivals(i))
        real, imag = inverse_tiles(
            lambda k, part: data[k // half, i, (2 * (k % half) + part) * rows : (2 * (k % half) + part + 1) * rows, :],
            rows,
            back,
            twist,
        )
        for a in range(radix):
            c, s = cos[i, a], sin[i, a]
            field[0, a] = real[a] * c - imag[a] * s
            field[1, a] = real[a] * s + imag[a] * c

        def store(part, a, value):
            fresh[part, i, :, lanes(a)] = value

        stencil(
            lambda part, a: field[part, a],
            lambda part, side, a: edge[part, a, pl.ds(2 * i + side, 1), :],
            (radix, lambda a: wei[i, a]),
            sign,
            store,
        )

        def fold(t, carry):
            row = pl.ds(pl.multiple_of(t * ROWS, ROWS), ROWS)
            forward_into(
                lambda a: (fresh[0, i, row, lanes(a)], fresh[1, i, row, lanes(a)]), row, twist, high, low, lambda k: (k,)
            )
            return carry

        lax.fori_loop(0, rows // ROWS, fold, 0)
        for slot, start in ((1, (1 - core) * half), (0, core * half)):
            h = high[pl.ds(start, half)].reshape(half * rows, 2 * LANES)
            l = low[pl.ds(start, half)].reshape(half * rows, 2 * LANES)
            result = dot_right(h, l, ahead)
            for k in range(half):
                for part in (0, 1):
                    at = 2 * k + part
                    out[slot, i, at * rows : (at + 1) * rows, :] = result[k * rows : (k + 1) * rows, lanes(part)]
        for copy in departures(i):
            copy.start()
        return carry

    lax.fori_loop(0, count, block, 0)
    leaving = []
    for target, parity in ((far, 1 - which), (near, which)):
        for t in range(groups // 2):
            leaving += copies((fresh.at[:, (parity + 2 * t) * across + y], target.at[:, t]))

    def settle(i, carry):
        done(departures(i))
        return carry

    lax.fori_loop(0, count, settle, 0)
    done(leaving)


def middle(ids, mine, other, factors, tab, groups, across, rows, half):
    count = groups * across
    radix = 2 * half
    width = radix * LANES
    out = jax.ShapeDtypeStruct((count, 2 * half * rows, LANES), F32)
    image = jax.ShapeDtypeStruct((2, groups // 2, rows, width), F32)
    cosine, sine, weight, halo_cos, halo_sin = factors
    blocks = pltpu.VMEM((count, radix, rows, LANES), F32)
    return call(
        functools.partial(middle_kernel, groups, across, rows),
        "middle",
        (out, out, image, image),
        [SMEM] + [VMEM] * 5 + [ANY] * 5,
        (ANY,) * 4,
        [
            pltpu.VMEM((2, count, 2 * half * rows, LANES), F32),
            pltpu.VMEM((2, count, 4 * half, LANES), F32),
            blocks,
            blocks,
            blocks,
            pltpu.VMEM((2, radix, rows, LANES), F32),
            pltpu.VMEM((2, radix, 2 * count, LANES), F32),
            pltpu.VMEM((2, count, rows, width), F32),
            pltpu.VMEM((radix, rows, 2 * LANES), BF16),
            pltpu.VMEM((radix, rows, 2 * LANES), BF16),
            pltpu.VMEM((2, count, 2 * half * rows, LANES), F32),
            pltpu.SemaphoreType.DMA((count, 5)),
            pltpu.SemaphoreType.DMA((2 + groups,)),
        ],
        16000000000,
        10000000,
        (
            ids,
            tab["right_inverse"],
            tab["right_forward"],
            tab["twist_y"],
            halo_cos,
            halo_sin,
            cosine,
            sine,
            weight,
            mine,
            other,
        ),
    )


def prepare_kernel(groups, across, ids, scales, *refs):
    number = across
    pieces, others = refs[:number], refs[number : 2 * number]
    cosine, sine, weight, halo_cos, halo_sin, speed, lasts, firsts, sems = refs[2 * number :]
    z, y, core = ids[0], ids[1], ids[2]
    count, radix, rows, _ = speed.shape
    one = jnp.ones((radix, 8, LANES), F32)
    lasts[0] = one
    firsts[count] = one
    copies = Copies(sems)
    moves, beside = [], []
    for r in range(across):
        for n, e in enumerate(gather_order(groups)):
            block = (z ^ e) * across + (y ^ r)
            moves.append((pieces[r].at[n], speed.at[block]))
            beside.append((others[r].at[n, :, pl.ds(rows - 8, 8)], lasts.at[block + 1 - core]))
            beside.append((others[r].at[n, :, pl.ds(0, 8)], firsts.at[block + 1 - core]))
    moves, beside = copies(*moves), copies(*beside)
    done(moves)

    def chunk(i, carry):
        for a in range(radix):
            cosine[i, a], sine[i, a], weight[i, a] = correction(speed[i, a], scales[0], scales[1])
        return carry

    lax.fori_loop(0, count, chunk, 0)
    done(beside)
    for a in range(radix):
        rows_beside = []
        for i in range(count):
            rows_beside += [lasts[i, a, 7:8, :], firsts[i + 1, a, 0:1, :]]
        halo_cos[a], halo_sin[a], _ = correction(jnp.concatenate(rows_beside, axis=0), scales[0], scales[1])


def prepare(ids, scales, pieces, others, groups, across):
    _, radix, rows, _ = pieces[0].shape
    count = groups * across
    out = jax.ShapeDtypeStruct((count, radix, rows, LANES), F32)
    halo = jax.ShapeDtypeStruct((radix, 2 * count, LANES), F32)
    return call(
        functools.partial(prepare_kernel, groups, across),
        "prepare",
        (out, out, out, halo, halo),
        [SMEM] * 2 + [ANY] * (2 * len(pieces)),
        (VMEM,) * 5,
        [
            pltpu.VMEM((count, radix, rows, LANES), F32),
            pltpu.VMEM((count + 1, radix, 8, LANES), F32),
            pltpu.VMEM((count + 1, radix, 8, LANES), F32),
            pltpu.SemaphoreType.DMA((3 * len(pieces) * groups,)),
        ],
        4000000000,
        8000000,
        (ids, scales, *pieces, *others),
    )


def last_kernel(groups, rows, ids, angulars, back, twist, speed, beside, *refs):
    source, receiver, image, data, field, edge, turns, sems = refs[-8:]
    pieces = refs[:-8]
    z, core = ids[0], ids[2]
    radix = twist.shape[1]
    half = radix // 2
    copies = Copies(sems)
    arrivals = copies(
        *[(pieces[2 * e + h], data.at[z ^ e, core ^ h]) for e in range(groups) for h in (0, 1)]
    )
    done(arrivals)

    def halo_rows(k, part):
        at = 2 * half * rows + (2 * (k % half) + part) * 2
        return jnp.concatenate(
            [data[g, k // half, at : at + 2, :] for g in range(groups)] + [jnp.zeros((tall - 2 * groups, LANES), F32)], axis=0
        )

    tall = -(-2 * groups // ROWS) * ROWS
    real, imag = inverse_tiles(halo_rows, tall, back, twist)
    for a in range(radix):
        for g in range(groups):
            c, s, _ = correction(beside[:, lanes(a)], angulars[g // 2], 2.0 * (g % 2) - 1.0)
            pair = slice(2 * g, 2 * g + 2)
            edge[0, a, pair, :] = real[a][pair] * c - imag[a][pair] * s
            edge[1, a, pair, :] = real[a][pair] * s + imag[a][pair] * c
    for number in range(groups // 2):
        for a in range(radix):
            turns[0, a], turns[1, a], turns[2, a] = correction(speed[:, lanes(a)], angulars[number], 1.0)
        for which, out in ((0, source), (1, receiver)):
            sign = 2.0 * which - 1.0
            g = 2 * number + which
            real, imag = inverse_tiles(
                lambda k, part: data[g, k // half, (2 * (k % half) + part) * rows : (2 * (k % half) + part + 1) * rows, :],
                rows,
                back,
                twist,
            )
            for a in range(radix):
                c, s = turns[0, a], turns[1, a] * sign
                field[0, a] = real[a] * c - imag[a] * s
                field[1, a] = real[a] * s + imag[a] * c

            def store(part, a, value):
                out[part, number, :, lanes(a)] = value

            stencil(
                lambda part, a: field[part, a],
                lambda part, side, a: edge[part, a, 2 * g + side : 2 * g + side + 1, :],
                (radix, lambda a: turns[2, a]),
                sign,
                store,
            )
    for a in range(radix):
        total = jnp.zeros((rows, LANES), F32)
        for number in range(groups // 2):
            for part in (0, 1):
                total = total + source[part, number, :, lanes(a)] * receiver[part, number, :, lanes(a)]
        image[:, lanes(a)] = total


def last(ids, angulars, speed, beside, pieces, tab, groups):
    rows, width = speed.shape
    radix = width // LANES
    out = jax.ShapeDtypeStruct((2, groups // 2, rows, width), F32)
    return call(
        functools.partial(last_kernel, groups, rows),
        "last",
        (out, out, jax.ShapeDtypeStruct((rows, width), F32)),
        [SMEM] * 2 + [VMEM] * 4 + [ANY] * (2 * groups),
        (VMEM,) * 3,
        [
            pltpu.VMEM((groups, 2, radix * rows + 2 * radix, LANES), F32),
            pltpu.VMEM((2, radix, rows, LANES), F32),
            pltpu.VMEM((2, radix, 2 * groups, LANES), F32),
            pltpu.VMEM((3, radix, rows, LANES), F32),
            pltpu.SemaphoreType.DMA((2 * groups,)),
        ],
        8000000000,
        8000000,
        (ids, angulars, tab["right_inverse"], tab["twist_y"], speed, beside, *pieces),
    )


def gather_order(groups):
    order = [0]
    for bit in bits(groups):
        order += [e ^ bit for e in order]
    return order


def after(value, *others):
    return lax.optimization_barrier((value, others))[0]


def bits(count):
    return [1 << n for n in reversed(range(count.bit_length() - 1))]


def centered(position, length):
    shifted = jnp.where(position < length // 2, position, position - length)
    return shifted.astype(F32) * (2.0 * math.pi / length)


def column_filter(angular, sign, height, width, first_block, blocks):
    radix_x, radix_y = height // LANES, width // LANES
    inner = jnp.arange(LANES, dtype=jnp.int32)
    wave_x = centered(jnp.arange(radix_x, dtype=jnp.int32)[:, None] + radix_x * inner[None, :], height)
    wave_y = centered(first_block + jnp.arange(blocks, dtype=jnp.int32)[:, None] + radix_y * inner[None, :], width)
    wave_x = wave_x[None, :, :, None]
    wave_y = wave_y[:, None, None, :]
    argument = angular * angular - (wave_x * wave_x + wave_y * wave_y)
    radius = step_length * jnp.sqrt(jnp.abs(argument))
    travel = argument >= 0.0
    scale = 1.0 / (height * width)
    cosine, ratio = turn(jnp.where(travel, radius * radius, 0.0))
    real = jnp.where(travel, cosine, jnp.exp(-radius)) * scale
    imag = jnp.where(travel, ratio * radius, 0.0) * (sign * scale)
    return real, imag


def local(source_field, receiver_field, velocity, slice_owner):
    freq_local, rows, width = source_field.shape[1:]
    strips = lax.axis_size("strip")
    planes = lax.axis_size("freq")
    height = rows * strips
    groups = 2 * freq_local
    members = strips // groups
    across = members // 2
    radix = width // LANES
    half = radix // 2
    freq_total = freq_local * planes
    me = lax.axis_index("strip")
    plane = lax.axis_index("freq")
    z, y, core = me // members, (me // 2) % across, me % 2
    ids = jnp.stack([z, y, core, plane]).astype(jnp.int32)

    def swap(value, bit):
        return lax.ppermute(value, "strip", [(i, i ^ bit) for i in range(strips)])

    def swap_z(value, e):
        return swap(value, e * members)

    def swap_y(value, r):
        return swap(value, 2 * r)

    def swap_core(value):
        return swap(value, 1)

    def ahead_plane(value, k):
        return lax.ppermute(value, "freq", [(i, (i + k) % planes) for i in range(planes)])

    forward, inverse = point_tables()
    stack = lambda table: jnp.asarray(np.stack(halves(table)))
    both = lambda table: jnp.asarray(np.concatenate(halves(table)))
    tab = {
        "right_forward": stack(forward),
        "right_inverse": stack(inverse),
        "left_forward": both(forward.T),
        "left_inverse": both(inverse.T),
        "twist_y": jnp.asarray(twiddles(radix)[:, :, None, :]),
        "twist_x": jnp.asarray(np.repeat(twiddles(height // LANES)[..., None], LANES, axis=-1)),
    }

    slots = velocity.shape[0]
    shelf = jnp.stack([velocity] + [ahead_plane(velocity, k) for k in range(1, planes)])

    def own_slice(depth):
        number = slice_owner[depth]
        return lax.dynamic_slice(
            shelf,
            ((plane - number // slots) % planes, number % slots, 0, 0),
            (1, 1, rows, width),
        )[0, 0]

    speeds = [own_slice(depth) for depth in range(DEPTHS)]

    final, top = groups - 1, groups // 2
    messages = {}
    order = [top, 0] + [e for e in range(1, final) if e != top] + [final]
    made = list(first_transform(ids, source_field, receiver_field, order, final, tab))
    for e in order:
        messages[e] = [made.pop(0) for _ in range(half // 2 if e == final else 1)]
    pieces, full = {0: messages[0]}, {}

    def share(e, *waits):
        ready = [after(piece, wait) for piece, wait in zip(pieces[e], waits)] if waits else pieces[e]
        mine = [pieces[e]] + [[] for r in range(1, across)]
        for piece in ready:
            sent = [swap_y(after(piece, mine[r][-1:]), r) for r in range(1, across)]
            for r in range(1, across):
                mine[r].append(sent[r - 1])
        full[e] = [lot for own in mine for lot in (own, [swap_core(piece) for piece in own])]

    angular = omega_top * (plane * freq_local + z // 2 + 1).astype(F32) / freq_total
    sign = jnp.where(z % 2 == 0, -1.0, 1.0).astype(F32)
    filt = column_filter(angular, sign, height, width, core * half, half)
    share(0, shelf)
    for e in range(final - 1, 0, -1):
        pieces[e] = [swap_z(messages[e][0], e)]
    for e in range(1, final):
        share(e)
    book = jnp.swapaxes(speeds[0].reshape(rows, -1, LANES), 0, 1)[None]
    book = jnp.concatenate([book, swap_z(book, top)])
    pieces[final] = []
    for i, message in enumerate(messages[final]):
        ready = (pieces[1], full[0][2]) if i == 0 else (pieces[top], full[1][2], filt)
        pieces[final].append(swap_z(after(message, ready), final))
    for bit in bits(groups)[1:]:
        book = jnp.concatenate([book, swap_z(book, bit)])
    share(final, *([(full[0], full[1][2])] + [(full[1], full[top][2])] * (half // 2 - 1)))
    books = [swap_y(after(book, pieces[final]), r) if r else book for r in range(across)]
    facing = [swap_core(part) for part in books]
    tops = lax.ppermute(after(speeds[1][-1:], pieces[final]), "strip", [(i, i + 1) for i in range(strips - 1)])
    tails = lax.ppermute(after(speeds[1][:1], pieces[final]), "strip", [(i + 1, i) for i in range(strips - 1)])

    scales = jnp.stack([angular, sign])
    books[0], tops, tails = lax.optimization_barrier((books[0], tops, tails))
    beside = jnp.concatenate([jnp.where(me == 0, 1.0, tops), jnp.where(me == strips - 1, 1.0, tails)])

    chosen = [piece for e in range(groups) for lot in full[e] for piece in lot]
    mine, give = enter_columns(ids, chosen, filt, tab, groups, across, rows, half)
    other = swap_core(give)
    factors = prepare(ids, scales, books, facing, groups, across)
    mine, give, near, far = middle(ids, mine, other, factors, tab, groups, across, rows, half)

    other = swap_core(give)
    outs = leave_columns(ids, mine, other, filt, tab, groups, across, rows, half)

    arrived = []
    for e in range(groups):
        kept, given = outs[2 * e], outs[2 * e + 1]
        if e:
            given, kept = swap_z(given, e), swap_z(kept, e)
        arrived += [kept, swap_core(given)]

    facing = swap_z(far, 1)
    facing = after(facing, arrived[2])
    image = near[0] * facing[0] + near[1] * facing[1]

    wide = width // planes

    def spread(value):
        part = lambda k: lax.dynamic_slice_in_dim(value, ((plane + k) % planes) * wide, wide, axis=value.ndim - 1)
        total = part(0)
        for k in range(1, planes):
            total = total + ahead_plane(part(k), k)
        return total

    image = spread(image)
    first_image = lax.dynamic_index_in_dim(image, z // 2, 0, keepdims=False)
    for d in range(1, groups // 2):
        piece = lax.dynamic_index_in_dim(image, (z // 2) ^ d, 0, keepdims=False)
        first_image = first_image + swap_z(piece, 2 * d)

    numbers = jnp.arange(freq_local, dtype=jnp.int32) + plane * freq_local
    angulars = omega_top * (numbers + 1).astype(F32) / freq_total
    source_out, receiver_out, last_image = last(ids, angulars, speeds[1], beside, arrived, tab, groups)
    depth_image = jnp.stack([first_image, spread(last_image)])
    return (depth_image, source_out, receiver_out)


def solution(mesh):
    return jax.shard_map(
        local,
        mesh=mesh,
        in_specs=(
            P(None, "freq", "strip", None),
            P(None, "freq", "strip", None),
            P("freq", "strip", None),
            P(),
        ),
        out_specs=(
            P(None, "strip", "freq"),
            P(None, "freq", "strip", None),
            P(None, "freq", "strip", None),
        ),
        check_vma=False,
    )
```

time: 555 us -> 232 us (0.42)
  the two profiles are of different devices: /device:TPU:0 before, /device:TPU:12 now
where the time goes in v2:
time: 232 us; the launch traced here: 231 us
  waiting for transfers between devices  94.2 us (41%)
  Pallas kernels  67.6 us (29%)
  starting transfers between devices  52.5 us (23%)
  other arithmetic  8.94 us (4%)
  local copies, waits for them, and re-layouts  5.53 us (2%)
  between operations  2.59 us (1%)
    ppermute x38, waiting for transfers between devices, swap(): return lax.ppermute(value, 'strip', [(i, i ^ bit) for i in range(strips)])  87.2 us
    pallas_call x6, Pallas kernels, call(): pl.pallas_call(kernel, out_shape=out_shape, in_specs=in_specs, out_specs=...  67.6 us
    ppermute x38, starting transfers between devices, swap(): return lax.ppermute(value, 'strip', [(i, i ^ bit) for i in range(strips)])  43.3 us
    ppermute x3, waiting for transfers between devices, ahead_plane(): lax.ppermute(value, 'freq', [(i, (i + k) % planes) for i in range(planes)])  4.78 us
  transfers between devices with their start and end apart: 43, of which 16 were waited for; matrix products, arithmetic and copies ran while one was open for 4% of the time, Pallas kernels for 19%

profile of v2, /device:TPU:12, one launch (start us, length us, event | category | flops | bytes accessed | tf_op | source)
XLA Modules:
  0.0 231.3 jit_solution(11199341299379235502)
XLA Ops:
  0.7 0.6 pad_add_fusion.ids
  1.3 5.3 %first_transform.1 = (f32[1024,128]{1,0:T(8,128)}, f32[1024,128]{1,0:T(8,128)}, f32[1024,128]{1,0:T(8,128)}, f32[512,128]{1,0:T(8,128)}, f32[512,128]{1,0:T(8,128)}) custom-call(s32[4]{0:T(128)} %pad_add_fusion.ids, f32[2,2,64,1024]{3,2,1,0:T(8,128)} %source.1, f32[2,2,64,1024]{3,2,1,0:T(8,128)} %receiver.1, ...), custom_call_target="tpu_custom_call" | custom-call | flops 4000000000 | bytes 4000000 | tf_op jit(solution)/shard_map/first_transform/pallas_call | solution.py:157
  6.5 0.5 collective-permute-start.3
  7.0 2.6 %collective-permute-start.6 = (f32[1024,128]{1,0:T(8,128)}, f32[1024,128]{1,0:T(8,128)S(1)}, u32[]{:S(2)}, u32[]{:S(2)}) collective-permute-start(f32[1024,128]{1,0:T(8,128)} %get-tuple-element.49), channel_id=1, source_target_pairs={{0,8},{1,9},{2,10},{3,11},{4,12},{5,13},{6,14},{7,15},{8,0},{9,1},... | collective-permute-start | bytes 1572872 | tf_op jit(solution)/shard_map/ppermute | solution.py:831
  9.6 0.5 collective-permute-start.4
  10.1 1.5 collective-permute-start
  11.6 18.0 %collective-permute-done.3.refs_4_ = f32[1024,128]{1,0:T(8,128)S(1)} collective-permute-done((f32[1024,128]{1,0:T(8,128)}, f32[1024,128]{1,0:T(8,128)S(1)}, u32[]{:S(2)}, u32[]{:S(2)}) %collective-permute-start.3) | collective-permute-done | bytes 524320 | tf_op jit(solution)/shard_map/ppermute | solution.py:831
  29.7 0.3 collective-permute-start.7
  30.0 0.6 fusion.11
  32.0 1.8 collective-permute-start.5
  34.1 3.1 %collective-permute-start.1 = (f32[1,8,64,128]{3,2,1,0:T(8,128)S(1)}, f32[1,8,64,128]{3,2,1,0:T(8,128)S(1)}, u32[]{:S(2)}, u32[]{:S(2)}) collective-permute-start(f32[1,8,64,128]{3,2,1,0:T(8,128)S(1)} %bitcast.39), channel_id=1, source_target_pairs={{0,8},{1,9},{2,10},{3,11},{4,12},{5,13},{6,14},{7,15},{8,0},{9,1},... | collective-permute-start | bytes 786440 | tf_op jit(solution)/shard_map/ppermute | solution.py:831
  37.2 1.7 collective-permute-start.19
  38.9 13.9 %collective-permute-done.5.refs_12_ = f32[512,128]{1,0:T(8,128)S(1)} collective-permute-done((f32[512,128]{1,0:T(8,128)}, f32[512,128]{1,0:T(8,128)S(1)}, u32[]{:S(2)}, u32[]{:S(2)}) %collective-permute-start.5) | collective-permute-done | bytes 262176 | tf_op jit(solution)/shard_map/ppermute | solution.py:831
  52.7 0.5 collective-permute-start.17
  53.3 4.5 %select_multiply_fusion = (f32[4,8,128,128]{3,2,1,0:T(8,128)}, f32[4,8,128,128]{3,2,1,0:T(8,128)}) fusion(f32[]{:T(128)S(6)} %mul.209, f32[4,128]{1,0:T(4,128)S(1)} %fusion.10, f32[8,128]{1,0:T(8,128)S(1)} %fusion.7, f32[]{:T(128)S(6)} %mul.172), kind=kLoop, calls=%fused_computation | loop fusion | flops 18350080 | bytes 4200456 | tf_op jit(solution)/shard_map/mul | solution.py:810
  57.8 1.8 collective-permute-start.8
  59.6 2.3 %collective-permute-done.1 = f32[1,8,64,128]{3,2,1,0:T(8,128)S(1)} collective-permute-done((f32[1,8,64,128]{3,2,1,0:T(8,128)S(1)}, f32[1,8,64,128]{3,2,1,0:T(8,128)S(1)}, u32[]{:S(2)}, u32[]{:S(2)}) %collective-permute-start.1) | collective-permute-done | bytes 262176 | tf_op jit(solution)/shard_map/ppermute | solution.py:831
  61.9 1.6 collective-permute-start.23
  63.6 2.4 %collective-permute-start.2 = (f32[2,8,64,128]{3,2,1,0:T(8,128)S(1)}, f32[2,8,64,128]{3,2,1,0:T(8,128)S(1)}, u32[]{:S(2)}, u32[]{:S(2)}) collective-permute-start(f32[2,8,64,128]{3,2,1,0:T(8,128)S(1)} %pad_maximum_fusion.2), channel_id=1, source_target_pairs={{0,4},{1,5},{2,6},{3,7},{4,0},{5,1},{6,2},{7,3},{8,12},{9,13},{10,... | collective-permute-start | bytes 1572872 | tf_op jit(solution)/shard_map/ppermute | solution.py:831
  66.1 1.5 collective-permute-done.8.refs_13_
  67.6 0.5 collective-permute-start.20
  68.1 0.2 collective-permute-done.23.refs_16_
  68.3 1.6 collective-permute-start.24
  69.9 4.7 %collective-permute-done.2 = f32[2,8,64,128]{3,2,1,0:T(8,128)S(1)} collective-permute-done((f32[2,8,64,128]{3,2,1,0:T(8,128)S(1)}, f32[2,8,64,128]{3,2,1,0:T(8,128)S(1)}, u32[]{:S(2)}, u32[]{:S(2)}) %collective-permute-start.2) | collective-permute-done | bytes 524320 | tf_op jit(solution)/shard_map/ppermute | solution.py:831
  74.6 1.8 collective-permute-done.24.refs_17_
  76.5 1.4 collective-permute-start.11
  78.1 0.7 copy-done.16
  78.9 0.7 copy-done.34
  79.6 14.5 %enter_columns.1 = (f32[8,528,128]{2,1,0:T(8,128)}, f32[8,528,128]{2,1,0:T(8,128)}) custom-call(s32[4]{0:T(128)} %pad_add_fusion.ids, f32[4,8,128,128]{3,2,1,0:T(8,128)} %get-tuple-element.88.filt_re, f32[4,8,128,128]{3,2,1,0:T(8,128)} %get-tuple-element.87.filt_im, bf16[512,256]{1,0:T(8,128)(2,1)} %constant.192.clone.ahead, ...), custom_call_target="tpu_custom_call" | custom-call | flops 8000000000 | bytes 8000000 | tf_op jit(solution)/shard_map/enter_columns/pallas_call | solution.py:157
  94.1 0.3 collective-permute-start.27
  94.4 0.3 collective-permute-start.12
  94.7 7.5 %collective-permute-done.11.refs_1_ = f32[4,8,64,128]{3,2,1,0:T(8,128)S(1)} collective-permute-done((f32[4,8,64,128]{3,2,1,0:T(8,128)S(1)}, f32[4,8,64,128]{3,2,1,0:T(8,128)S(1)}, u32[]{:S(2)}, u32[]{:S(2)}) %collective-permute-start.11) | collective-permute-done | bytes 1048608 | tf_op jit(solution)/shard_map/ppermute | solution.py:831
  102.2 3.4 %collective-permute-start.10 = (f32[1,1024]{1,0:T(1,128)S(1)}, f32[1,1024]{1,0:T(1,128)S(1)}, u32[]{:S(2)}, u32[]{:S(2)}) collective-permute-start(f32[1,1024]{1,0:T(1,128)S(1)} %get-tuple-element.52), channel_id=1, source_target_pairs={{1,0},{2,1},{3,2},{4,3},{5,4},{6,5},{7,6},{8,7},{9,8},{10,9},{11,1... | collective-permute-start | bytes 12296 | tf_op jit(solution)/shard_map/ppermute | solution.py:907
  105.6 2.1 collective-permute-start.9
  107.7 0.6 pad_maximum_fusion.5.scales
  108.3 2.3 collective-permute-done.9
  110.5 7.4 %prepare.1 = (f32[8,8,64,128]{3,2,1,0:T(8,128)}, f32[8,8,64,128]{3,2,1,0:T(8,128)}, f32[8,8,64,128]{3,2,1,0:T(8,128)}, f32[8,16,128]{2,1,0:T(8,128)}, f32[8,16,128]{2,1,0:T(8,128)}) custom-call(s32[4]{0:T(128)} %pad_add_fusion.ids, f32[2]{0:T(128)} %pad_maximum_fusion.5.scales, f32[4,8,64,128]{3,2,1,0:T(8,128)} %copy-done.1, f32[4,8,64,128]{3,2,1,0:T(8,128)} %copy-done.6, ...), custom_call_target="tpu_custom_call" | custom-call | flops 4000000000 | bytes 8000000 | tf_op jit(solution)/shard_map/prepare/pallas_call | solution.py:157
  117.9 18.8 %middle.1 = (f32[8,512,128]{2,1,0:T(8,128)}, f32[8,512,128]{2,1,0:T(8,128)}, f32[2,2,64,1024]{3,2,1,0:T(8,128)}, f32[2,2,64,1024]{3,2,1,0:T(8,128)}) custom-call(s32[4]{0:T(128)} %pad_add_fusion.ids, bf16[2,256,256]{2,1,0:T(8,128)(2,1)} %constant.191.clone.back, bf16[2,256,256]{2,1,0:T(8,128)(2,1)} %constant.190.clone.table.ahead, ...), custom_call_target="tpu_custom_call" | custom-call | flops 16000000000 | bytes 10000000 | tf_op jit(solution)/shard_map/middle/pallas_call | solution.py:157
  136.9 2.6 %collective-permute-start.28 = (f32[2,2,64,1024]{3,2,1,0:T(8,128)}, f32[2,2,64,1024]{3,2,1,0:T(8,128)S(1)}, u32[]{:S(2)}, u32[]{:S(2)}) collective-permute-start(f32[2,2,64,1024]{3,2,1,0:T(8,128)} %get-tuple-element.66), channel_id=1, source_target_pairs={{0,4},{1,5},{2,6},{3,7},{4,0},{5,1},{6,2},{7,3},{8,12},{9,13},{10,... | collective-permute-start | bytes 3145736 | tf_op jit(solution)/shard_map/ppermute | solution.py:831
  139.4 1.8 collective-permute-done.29.other
  141.2 1.3 copy-done.5
  142.5 14.3 %leave_columns.1 = (f32[528,128]{1,0:T(8,128)}, f32[528,128]{1,0:T(8,128)}, f32[528,128]{1,0:T(8,128)}, f32[528,128]{1,0:T(8,128)}, f32[528,128]{1,0:T(8,128)}, ...) custom-call(s32[4]{0:T(128)} %pad_add_fusion.ids, f32[4,8,128,128]{3,2,1,0:T(8,128)} %get-tuple-element.88.filt_re, ...), custom_call_target="tpu_custom_call" | custom-call | flops 8000000000 | bytes 8000000 | tf_op jit(solution)/shard_map/leave_columns/pallas_call | solution.py:157
  156.8 2.6 %collective-permute-start.30 = (f32[528,128]{1,0:T(8,128)}, f32[528,128]{1,0:T(8,128)S(1)}, u32[]{:S(2)}, u32[]{:S(2)}) collective-permute-start(f32[528,128]{1,0:T(8,128)} %get-tuple-element.69), channel_id=1, source_target_pairs={{0,4},{1,5},{2,6},{3,7},{4,0},{5,1},{6,2},{7,3},{8,12},{9,13},{10,... | collective-permute-start | bytes 811016 | tf_op jit(solution)/shard_map/ppermute | solution.py:831
  159.4 0.5 convert_multiply_fusion.angulars
  159.9 3.4 %collective-permute-start.37 = (f32[528,128]{1,0:T(8,128)}, f32[528,128]{1,0:T(8,128)S(1)}, u32[]{:S(2)}, u32[]{:S(2)}) collective-permute-start(f32[528,128]{1,0:T(8,128)} %get-tuple-element.77), channel_id=1, source_target_pairs={{0,8},{1,9},{2,10},{3,11},{4,12},{5,13},{6,14},{7,15},{8,0},{9,1},... | collective-permute-start | bytes 811016 | tf_op jit(solution)/shard_map/ppermute | solution.py:831
  163.4 0.3 collective-permute-done.28
  163.7 11.2 %collective-permute-done.30.refs_2_ = f32[528,128]{1,0:T(8,128)S(1)} collective-permute-done((f32[528,128]{1,0:T(8,128)}, f32[528,128]{1,0:T(8,128)S(1)}, u32[]{:S(2)}, u32[]{:S(2)}) %collective-permute-start.30) | collective-permute-done | bytes 270368 | tf_op jit(solution)/shard_map/ppermute | solution.py:831
  174.8 0.2 multiply_add_fusion
  175.0 1.9 collective-permute-start.31
  177.0 0.6 pad_maximum_fusion.4.beside
  177.6 2.6 %collective-permute-done.34 = f32[528,128]{1,0:T(8,128)S(1)} collective-permute-done((f32[528,128]{1,0:T(8,128)}, f32[528,128]{1,0:T(8,128)S(1)}, u32[]{:S(2)}, u32[]{:S(2)}) %collective-permute-start.34) | collective-permute-done | bytes 270368 | tf_op jit(solution)/shard_map/ppermute | solution.py:831
  180.2 9.6 %collective-permute-start.36 = (f32[528,128]{1,0:T(8,128)S(1)}, f32[528,128]{1,0:T(8,128)S(1)}, u32[]{:S(2)}, u32[]{:S(2)}) collective-permute-start(f32[528,128]{1,0:T(8,128)S(1)} %copy-done.19), channel_id=1, source_target_pairs={{0,8},{1,9},{2,10},{3,11},{4,12},{5,13},{6,14},{7,15},{8,0},{9,1},... | collective-permute-start | bytes 811016 | tf_op jit(solution)/shard_map/ppermute | solution.py:831
  189.9 0.5 collective-permute-start.38
  190.5 14.0 %collective-permute-done.36.refs_4_ = f32[528,128]{1,0:T(8,128)S(1)} collective-permute-done((f32[528,128]{1,0:T(8,128)S(1)}, f32[528,128]{1,0:T(8,128)S(1)}, u32[]{:S(2)}, u32[]{:S(2)}) %collective-permute-start.36) | collective-permute-done | bytes 270368 | tf_op jit(solution)/shard_map/ppermute | solution.py:831
  204.6 3.4 %collective-permute-start.32 = (f32[64,512]{1,0:T(8,128)S(1)}, f32[64,512]{1,0:T(8,128)S(1)}, u32[]{:S(2)}, u32[]{:S(2)}) collective-permute-start(f32[64,512]{1,0:T(8,128)S(1)} %dynamic-slice_bitcast_fusion.1), channel_id=1, source_target_pairs={{0,8},{1,9},{2,10},{3,11},{4,12},{5,13},{6,14},{7,15},{8,0},{9,1},... | collective-permute-start | bytes 393224 | tf_op jit(solution)/shard_map/ppermute | solution.py:831
  208.0 7.4 %collective-permute-done.39.refs_6_ = f32[528,128]{1,0:T(8,128)S(1)} collective-permute-done((f32[528,128]{1,0:T(8,128)S(1)}, f32[528,128]{1,0:T(8,128)S(1)}, u32[]{:S(2)}, u32[]{:S(2)}) %collective-permute-start.39) | collective-permute-done | bytes 270368 | tf_op jit(solution)/shard_map/ppermute | solution.py:831
  215.4 0.7 copy-done.22
  216.2 0.1 copy-done.24
  216.3 7.3 %last.1 = (f32[2,2,64,1024]{3,2,1,0:T(8,128)}, f32[2,2,64,1024]{3,2,1,0:T(8,128)}, f32[64,1024]{1,0:T(8,128)}) custom-call(s32[4]{0:T(128)} %pad_add_fusion.ids, f32[2]{0:T(128)} %convert_multiply_fusion.angulars, bf16[2,256,256]{2,1,0:T(8,128)(2,1)} %constant.191.clone.back, f32[2,8,1,128]{3,2,1,0:T(1,128)} %constant.194.clone.twist, f32[64,1024]{1,0:T(8,128)} %bitcast.43, ...), custom_call_target="tpu_custom_call" | custom-call | flops 8000000000 | bytes 8000000 | tf_op jit(solution)/shard_map/last/pallas_call | solution.py:157
  223.7 0.9 constant_dynamic-slice_fusion
  224.6 0.2 collective-permute-start.42
  224.9 4.8 %collective-permute-done.42 = f32[64,512]{1,0:T(8,128)S(1)} collective-permute-done((f32[64,512]{1,0:T(8,128)S(1)}, f32[64,512]{1,0:T(8,128)S(1)}, u32[]{:S(2)}, u32[]{:S(2)}) %collective-permute-start.42) | collective-permute-done | bytes 131104 | tf_op jit(solution)/shard_map/ppermute | solution.py:843
  229.6 0.9 add_bitcast_fusion
  230.6 0.7 pad_maximum_fusion.3
  (124 shorter events, 1.5 us)
Async XLA Ops:
  1.3 28.7 %copy-start.4 = (s32[2]{0:T(128)S(1)}, s32[2]{0:T(128)}, u32[]{:S(2)}) copy-start(s32[2]{0:T(128)} %param.13) | copy-start | bytes 28
  6.5 23.1 %collective-permute-start.3 = (f32[1024,128]{1,0:T(8,128)}, f32[1024,128]{1,0:T(8,128)S(1)}, u32[]{:S(2)}, u32[]{:S(2)}) collective-permute-start(f32[1024,128]{1,0:T(8,128)} %get-tuple-element.44), channel_id=1, source_target_pairs={{0,4},{1,5},{2,6},{3,7},{4,0},{5,1},{6,2},{7,3},{8,12},{9,13},{10,... | collective-permute-start | bytes 1572872 | tf_op jit(solution)/shard_map/ppermute | solution.py:831
  7.0 30.1 %collective-permute-start.6 = (f32[1024,128]{1,0:T(8,128)}, f32[1024,128]{1,0:T(8,128)S(1)}, u32[]{:S(2)}, u32[]{:S(2)}) collective-permute-start(f32[1024,128]{1,0:T(8,128)} %get-tuple-element.49), channel_id=1, source_target_pairs={{0,8},{1,9},{2,10},{3,11},{4,12},{5,13},{6,14},{7,15},{8,0},{9,1},... | collective-permute-start | bytes 1572872 | tf_op jit(solution)/shard_map/ppermute | solution.py:831
  9.6 29.2 %collective-permute-start.14 = (f32[1024,128]{1,0:T(8,128)}, f32[1024,128]{1,0:T(8,128)S(1)}, u32[]{:S(2)}, u32[]{:S(2)}) collective-permute-start(f32[1024,128]{1,0:T(8,128)} %get-tuple-element.46.refs_0_), channel_id=1, source_target_pairs={{0,1},{1,0},{2,3},{3,2},{4,5},{5,4},{6,7},{7,6},{8,9},{9,8},{10,11... | collective-permute-start | bytes 1572872 | tf_op jit(solution)/shard_map/ppermute | solution.py:831
  9.6 22.3 %collective-permute-start.4 = (f32[1024,128]{1,0:T(8,128)}, f32[1024,128]{1,0:T(8,128)S(1)}, u32[]{:S(2)}, u32[]{:S(2)}) collective-permute-start(f32[1024,128]{1,0:T(8,128)} %get-tuple-element.46.refs_0_), channel_id=1, source_target_pairs={{0,2},{1,3},{2,0},{3,1},{4,6},{5,7},{6,4},{7,5},{8,10},{9,11},{10,... | collective-permute-start | bytes 1572872 | tf_op jit(solution)/shard_map/ppermute | solution.py:831
  10.1 23.7 %collective-permute-start = (f32[1,64,1024]{2,1,0:T(8,128)S(1)}, f32[1,64,1024]{2,1,0:T(8,128)S(1)}, u32[]{:S(2)}, u32[]{:S(2)}) collective-permute-start(f32[1,64,1024]{2,1,0:T(8,128)S(1)} %copy-done.3), channel_id=1, source_target_pairs={{0,16},{16,0},{1,17},{17,1},{2,18},{18,2},{3,19},{19,3},{4,20},{20... | collective-permute-start | bytes 786440 | tf_op jit(solution)/shard_map/ppermute | solution.py:843
  29.7 28.1 %copy-start.7 = (f32[1024,128]{1,0:T(8,128)}, f32[1024,128]{1,0:T(8,128)S(1)}, u32[]{:S(2)}) copy-start(f32[1024,128]{1,0:T(8,128)S(1)} %collective-permute-done.3.refs_4_) | copy-start | bytes 1572868
  29.7 23.1 %collective-permute-start.7 = (f32[1024,128]{1,0:T(8,128)S(1)}, f32[1024,128]{1,0:T(8,128)}, u32[]{:S(2)}, u32[]{:S(2)}) collective-permute-start(f32[1024,128]{1,0:T(8,128)S(1)} %collective-permute-done.3.refs_4_), channel_id=1, source_target_pairs={{0,2},{1,3},{2,0},{3,1},{4,6},{5,7},{6,4},{7,5},{8,10},{9,11},{10,... | collective-permute-start | bytes 1572872 | tf_op jit(solution)/shard_map/ppermute | solution.py:831
  32.0 25.7 %copy-start.10 = (f32[1024,128]{1,0:T(8,128)}, f32[1024,128]{1,0:T(8,128)S(1)}, u32[]{:S(2)}) copy-start(f32[1024,128]{1,0:T(8,128)S(1)} %collective-permute-done.4.refs_2_) | copy-start | bytes 1572868
  32.0 20.8 %collective-permute-start.5 = (f32[512,128]{1,0:T(8,128)}, f32[512,128]{1,0:T(8,128)S(1)}, u32[]{:S(2)}, u32[]{:S(2)}) collective-permute-start(f32[512,128]{1,0:T(8,128)} %get-tuple-element.47), channel_id=1, source_target_pairs={{0,12},{1,13},{2,14},{3,15},{4,8},{5,9},{6,10},{7,11},{8,4},{9,5},... | collective-permute-start | bytes 786440 | tf_op jit(solution)/shard_map/ppermute | solution.py:831
  34.0 68.2 %copy-start.2 = (f32[1,1,64,1024]{3,2,1,0:T(8,128)}, f32[1,1,64,1024]{3,2,1,0:T(8,128)S(1)}, u32[]{:S(2)}) copy-start(f32[1,1,64,1024]{3,2,1,0:T(8,128)S(1)} %get-tuple-element.84) | copy-start | bytes 786436
  34.1 23.6 %copy-start.26 = (f32[512,128]{1,0:T(8,128)S(1)}, f32[512,128]{1,0:T(8,128)}, u32[]{:S(2)}) copy-start(f32[512,128]{1,0:T(8,128)} %get-tuple-element.50) | copy-start | bytes 786436
  34.1 27.8 %collective-permute-start.1 = (f32[1,8,64,128]{3,2,1,0:T(8,128)S(1)}, f32[1,8,64,128]{3,2,1,0:T(8,128)S(1)}, u32[]{:S(2)}, u32[]{:S(2)}) collective-permute-start(f32[1,8,64,128]{3,2,1,0:T(8,128)S(1)} %bitcast.39), channel_id=1, source_target_pairs={{0,8},{1,9},{2,10},{3,11},{4,12},{5,13},{6,14},{7,15},{8,0},{9,1},... | collective-permute-start | bytes 786440 | tf_op jit(solution)/shard_map/ppermute | solution.py:831
  37.2 28.8 %copy-start.8 = (f32[1024,128]{1,0:T(8,128)}, f32[1024,128]{1,0:T(8,128)S(1)}, u32[]{:S(2)}) copy-start(f32[1024,128]{1,0:T(8,128)S(1)} %collective-permute-done.6.refs_8_) | copy-start | bytes 1572868
  37.2 28.8 %collective-permute-start.19 = (f32[1024,128]{1,0:T(8,128)S(1)}, f32[1024,128]{1,0:T(8,128)S(1)}, u32[]{:S(2)}, u32[]{:S(2)}) collective-permute-start(f32[1024,128]{1,0:T(8,128)S(1)} %collective-permute-done.6.refs_8_), channel_id=1, source_target_pairs={{0,2},{1,3},{2,0},{3,1},{4,6},{5,7},{6,4},{7,5},{8,10},{9,11},{10,... | collective-permute-start | bytes 1572872 | tf_op jit(solution)/shard_map/ppermute | solution.py:831
  38.9 18.9 %copy-start.9 = (f32[1024,128]{1,0:T(8,128)}, f32[1024,128]{1,0:T(8,128)S(1)}, u32[]{:S(2)}) copy-start(f32[1024,128]{1,0:T(8,128)S(1)} %collective-permute-done.14.refs_1_) | copy-start | bytes 1572868
  38.9 24.7 %collective-permute-start.16 = (f32[1024,128]{1,0:T(8,128)S(1)}, f32[1024,128]{1,0:T(8,128)S(1)}, u32[]{:S(2)}, u32[]{:S(2)}) collective-permute-start(f32[1024,128]{1,0:T(8,128)S(1)} %collective-permute-done.3.refs_4_), channel_id=1, source_target_pairs={{0,1},{1,0},{2,3},{3,2},{4,5},{5,4},{6,7},{7,6},{8,9},{9,8},{10,11... | collective-permute-start | bytes 1572872 | tf_op jit(solution)/shard_map/ppermute | solution.py:831
  52.7 14.8 %copy-start.27 = (f32[512,128]{1,0:T(8,128)}, f32[512,128]{1,0:T(8,128)S(1)}, u32[]{:S(2)}) copy-start(f32[512,128]{1,0:T(8,128)S(1)} %collective-permute-done.5.refs_12_) | copy-start | bytes 786436
  52.7 5.0 %collective-permute-start.15 = (f32[1024,128]{1,0:T(8,128)S(1)}, f32[1024,128]{1,0:T(8,128)S(1)}, u32[]{:S(2)}, u32[]{:S(2)}) collective-permute-start(f32[1024,128]{1,0:T(8,128)S(1)} %collective-permute-done.4.refs_2_), channel_id=1, source_target_pairs={{0,1},{1,0},{2,3},{3,2},{4,5},{5,4},{6,7},{7,6},{8,9},{9,8},{10,11... | collective-permute-start | bytes 1572872 | tf_op jit(solution)/shard_map/ppermute | solution.py:831
  52.7 14.8 %collective-permute-start.17 = (f32[1024,128]{1,0:T(8,128)}, f32[1024,128]{1,0:T(8,128)S(1)}, u32[]{:S(2)}, u32[]{:S(2)}) collective-permute-start(f32[1024,128]{1,0:T(8,128)} %collective-permute-done.7.refs_6_), channel_id=1, source_target_pairs={{0,1},{1,0},{2,3},{3,2},{4,5},{5,4},{6,7},{7,6},{8,9},{9,8},{10,11... | collective-permute-start | bytes 1572872 | tf_op jit(solution)/shard_map/ppermute | solution.py:831
  57.7 20.3 %copy-start.13 = (f32[1024,128]{1,0:T(8,128)}, f32[1024,128]{1,0:T(8,128)S(1)}, u32[]{:S(2)}) copy-start(f32[1024,128]{1,0:T(8,128)S(1)} %collective-permute-done.15.refs_3_) | copy-start | bytes 1572868
  57.8 9.8 %collective-permute-start.8 = (f32[512,128]{1,0:T(8,128)S(1)}, f32[512,128]{1,0:T(8,128)S(1)}, u32[]{:S(2)}, u32[]{:S(2)}) collective-permute-start(f32[512,128]{1,0:T(8,128)S(1)} %copy-done.26), channel_id=1, source_target_pairs={{0,12},{1,13},{2,14},{3,15},{4,8},{5,9},{6,10},{7,11},{8,4},{9,5},... | collective-permute-start | bytes 786440 | tf_op jit(solution)/shard_map/ppermute | solution.py:831
  61.9 6.4 %collective-permute-start.23 = (f32[512,128]{1,0:T(8,128)S(1)}, f32[512,128]{1,0:T(8,128)S(1)}, u32[]{:S(2)}, u32[]{:S(2)}) collective-permute-start(f32[512,128]{1,0:T(8,128)S(1)} %collective-permute-done.5.refs_12_), channel_id=1, source_target_pairs={{0,2},{1,3},{2,0},{3,1},{4,6},{5,7},{6,4},{7,5},{8,10},{9,11},{10,... | collective-permute-start | bytes 786440 | tf_op jit(solution)/shard_map/ppermute | solution.py:831
  63.6 14.5 %copy-start.12 = (f32[1024,128]{1,0:T(8,128)}, f32[1024,128]{1,0:T(8,128)S(1)}, u32[]{:S(2)}) copy-start(f32[1024,128]{1,0:T(8,128)S(1)} %collective-permute-done.16.refs_5_) | copy-start | bytes 1572868
  63.6 11.0 %collective-permute-start.2 = (f32[2,8,64,128]{3,2,1,0:T(8,128)S(1)}, f32[2,8,64,128]{3,2,1,0:T(8,128)S(1)}, u32[]{:S(2)}, u32[]{:S(2)}) collective-permute-start(f32[2,8,64,128]{3,2,1,0:T(8,128)S(1)} %pad_maximum_fusion.2), channel_id=1, source_target_pairs={{0,4},{1,5},{2,6},{3,7},{4,0},{5,1},{6,2},{7,3},{8,12},{9,13},{10,... | collective-permute-start | bytes 1572872 | tf_op jit(solution)/shard_map/ppermute | solution.py:831
  66.0 12.0 %copy-start.11 = (f32[1024,128]{1,0:T(8,128)}, f32[1024,128]{1,0:T(8,128)S(1)}, u32[]{:S(2)}) copy-start(f32[1024,128]{1,0:T(8,128)S(1)} %collective-permute-done.19.refs_10_) | copy-start | bytes 1572868
  66.0 10.5 %collective-permute-start.18 = (f32[1024,128]{1,0:T(8,128)S(1)}, f32[1024,128]{1,0:T(8,128)S(1)}, u32[]{:S(2)}, u32[]{:S(2)}) collective-permute-start(f32[1024,128]{1,0:T(8,128)S(1)} %collective-permute-done.6.refs_8_), channel_id=1, source_target_pairs={{0,1},{1,0},{2,3},{3,2},{4,5},{5,4},{6,7},{7,6},{8,9},{9,8},{10,11... | collective-permute-start | bytes 1572872 | tf_op jit(solution)/shard_map/ppermute | solution.py:831
  67.6 10.5 %copy-start.28 = (f32[512,128]{1,0:T(8,128)}, f32[512,128]{1,0:T(8,128)S(1)}, u32[]{:S(2)}) copy-start(f32[512,128]{1,0:T(8,128)S(1)} %collective-permute-done.8.refs_13_) | copy-start | bytes 786436
  67.6 2.3 %collective-permute-start.21 = (f32[512,128]{1,0:T(8,128)S(1)}, f32[512,128]{1,0:T(8,128)S(1)}, u32[]{:S(2)}, u32[]{:S(2)}) collective-permute-start(f32[512,128]{1,0:T(8,128)S(1)} %collective-permute-done.5.refs_12_), channel_id=1, source_target_pairs={{0,1},{1,0},{2,3},{3,2},{4,5},{5,4},{6,7},{7,6},{8,9},{9,8},{10,11... | collective-permute-start | bytes 786440 | tf_op jit(solution)/shard_map/ppermute | solution.py:831
  67.6 10.5 %copy-start.14 = (f32[1024,128]{1,0:T(8,128)}, f32[1024,128]{1,0:T(8,128)S(1)}, u32[]{:S(2)}) copy-start(f32[1024,128]{1,0:T(8,128)S(1)} %collective-permute-done.17.refs_7_) | copy-start | bytes 1572868
  67.6 10.4 %collective-permute-start.20 = (f32[1024,128]{1,0:T(8,128)S(1)}, f32[1024,128]{1,0:T(8,128)S(1)}, u32[]{:S(2)}, u32[]{:S(2)}) collective-permute-start(f32[1024,128]{1,0:T(8,128)S(1)} %collective-permute-done.19.refs_10_), channel_id=1, source_target_pairs={{0,1},{1,0},{2,3},{3,2},{4,5},{5,4},{6,7},{7,6},{8,9},{9,8},{10,11... | collective-permute-start | bytes 1572872 | tf_op jit(solution)/shard_map/ppermute | solution.py:831
  68.3 9.8 %copy-start.29 = (f32[512,128]{1,0:T(8,128)}, f32[512,128]{1,0:T(8,128)S(1)}, u32[]{:S(2)}) copy-start(f32[512,128]{1,0:T(8,128)S(1)} %collective-permute-done.23.refs_16_) | copy-start | bytes 786436
  68.3 8.1 %collective-permute-start.24 = (f32[512,128]{1,0:T(8,128)S(1)}, f32[512,128]{1,0:T(8,128)S(1)}, u32[]{:S(2)}, u32[]{:S(2)}) collective-permute-start(f32[512,128]{1,0:T(8,128)S(1)} %collective-permute-done.8.refs_13_), channel_id=1, source_target_pairs={{0,2},{1,3},{2,0},{3,1},{4,6},{5,7},{6,4},{7,5},{8,10},{9,11},{10,... | collective-permute-start | bytes 786440 | tf_op jit(solution)/shard_map/ppermute | solution.py:831
  69.9 8.1 %collective-permute-start.25 = (f32[512,128]{1,0:T(8,128)S(1)}, f32[512,128]{1,0:T(8,128)S(1)}, u32[]{:S(2)}, u32[]{:S(2)}) collective-permute-start(f32[512,128]{1,0:T(8,128)S(1)} %collective-permute-done.23.refs_16_), channel_id=1, source_target_pairs={{0,1},{1,0},{2,3},{3,2},{4,5},{5,4},{6,7},{7,6},{8,9},{9,8},{10,11... | collective-permute-start | bytes 786440 | tf_op jit(solution)/shard_map/ppermute | solution.py:831
  74.6 3.4 %collective-permute-start.22 = (f32[512,128]{1,0:T(8,128)S(1)}, f32[512,128]{1,0:T(8,128)S(1)}, u32[]{:S(2)}, u32[]{:S(2)}) collective-permute-start(f32[512,128]{1,0:T(8,128)S(1)} %collective-permute-done.8.refs_13_), channel_id=1, source_target_pairs={{0,1},{1,0},{2,3},{3,2},{4,5},{5,4},{6,7},{7,6},{8,9},{9,8},{10,11... | collective-permute-start | bytes 786440 | tf_op jit(solution)/shard_map/ppermute | solution.py:831
  76.4 1.6 collective-permute-start.26
  76.5 17.9 %copy-start.1 = (f32[4,8,64,128]{3,2,1,0:T(8,128)}, f32[4,8,64,128]{3,2,1,0:T(8,128)S(1)}, u32[]{:S(2)}) copy-start(f32[4,8,64,128]{3,2,1,0:T(8,128)S(1)} %pad_maximum_fusion.refs_0_) | copy-start | bytes 3145732
  76.5 25.6 %collective-permute-start.11 = (f32[4,8,64,128]{3,2,1,0:T(8,128)S(1)}, f32[4,8,64,128]{3,2,1,0:T(8,128)S(1)}, u32[]{:S(2)}, u32[]{:S(2)}) collective-permute-start(f32[4,8,64,128]{3,2,1,0:T(8,128)S(1)} %pad_maximum_fusion.refs_0_), channel_id=1, source_target_pairs={{0,2},{1,3},{2,0},{3,1},{4,6},{5,7},{6,4},{7,5},{8,10},{9,11},{10,... | collective-permute-start | bytes 3145736 | tf_op jit(solution)/shard_map/ppermute | solution.py:831
  94.1 23.8 %collective-permute-start.27 = (f32[8,528,128]{2,1,0:T(8,128)}, f32[8,528,128]{2,1,0:T(8,128)}, u32[]{:S(2)}, u32[]{:S(2)}) collective-permute-start(f32[8,528,128]{2,1,0:T(8,128)} %get-tuple-element.64), channel_id=1, source_target_pairs={{0,1},{1,0},{2,3},{3,2},{4,5},{5,4},{6,7},{7,6},{8,9},{9,8},{10,11... | collective-permute-start | bytes 6488072 | tf_op jit(solution)/shard_map/ppermute | solution.py:831
  94.4 16.1 %collective-permute-start.12 = (f32[4,8,64,128]{3,2,1,0:T(8,128)S(1)}, f32[4,8,64,128]{3,2,1,0:T(8,128)}, u32[]{:S(2)}, u32[]{:S(2)}) collective-permute-start(f32[4,8,64,128]{3,2,1,0:T(8,128)S(1)} %pad_maximum_fusion.refs_0_), channel_id=1, source_target_pairs={{0,1},{1,0},{2,3},{3,2},{4,5},{5,4},{6,7},{7,6},{8,9},{9,8},{10,11... | collective-permute-start | bytes 3145736 | tf_op jit(solution)/shard_map/ppermute | solution.py:831
  102.2 8.3 %collective-permute-start.13 = (f32[4,8,64,128]{3,2,1,0:T(8,128)S(1)}, f32[4,8,64,128]{3,2,1,0:T(8,128)}, u32[]{:S(2)}, u32[]{:S(2)}) collective-permute-start(f32[4,8,64,128]{3,2,1,0:T(8,128)S(1)} %collective-permute-done.11.refs_1_), channel_id=1, source_target_pairs={{0,1},{1,0},{2,3},{3,2},{4,5},{5,4},{6,7},{7,6},{8,9},{9,8},{10,11... | collective-permute-start | bytes 3145736 | tf_op jit(solution)/shard_map/ppermute | solution.py:831
  102.2 6.1 %collective-permute-start.10 = (f32[1,1024]{1,0:T(1,128)S(1)}, f32[1,1024]{1,0:T(1,128)S(1)}, u32[]{:S(2)}, u32[]{:S(2)}) collective-permute-start(f32[1,1024]{1,0:T(1,128)S(1)} %get-tuple-element.52), channel_id=1, source_target_pairs={{1,0},{2,1},{3,2},{4,3},{5,4},{6,5},{7,6},{8,7},{9,8},{10,9},{11,1... | collective-permute-start | bytes 12296 | tf_op jit(solution)/shard_map/ppermute | solution.py:907
  105.6 4.9 %collective-permute-start.9 = (f32[1,1024]{1,0:T(1,128)S(1)}, f32[1,1024]{1,0:T(1,128)S(1)}, u32[]{:S(2)}, u32[]{:S(2)}) collective-permute-start(f32[1,1024]{1,0:T(1,128)S(1)} %get-tuple-element.51), channel_id=1, source_target_pairs={{0,1},{1,2},{2,3},{3,4},{4,5},{5,6},{6,7},{7,8},{8,9},{9,10},{10,1... | collective-permute-start | bytes 12296 | tf_op jit(solution)/shard_map/ppermute | solution.py:906
  136.8 4.4 %collective-permute-start.29 = (f32[8,512,128]{2,1,0:T(8,128)}, f32[8,512,128]{2,1,0:T(8,128)S(1)}, u32[]{:S(2)}, u32[]{:S(2)}) collective-permute-start(f32[8,512,128]{2,1,0:T(8,128)} %get-tuple-element.68), channel_id=1, source_target_pairs={{0,1},{1,0},{2,3},{3,2},{4,5},{5,4},{6,7},{7,6},{8,9},{9,8},{10,11... | collective-permute-start | bytes 6291464 | tf_op jit(solution)/shard_map/ppermute | solution.py:831
  136.9 26.8 %collective-permute-start.28 = (f32[2,2,64,1024]{3,2,1,0:T(8,128)}, f32[2,2,64,1024]{3,2,1,0:T(8,128)S(1)}, u32[]{:S(2)}, u32[]{:S(2)}) collective-permute-start(f32[2,2,64,1024]{3,2,1,0:T(8,128)} %get-tuple-element.66), channel_id=1, source_target_pairs={{0,4},{1,5},{2,6},{3,7},{4,0},{5,1},{6,2},{7,3},{8,12},{9,13},{10,... | collective-permute-start | bytes 3145736 | tf_op jit(solution)/shard_map/ppermute | solution.py:831
  142.5 32.3 %copy-start = (f32[2,2,64,1024]{3,2,1,0:T(8,128)S(1)}, f32[2,2,64,1024]{3,2,1,0:T(8,128)}, u32[]{:S(2)}) copy-start(f32[2,2,64,1024]{3,2,1,0:T(8,128)} %get-tuple-element.65) | copy-start | bytes 3145732
  156.8 23.4 %copy-start.19 = (f32[528,128]{1,0:T(8,128)S(1)}, f32[528,128]{1,0:T(8,128)}, u32[]{:S(2)}) copy-start(f32[528,128]{1,0:T(8,128)} %get-tuple-element.76) | copy-start | bytes 811012
  156.8 32.9 %copy-start.18 = (f32[528,128]{1,0:T(8,128)S(1)}, f32[528,128]{1,0:T(8,128)}, u32[]{:S(2)}) copy-start(f32[528,128]{1,0:T(8,128)} %get-tuple-element.78) | copy-start | bytes 811012
  156.8 18.0 %collective-permute-start.30 = (f32[528,128]{1,0:T(8,128)}, f32[528,128]{1,0:T(8,128)S(1)}, u32[]{:S(2)}, u32[]{:S(2)}) collective-permute-start(f32[528,128]{1,0:T(8,128)} %get-tuple-element.69), channel_id=1, source_target_pairs={{0,4},{1,5},{2,6},{3,7},{4,0},{5,1},{6,2},{7,3},{8,12},{9,13},{10,... | collective-permute-start | bytes 811016 | tf_op jit(solution)/shard_map/ppermute | solution.py:831
  159.9 20.2 %collective-permute-start.34 = (f32[528,128]{1,0:T(8,128)}, f32[528,128]{1,0:T(8,128)S(1)}, u32[]{:S(2)}, u32[]{:S(2)}) collective-permute-start(f32[528,128]{1,0:T(8,128)} %get-tuple-element.75), channel_id=1, source_target_pairs={{0,4},{1,5},{2,6},{3,7},{4,0},{5,1},{6,2},{7,3},{8,12},{9,13},{10,... | collective-permute-start | bytes 811016 | tf_op jit(solution)/shard_map/ppermute | solution.py:831
  159.9 29.8 %collective-permute-start.37 = (f32[528,128]{1,0:T(8,128)}, f32[528,128]{1,0:T(8,128)S(1)}, u32[]{:S(2)}, u32[]{:S(2)}) collective-permute-start(f32[528,128]{1,0:T(8,128)} %get-tuple-element.77), channel_id=1, source_target_pairs={{0,8},{1,9},{2,10},{3,11},{4,12},{5,13},{6,14},{7,15},{8,0},{9,1},... | collective-permute-start | bytes 811016 | tf_op jit(solution)/shard_map/ppermute | solution.py:831
  163.4 26.4 %collective-permute-start.40 = (f32[528,128]{1,0:T(8,128)}, f32[528,128]{1,0:T(8,128)S(1)}, u32[]{:S(2)}, u32[]{:S(2)}) collective-permute-start(f32[528,128]{1,0:T(8,128)} %get-tuple-element.79), channel_id=1, source_target_pairs={{0,12},{1,13},{2,14},{3,15},{4,8},{5,9},{6,10},{7,11},{8,4},{9,5},... | collective-permute-start | bytes 811016 | tf_op jit(solution)/shard_map/ppermute | solution.py:831
  163.7 26.2 %collective-permute-start.33 = (f32[528,128]{1,0:T(8,128)}, f32[528,128]{1,0:T(8,128)S(1)}, u32[]{:S(2)}, u32[]{:S(2)}) collective-permute-start(f32[528,128]{1,0:T(8,128)} %get-tuple-element.74), channel_id=1, source_target_pairs={{0,1},{1,0},{2,3},{3,2},{4,5},{5,4},{6,7},{7,6},{8,9},{9,8},{10,11... | collective-permute-start | bytes 811016 | tf_op jit(solution)/shard_map/ppermute | solution.py:831
  174.8 15.7 %copy-start.17 = (f32[528,128]{1,0:T(8,128)}, f32[528,128]{1,0:T(8,128)S(1)}, u32[]{:S(2)}) copy-start(f32[528,128]{1,0:T(8,128)S(1)} %collective-permute-done.30.refs_2_) | copy-start | bytes 811012
  175.0 15.3 %collective-permute-start.31 = (f32[2,64,512]{2,1,0:T(8,128)S(1)}, f32[2,64,512]{2,1,0:T(8,128)S(1)}, u32[]{:S(2)}, u32[]{:S(2)}) collective-permute-start(f32[2,64,512]{2,1,0:T(8,128)S(1)} %dynamic-slice_bitcast_fusion), channel_id=1, source_target_pairs={{0,16},{16,0},{1,17},{17,1},{2,18},{18,2},{3,19},{19,3},{4,20},{20... | collective-permute-start | bytes 786440 | tf_op jit(solution)/shard_map/ppermute | solution.py:843
  180.2 24.4 %collective-permute-start.36 = (f32[528,128]{1,0:T(8,128)S(1)}, f32[528,128]{1,0:T(8,128)S(1)}, u32[]{:S(2)}, u32[]{:S(2)}) collective-permute-start(f32[528,128]{1,0:T(8,128)S(1)} %copy-done.19), channel_id=1, source_target_pairs={{0,8},{1,9},{2,10},{3,11},{4,12},{5,13},{6,14},{7,15},{8,0},{9,1},... | collective-permute-start | bytes 811016 | tf_op jit(solution)/shard_map/ppermute | solution.py:831
  189.8 25.6 %collective-permute-start.39 = (f32[528,128]{1,0:T(8,128)S(1)}, f32[528,128]{1,0:T(8,128)S(1)}, u32[]{:S(2)}, u32[]{:S(2)}) collective-permute-start(f32[528,128]{1,0:T(8,128)S(1)} %copy-done.18), channel_id=1, source_target_pairs={{0,12},{1,13},{2,14},{3,15},{4,8},{5,9},{6,10},{7,11},{8,4},{9,5},... | collective-permute-start | bytes 811016 | tf_op jit(solution)/shard_map/ppermute | solution.py:831
  189.8 25.6 %collective-permute-start.35 = (f32[528,128]{1,0:T(8,128)S(1)}, f32[528,128]{1,0:T(8,128)S(1)}, u32[]{:S(2)}, u32[]{:S(2)}) collective-permute-start(f32[528,128]{1,0:T(8,128)S(1)} %collective-permute-done.34), channel_id=1, source_target_pairs={{0,1},{1,0},{2,3},{3,2},{4,5},{5,4},{6,7},{7,6},{8,9},{9,8},{10,11... | collective-permute-start | bytes 811016 | tf_op jit(solution)/shard_map/ppermute | solution.py:831
  189.9 25.6 %copy-start.20 = (f32[528,128]{1,0:T(8,128)}, f32[528,128]{1,0:T(8,128)S(1)}, u32[]{:S(2)}) copy-start(f32[528,128]{1,0:T(8,128)S(1)} %collective-permute-done.33.refs_1_) | copy-start | bytes 811012
  189.9 25.5 %collective-permute-start.38 = (f32[528,128]{1,0:T(8,128)S(1)}, f32[528,128]{1,0:T(8,128)S(1)}, u32[]{:S(2)}, u32[]{:S(2)}) collective-permute-start(f32[528,128]{1,0:T(8,128)S(1)} %collective-permute-done.37), channel_id=1, source_target_pairs={{0,1},{1,0},{2,3},{3,2},{4,5},{5,4},{6,7},{7,6},{8,9},{9,8},{10,11... | collective-permute-start | bytes 811016 | tf_op jit(solution)/shard_map/ppermute | solution.py:831
  190.4 25.0 %collective-permute-start.41 = (f32[528,128]{1,0:T(8,128)S(1)}, f32[528,128]{1,0:T(8,128)S(1)}, u32[]{:S(2)}, u32[]{:S(2)}) collective-permute-start(f32[528,128]{1,0:T(8,128)S(1)} %collective-permute-done.40), channel_id=1, source_target_pairs={{0,1},{1,0},{2,3},{3,2},{4,5},{5,4},{6,7},{7,6},{8,9},{9,8},{10,11... | collective-permute-start | bytes 811016 | tf_op jit(solution)/shard_map/ppermute | solution.py:831
  204.6 10.9 %copy-start.21 = (f32[528,128]{1,0:T(8,128)}, f32[528,128]{1,0:T(8,128)S(1)}, u32[]{:S(2)}) copy-start(f32[528,128]{1,0:T(8,128)S(1)} %collective-permute-done.36.refs_4_) | copy-start | bytes 811012
  204.6 20.3 %collective-permute-start.32 = (f32[64,512]{1,0:T(8,128)S(1)}, f32[64,512]{1,0:T(8,128)S(1)}, u32[]{:S(2)}, u32[]{:S(2)}) collective-permute-start(f32[64,512]{1,0:T(8,128)S(1)} %dynamic-slice_bitcast_fusion.1), channel_id=1, source_target_pairs={{0,8},{1,9},{2,10},{3,11},{4,12},{5,13},{6,14},{7,15},{8,0},{9,1},... | collective-permute-start | bytes 393224 | tf_op jit(solution)/shard_map/ppermute | solution.py:831
  224.6 5.0 %collective-permute-start.42 = (f32[64,512]{1,0:T(8,128)S(1)}, f32[64,512]{1,0:T(8,128)S(1)}, u32[]{:S(2)}, u32[]{:S(2)}) collective-permute-start(f32[64,512]{1,0:T(8,128)S(1)} %constant_dynamic-slice_fusion), channel_id=1, source_target_pairs={{0,16},{16,0},{1,17},{17,1},{2,18},{18,2},{3,19},{19,3},{4,20},{20... | collective-permute-start | bytes 393224 | tf_op jit(solution)/shard_map/ppermute | solution.py:843
  (14 other events, 36.7 us)

commit v3 on v2

--- a/solution.py
+++ b/solution.py
@@ -18,7 +18,7 @@
 
 LANES = 128
 ROWS = 16
-VMEM_LIMIT = 56 * 1024 * 1024
+MIB = 1024 * 1024
 ANY = pl.BlockSpec(memory_space=pl.ANY)
 VMEM = pl.BlockSpec(memory_space=pltpu.VMEM)
 SMEM = pl.BlockSpec(memory_space=pltpu.SMEM)
@@ -153,14 +153,14 @@
         copy.wait()
 
 
-def call(kernel, name, out_shape, in_specs, out_specs, scratch, flops, moved, args):
+def call(kernel, name, out_shape, in_specs, out_specs, scratch, limit, flops, moved, args):
     return pl.pallas_call(
         kernel,
         out_shape=out_shape,
         in_specs=in_specs,
         out_specs=out_specs,
         scratch_shapes=scratch,
-        compiler_params=pltpu.CompilerParams(vmem_limit_bytes=VMEM_LIMIT),
+        compiler_params=pltpu.CompilerParams(vmem_limit_bytes=limit * MIB),
         cost_estimate=pl.CostEstimate(flops=flops, bytes_accessed=moved, transcendentals=0),
         name=name,
     )(*args)
@@ -249,68 +249,84 @@
             pltpu.VMEM((count, tall, LANES), F32),
             pltpu.SemaphoreType.DMA((count + 2 * len(shapes),)),
         ],
+        56,
         count * 1000000000,
         count * 1000000,
         (ids, source, receiver, tab["right_forward"], tab["twist_y"]),
     )
 
 
-def shift_pair(pair, rows, data, filt_re, filt_im, ahead, back, twist, high, low, line):
+def shift_columns(pairs, ready, leave, rows, data, filt_re, filt_im, ahead, back, twist, high, low, line):
     radix = twist.shape[1]
     per = rows // ROWS
 
     def spot(k, part, a, t):
         index = a * (LANES // ROWS) + t
-        block, inner = lax.div(index, per), lax.rem(index, per)
-        start = pl.multiple_of((2 * k + part) * rows + inner * ROWS, ROWS)
-        return lax.div(block, 2), lax.rem(block, 2), pl.ds(start, ROWS)
-
-    def fold(t, carry):
-        off = pl.multiple_of(t * ROWS, ROWS)
-        row = pl.ds(off, ROWS)
+        block, inner = index // per, index % per
+        start = (2 * k + part) * rows + inner * ROWS
+        return block // 2, block % 2, slice(start, start + ROWS)
+
+    def fold(pair, t):
+        slot = pair % 2
+        off = t * ROWS
+        row = slice(off, off + ROWS)
         for kk in (0, 1):
-            real, imag = ([data[spot(pair + kk, part, a, t)] for a in range(radix)] for part in (0, 1))
+            real, imag = ([data[spot(2 * pair + kk, part, a, t)] for a in range(radix)] for part in (0, 1))
             real, imag = small_dft(real, imag, -1)
             for k in range(radix):
                 turn_pair = turned(real[k], imag[k], twist, k, row, False)
                 for part in (0, 1):
                     h, l = parts(turn_pair[part])
-                    high[k, pl.ds(part * LANES + off, ROWS), lanes(kk)] = h
-                    low[k, pl.ds(part * LANES + off, ROWS), lanes(kk)] = l
-        return carry
-
-    lax.fori_loop(0, LANES // ROWS, fold, 0)
-
-    def spectral(k, carry):
-        value = dot_left(ahead, high[k], low[k])
+                    at = slice(part * LANES + off, part * LANES + off + ROWS)
+                    high[slot, k, at, lanes(kk)] = h
+                    low[slot, k, at, lanes(kk)] = l
+
+    def spectral(pair, k):
+        slot = pair % 2
+        value = dot_left(ahead, high[slot, k], low[slot, k])
         re, im = value[:LANES], value[LANES:]
-        fr = jnp.concatenate([filt_re[pair, k], filt_re[pair + 1, k]], axis=1)
-        fi = jnp.concatenate([filt_im[pair, k], filt_im[pair + 1, k]], axis=1)
+        fr = jnp.concatenate([filt_re[2 * pair, k], filt_re[2 * pair + 1, k]], axis=1)
+        fi = jnp.concatenate([filt_im[2 * pair, k], filt_im[2 * pair + 1, k]], axis=1)
         both = jnp.concatenate([re * fr - im * fi, re * fi + im * fr], axis=0)
         h, l = parts(both)
-        line[k] = dot_left(back, h, l)
-        return carry
-
-    lax.fori_loop(0, radix, spectral, 0, unroll=4)
-
-    def unfold(t, carry):
-        off = pl.multiple_of(t * ROWS, ROWS)
-        row = pl.ds(off, ROWS)
+        line[slot, k] = dot_left(back, h, l)
+
+    def unfold(pair, t):
+        slot = pair % 2
+        off = t * ROWS
+        row = slice(off, off + ROWS)
         for kk in (0, 1):
             real, imag = [], []
             for k in range(radix):
-                re = line[k, pl.ds(off, ROWS), lanes(kk)]
-                im = line[k, pl.ds(LANES + off, ROWS), lanes(kk)]
+                re = line[slot, k, off : off + ROWS, lanes(kk)]
+                im = line[slot, k, LANES + off : LANES + off + ROWS, lanes(kk)]
                 re, im = turned(re, im, twist, k, row, True)
                 real.append(re)
                 imag.append(im)
             both = small_dft(real, imag, 1)
             for part in (0, 1):
                 for a in range(radix):
-                    data[spot(pair + kk, part, a, t)] = both[part][a]
-        return carry
-
-    lax.fori_loop(0, LANES // ROWS, unfold, 0)
+                    data[spot(2 * pair + kk, part, a, t)] = both[part][a]
+
+    chunks = LANES // ROWS
+    ready(0)
+    for t in range(chunks):
+        fold(0, t)
+    for pair in range(pairs):
+        if pair + 1 < pairs:
+            ready(pair + 1)
+        for t in range(max(radix, chunks)):
+            if t < radix:
+                spectral(pair, t)
+            if t < chunks and pair + 1 < pairs:
+                fold(pair + 1, t)
+            if t < chunks and pair > 0:
+                unfold(pair - 1, t)
+        if pair > 0:
+            leave(pair - 1)
+    for t in range(chunks):
+        unfold(pairs - 1, t)
+    leave(pairs - 1)
 
 
 def outer_rows(rows, half, data):
@@ -358,11 +374,13 @@
         arrivals.append(copies(*moves))
     done(first)
     leaving = []
-    for p in range(pairs):
-        done(arrivals[p])
-        shift_pair(2 * p, rows, data, fre, fim, ahead, back, tw, high, low, line)
+
+    def leave(p):
         lot = pl.ds(4 * p * rows, 4 * rows)
-        leaving += copies(*[(data.at[:, par, lot], out.at[:, lot]) for out, par in ((send, 1 - core), (keep, core))])
+        leaving.extend(copies(*[(data.at[:, par, lot], out.at[:, lot]) for out, par in ((send, 1 - core), (keep, core))]))
+
+    ready = lambda p: done(arrivals[p])
+    shift_columns(pairs, ready, leave, rows, data, fre, fim, ahead, back, tw, high, low, line)
     outer_rows(rows, half, data)
     lot = pl.ds(2 * half * rows, 4 * half)
     leaving += copies(*[(data.at[:, par, lot], out.at[:, lot]) for out, par in ((send, 1 - core), (keep, core))])
@@ -384,14 +402,13 @@
         moves += [(a.at[pl.ds(2 * p, 2)], b.at[pl.ds(2 * p, 2)]) for a, b in ((filt_re, fre), (filt_im, fim))]
         arrivals.append(copies(*moves))
     done(first)
-    for p in range(pairs):
-        done(arrivals[p])
-        shift_pair(2 * p, rows, data, fre, fim, ahead, back, tw, high, low, line)
+    ready = lambda p: done(arrivals[p])
+    shift_columns(pairs, ready, lambda p: None, rows, data, fre, fim, ahead, back, tw, high, low, line)
     outer_rows(rows, half, data)
     moves = []
     for e in range(groups):
         for h in (0, 1):
-            moves.append((data.at[(z ^ e) * across + y, core ^ h], outs[2 * e + h]))
+            moves.append((data.at[(z ^ e) * across + y, core ^ h], outs[e].at[h]))
     done(copies(*moves))
 
 
@@ -402,9 +419,9 @@
         pltpu.VMEM((half, radix, LANES, LANES), F32),
         pltpu.VMEM((half, radix, LANES, LANES), F32),
         pltpu.VMEM((2, radix, LANES, LANES), F32),
-        pltpu.VMEM((radix, 2 * LANES, 2 * LANES), BF16),
-        pltpu.VMEM((radix, 2 * LANES, 2 * LANES), BF16),
-        pltpu.VMEM((radix, 2 * LANES, 2 * LANES), F32),
+        pltpu.VMEM((2, radix, 2 * LANES, 2 * LANES), BF16),
+        pltpu.VMEM((2, radix, 2 * LANES, 2 * LANES), BF16),
+        pltpu.VMEM((2, radix, 2 * LANES, 2 * LANES), F32),
         pltpu.SemaphoreType.DMA((copies,)),
     ]
 
@@ -420,6 +437,7 @@
         [SMEM, ANY, ANY, VMEM, VMEM, ANY] + [ANY] * len(pieces),
         (ANY, ANY),
         column_scratch(half, count, rows, 1 + pairs * (2 * count + 4) + 2),
+        56,
         8000000000,
         8000000,
         (ids, *filt, tab["left_forward"], tab["left_inverse"], tab["twist_x"], *pieces),
@@ -428,14 +446,15 @@
 
 def leave_columns(ids, mine, other, filt, tab, groups, across, rows, half):
     count = groups * across
-    out = jax.ShapeDtypeStruct((2 * half * rows + 4 * half, LANES), F32)
+    out = jax.ShapeDtypeStruct((2, 2 * half * rows + 4 * half, LANES), F32)
     return call(
         functools.partial(leave_kernel, groups, across, rows),
         "leave_columns",
-        (out,) * (2 * groups),
+        (out,) * groups,
         [SMEM, ANY, ANY, VMEM, VMEM, ANY, ANY, ANY],
-        (ANY,) * (2 * groups),
+        (ANY,) * groups,
         column_scratch(half, count, rows, 1 + 2 * half + 2 * groups),
+        19,
         8000000000,
         8000000,
         (ids, *filt, tab["left_forward"], tab["left_inverse"], tab["twist_x"], mine, other),
@@ -443,10 +462,8 @@
 
 
 def turn(square):
-    cosine, ratio = 1.0, 1.0
-    for n in (4, 3, 2, 1):
-        cosine = 1.0 - cosine * square * (1.0 / ((2 * n - 1) * (2 * n)))
-        ratio = 1.0 - ratio * square * (1.0 / ((2 * n) * (2 * n + 1)))
+    cosine = 1.0 + square * (-1.0 / 2 + square * (1.0 / 24 + square * (-1.0 / 720)))
+    ratio = 1.0 + square * (-1.0 / 6 + square * (1.0 / 120 + square * (-1.0 / 5040)))
     return cosine, ratio
 
 
@@ -528,51 +545,58 @@
         pairs = ((out.at[1, i], send.at[i]), (out.at[0, i], keep.at[i]))
         return [pltpu.make_async_copy(a, b, block_sems.at[i, n]) for n, (a, b) in enumerate(pairs)]
 
-    def block(i, carry):
-        done(arrivals(i))
-        real, imag = inverse_tiles(
-            lambda k, part: data[k // half, i, (2 * (k % half) + part) * rows : (2 * (k % half) + part + 1) * rows, :],
-            rows,
-            back,
-            twist,
-        )
-        for a in range(radix):
-            c, s = cos[i, a], sin[i, a]
-            field[0, a] = real[a] * c - imag[a] * s
-            field[1, a] = real[a] * s + imag[a] * c
-
-        def store(part, a, value):
-            fresh[part, i, :, lanes(a)] = value
-
-        stencil(
-            lambda part, a: field[part, a],
-            lambda part, side, a: edge[part, a, pl.ds(2 * i + side, 1), :],
-            (radix, lambda a: wei[i, a]),
-            sign,
-            store,
-        )
-
-        def fold(t, carry):
-            row = pl.ds(pl.multiple_of(t * ROWS, ROWS), ROWS)
-            forward_into(
-                lambda a: (fresh[0, i, row, lanes(a)], fresh[1, i, row, lanes(a)]), row, twist, high, low, lambda k: (k,)
+    def step(j, carry):
+        for b in (0, 1):
+            i = 2 * j + b
+            done(arrivals(i))
+            real, imag = inverse_tiles(
+                lambda k, part: data[k // half, i, (2 * (k % half) + part) * rows : (2 * (k % half) + part + 1) * rows, :],
+                rows,
+                back,
+                twist,
             )
-            return carry
-
-        lax.fori_loop(0, rows // ROWS, fold, 0)
-        for slot, start in ((1, (1 - core) * half), (0, core * half)):
-            h = high[pl.ds(start, half)].reshape(half * rows, 2 * LANES)
-            l = low[pl.ds(start, half)].reshape(half * rows, 2 * LANES)
-            result = dot_right(h, l, ahead)
-            for k in range(half):
-                for part in (0, 1):
-                    at = 2 * k + part
-                    out[slot, i, at * rows : (at + 1) * rows, :] = result[k * rows : (k + 1) * rows, lanes(part)]
-        for copy in departures(i):
-            copy.start()
+            for a in range(radix):
+                c, s = cos[i, a], sin[i, a]
+                field[b, 0, a] = real[a] * c - imag[a] * s
+                field[b, 1, a] = real[a] * s + imag[a] * c
+        for b in (0, 1):
+            i = 2 * j + b
+
+            def store(part, a, value):
+                fresh[part, i, :, lanes(a)] = value
+
+            stencil(
+                lambda part, a: field[b, part, a],
+                lambda part, side, a: edge[part, a, pl.ds(2 * i + side, 1), :],
+                (radix, lambda a: wei[i, a]),
+                sign,
+                store,
+            )
+            for t in range(rows // ROWS):
+                row = slice(t * ROWS, (t + 1) * ROWS)
+                forward_into(
+                    lambda a: (fresh[0, i, row, lanes(a)], fresh[1, i, row, lanes(a)]),
+                    row,
+                    twist,
+                    high,
+                    low,
+                    lambda k: (b, k),
+                )
+        for b in (0, 1):
+            i = 2 * j + b
+            for slot, start in ((1, (1 - core) * half), (0, core * half)):
+                h = high[b, pl.ds(start, half)].reshape(half * rows, 2 * LANES)
+                l = low[b, pl.ds(start, half)].reshape(half * rows, 2 * LANES)
+                result = dot_right(h, l, ahead)
+                for k in range(half):
+                    for part in (0, 1):
+                        at = 2 * k + part
+                        out[slot, i, at * rows : (at + 1) * rows, :] = result[k * rows : (k + 1) * rows, lanes(part)]
+            for copy in departures(i):
+                copy.start()
         return carry
 
-    lax.fori_loop(0, count, block, 0)
+    lax.fori_loop(0, count // 2, step, 0)
     leaving = []
     for target, parity in ((far, 1 - which), (near, which)):
         for t in range(groups // 2):
@@ -606,15 +630,16 @@
             blocks,
             blocks,
             blocks,
-            pltpu.VMEM((2, radix, rows, LANES), F32),
+            pltpu.VMEM((2, 2, radix, rows, LANES), F32),
             pltpu.VMEM((2, radix, 2 * count, LANES), F32),
             pltpu.VMEM((2, count, rows, width), F32),
-            pltpu.VMEM((radix, rows, 2 * LANES), BF16),
-            pltpu.VMEM((radix, rows, 2 * LANES), BF16),
+            pltpu.VMEM((2, radix, rows, 2 * LANES), BF16),
+            pltpu.VMEM((2, radix, rows, 2 * LANES), BF16),
             pltpu.VMEM((2, count, 2 * half * rows, LANES), F32),
             pltpu.SemaphoreType.DMA((count, 5)),
             pltpu.SemaphoreType.DMA((2 + groups,)),
         ],
+        23,
         16000000000,
         10000000,
         (
@@ -633,29 +658,42 @@
     )
 
 
-def prepare_kernel(groups, across, ids, scales, *refs):
-    number = across
+def prepare_kernel(groups, across, lots, ids, scales, *refs):
+    number = len(lots)
     pieces, others = refs[:number], refs[number : 2 * number]
-    cosine, sine, weight, halo_cos, halo_sin, speed, lasts, firsts, sems = refs[2 * number :]
+    outs, (halo_cos, halo_sin, ends) = refs[2 * number : 2 * number + 3], refs[2 * number + 3 : 2 * number + 6]
+    speed, held, lasts, firsts, later, block_sems, sems = refs[2 * number + 6 :]
     z, y, core = ids[0], ids[1], ids[2]
     count, radix, rows, _ = speed.shape
     one = jnp.ones((radix, 8, LANES), F32)
     lasts[0] = one
     firsts[count] = one
+    later[0] = one
+    later[count] = one
     copies = Copies(sems)
-    moves, beside = [], []
-    for r in range(across):
-        for n, e in enumerate(gather_order(groups)):
+    moves, beside, places = [], [], []
+    for piece, other, (offsets, r) in zip(pieces, others, lots):
+        for n, e in enumerate(offsets):
             block = (z ^ e) * across + (y ^ r)
-            moves.append((pieces[r].at[n], speed.at[block]))
-            beside.append((others[r].at[n, :, pl.ds(rows - 8, 8)], lasts.at[block + 1 - core]))
-            beside.append((others[r].at[n, :, pl.ds(0, 8)], firsts.at[block + 1 - core]))
+            places.append((e, r))
+            moves.append((piece.at[n, :, pl.ds(0, rows)], speed.at[len(moves)]))
+            beside.append((other.at[n, :, pl.ds(16, 8)], later.at[block + 1 - core]))
+            beside.append((other.at[n, :, pl.ds(8, 8)], lasts.at[block + 1 - core]))
+            beside.append((other.at[n, :, pl.ds(0, 8)], firsts.at[block + 1 - core]))
     moves, beside = copies(*moves), copies(*beside)
     done(moves)
 
+    def departures(i):
+        e = sum(jnp.where(i == at, e, 0) for at, (e, _) in enumerate(places))
+        r = sum(jnp.where(i == at, r, 0) for at, (_, r) in enumerate(places))
+        block = (z ^ e) * across + (y ^ r)
+        return [pltpu.make_async_copy(held.at[m, i], outs[m].at[block], block_sems.at[i, m]) for m in range(3)]
+
     def chunk(i, carry):
         for a in range(radix):
-            cosine[i, a], sine[i, a], weight[i, a] = correction(speed[i, a], scales[0], scales[1])
+            held[0, i, a], held[1, i, a], held[2, i, a] = correction(speed[i, a], scales[0], scales[1])
+        for copy in departures(i):
+            copy.start()
         return carry
 
     lax.fori_loop(0, count, chunk, 0)
@@ -665,25 +703,40 @@
         for i in range(count):
             rows_beside += [lasts[i, a, 7:8, :], firsts[i + 1, a, 0:1, :]]
         halo_cos[a], halo_sin[a], _ = correction(jnp.concatenate(rows_beside, axis=0), scales[0], scales[1])
-
-
-def prepare(ids, scales, pieces, others, groups, across):
-    _, radix, rows, _ = pieces[0].shape
+    mine = z * across + y
+    for a in range(radix):
+        ends[a] = jnp.concatenate([later[mine, a, 1:2, :], later[mine + 1, a, 0:1, :]], axis=0)
+
+    def settle(i, carry):
+        done(departures(i))
+        return carry
+
+    lax.fori_loop(0, count, settle, 0)
+
+
+def prepare(ids, scales, books, others, groups, across, rows):
+    pieces = [held for held, _, _ in books]
+    lots = [(tuple(offsets), r) for _, offsets, r in books]
+    radix = pieces[0].shape[1]
     count = groups * across
     out = jax.ShapeDtypeStruct((count, radix, rows, LANES), F32)
     halo = jax.ShapeDtypeStruct((radix, 2 * count, LANES), F32)
     return call(
-        functools.partial(prepare_kernel, groups, across),
+        functools.partial(prepare_kernel, groups, across, lots),
         "prepare",
-        (out, out, out, halo, halo),
+        (out, out, out, halo, halo, jax.ShapeDtypeStruct((radix, 2, LANES), F32)),
         [SMEM] * 2 + [ANY] * (2 * len(pieces)),
-        (VMEM,) * 5,
+        (ANY,) * 3 + (VMEM,) * 3,
         [
             pltpu.VMEM((count, radix, rows, LANES), F32),
+            pltpu.VMEM((3, count, radix, rows, LANES), F32),
             pltpu.VMEM((count + 1, radix, 8, LANES), F32),
             pltpu.VMEM((count + 1, radix, 8, LANES), F32),
-            pltpu.SemaphoreType.DMA((3 * len(pieces) * groups,)),
+            pltpu.VMEM((count + 1, radix, 8, LANES), F32),
+            pltpu.SemaphoreType.DMA((count, 3)),
+            pltpu.SemaphoreType.DMA((4 * count,)),
         ],
+        11,
         4000000000,
         8000000,
         (ids, scales, *pieces, *others),
@@ -698,7 +751,7 @@
     half = radix // 2
     copies = Copies(sems)
     arrivals = copies(
-        *[(pieces[2 * e + h], data.at[z ^ e, core ^ h]) for e in range(groups) for h in (0, 1)]
+        *[(pieces[2 * e + h].at[h], data.at[z ^ e, core ^ h]) for e in range(groups) for h in (0, 1)]
     )
     done(arrivals)
 
@@ -712,7 +765,7 @@
     real, imag = inverse_tiles(halo_rows, tall, back, twist)
     for a in range(radix):
         for g in range(groups):
-            c, s, _ = correction(beside[:, lanes(a)], angulars[g // 2], 2.0 * (g % 2) - 1.0)
+            c, s, _ = correction(beside[a], angulars[g // 2], 2.0 * (g % 2) - 1.0)
             pair = slice(2 * g, 2 * g + 2)
             edge[0, a, pair, :] = real[a][pair] * c - imag[a][pair] * s
             edge[1, a, pair, :] = real[a][pair] * s + imag[a][pair] * c
@@ -768,6 +821,7 @@
             pltpu.VMEM((3, radix, rows, LANES), F32),
             pltpu.SemaphoreType.DMA((2 * groups,)),
         ],
+        12,
         8000000000,
         8000000,
         (ids, angulars, tab["right_inverse"], tab["twist_y"], speed, beside, *pieces),
@@ -892,28 +946,29 @@
         pieces[e] = [swap_z(messages[e][0], e)]
     for e in range(1, final):
         share(e)
-    book = jnp.swapaxes(speeds[0].reshape(rows, -1, LANES), 0, 1)[None]
-    book = jnp.concatenate([book, swap_z(book, top)])
+    book = jnp.concatenate([speeds[0], speeds[1][:1], speeds[1][-1:], jnp.zeros((6, width), F32)])
+    book = jnp.swapaxes(book.reshape(rows + 8, -1, LANES), 0, 1)[None]
+    books = [(book, [0]), (swap_z(book, top), [top])]
     pieces[final] = []
     for i, message in enumerate(messages[final]):
         ready = (pieces[1], full[0][2]) if i == 0 else (pieces[top], full[1][2], filt)
         pieces[final].append(swap_z(after(message, ready), final))
     for bit in bits(groups)[1:]:
-        book = jnp.concatenate([book, swap_z(book, bit)])
+        book, offsets = jnp.concatenate([held for held, _ in books]), [e for _, lot in books for e in lot]
+        books = [(book, offsets), (swap_z(book, bit), [e ^ bit for e in offsets])]
     share(final, *([(full[0], full[1][2])] + [(full[1], full[top][2])] * (half // 2 - 1)))
-    books = [swap_y(after(book, pieces[final]), r) if r else book for r in range(across)]
-    facing = [swap_core(part) for part in books]
-    tops = lax.ppermute(after(speeds[1][-1:], pieces[final]), "strip", [(i, i + 1) for i in range(strips - 1)])
-    tails = lax.ppermute(after(speeds[1][:1], pieces[final]), "strip", [(i + 1, i) for i in range(strips - 1)])
-
+    books = [(held, lot, 0) for held, lot in books] + [
+        (swap_y(held if n == 0 else after(held, pieces[final]), r), lot, r)
+        for n, (held, lot) in enumerate(books)
+        for r in range(1, across)
+    ]
+    edges = lambda held: jnp.concatenate([held[:, :, :8], held[:, :, rows - 8 :]], axis=2)
+    facing = [swap_core(edges(held)) for held, _, _ in books]
     scales = jnp.stack([angular, sign])
-    books[0], tops, tails = lax.optimization_barrier((books[0], tops, tails))
-    beside = jnp.concatenate([jnp.where(me == 0, 1.0, tops), jnp.where(me == strips - 1, 1.0, tails)])
-
     chosen = [piece for e in range(groups) for lot in full[e] for piece in lot]
     mine, give = enter_columns(ids, chosen, filt, tab, groups, across, rows, half)
     other = swap_core(give)
-    factors = prepare(ids, scales, books, facing, groups, across)
+    *factors, beside = prepare(ids, scales, books, facing, groups, across, rows)
     mine, give, near, far = middle(ids, mine, other, factors, tab, groups, across, rows, half)
 
     other = swap_core(give)
@@ -921,10 +976,8 @@
 
     arrived = []
     for e in range(groups):
-        kept, given = outs[2 * e], outs[2 * e + 1]
-        if e:
-            given, kept = swap_z(given, e), swap_z(kept, e)
-        arrived += [kept, swap_core(given)]
+        piece = swap_z(outs[e], e) if e else outs[e]
+        arrived += [piece, swap_core(piece)]
 
     facing = swap_z(far, 1)
     facing = after(facing, arrived[2])

time: 232 us -> 215 us (0.927)
  the two profiles are of different devices: /device:TPU:12 before, /device:TPU:0 now
where the time goes in v3:
time: 215 us
  waiting for transfers between devices  107 us (50%)
  Pallas kernels  49.7 us (23%)
  starting transfers between devices  43.1 us (20%)
  other arithmetic  10.4 us (5%)
  local copies, waits for them, and re-layouts  2.61 us (1%)
  between operations  2.57 us (1%)
    ppermute x38, waiting for transfers between devices, swap(): return lax.ppermute(value, 'strip', [(i, i ^ bit) for i in range(strips)])  103 us
    pallas_call x6, Pallas kernels, call(): pl.pallas_call(kernel, out_shape=out_shape, in_specs=in_specs, out_specs=...  49.7 us
    ppermute x38, starting transfers between devices, swap(): return lax.ppermute(value, 'strip', [(i, i ^ bit) for i in range(strips)])  38.5 us
    ppermute x3, starting transfers between devices, ahead_plane(): lax.ppermute(value, 'freq', [(i, (i + k) % planes) for i in range(planes)])  4.66 us
    mul x1, other arithmetic, column_filter(): imag = jnp.where(travel, ratio * radius, 0.0) * (sign * scale)  4.39 us
  transfers between devices with their start and end apart: 41, of which 15 were waited for; matrix products, arithmetic and copies ran while one was open for 5% of the time, Pallas kernels for 14%

profile of v3, /device:TPU:0, one launch (start us, length us, event | category | flops | bytes accessed | tf_op | source)
XLA Modules:
  0.0 215.2 jit_solution(15365208959502586350)
XLA Ops:
  0.7 0.6 pad_add_fusion.ids
  1.3 5.2 %first_transform.1 = (f32[1024,128]{1,0:T(8,128)}, f32[1024,128]{1,0:T(8,128)}, f32[1024,128]{1,0:T(8,128)}, f32[512,128]{1,0:T(8,128)}, f32[512,128]{1,0:T(8,128)}) custom-call(s32[4]{0:T(128)} %pad_add_fusion.ids, f32[2,2,64,1024]{3,2,1,0:T(8,128)} %source.1, f32[2,2,64,1024]{3,2,1,0:T(8,128)} %receiver.1, ...), custom_call_target="tpu_custom_call" | custom-call | flops 4000000000 | bytes 4000000 | tf_op jit(solution)/shard_map/first_transform/pallas_call | solution.py:157
  6.5 3.1 %collective-permute-start.4 = (f32[1024,128]{1,0:T(8,128)}, f32[1024,128]{1,0:T(8,128)S(1)}, u32[]{:S(2)}, u32[]{:S(2)}) collective-permute-start(f32[1024,128]{1,0:T(8,128)} %get-tuple-element.36), channel_id=1, source_target_pairs={{0,4},{1,5},{2,6},{3,7},{4,0},{5,1},{6,2},{7,3},{8,12},{9,13},{10,... | collective-permute-start | bytes 1572872 | tf_op jit(solution)/shard_map/ppermute | solution.py:885
  9.6 1.5 collective-permute-start.5
  11.1 2.6 %collective-permute-start.7 = (f32[1024,128]{1,0:T(8,128)}, f32[1024,128]{1,0:T(8,128)S(1)}, u32[]{:S(2)}, u32[]{:S(2)}) collective-permute-start(f32[1024,128]{1,0:T(8,128)} %get-tuple-element.41), channel_id=1, source_target_pairs={{0,8},{1,9},{2,10},{3,11},{4,12},{5,13},{6,14},{7,15},{8,0},{9,1},... | collective-permute-start | bytes 1572872 | tf_op jit(solution)/shard_map/ppermute | solution.py:885
  13.7 16.7 %collective-permute-done.4.refs_4_ = f32[1024,128]{1,0:T(8,128)S(1)} collective-permute-done((f32[1024,128]{1,0:T(8,128)}, f32[1024,128]{1,0:T(8,128)S(1)}, u32[]{:S(2)}, u32[]{:S(2)}) %collective-permute-start.4) | collective-permute-done | bytes 524320 | tf_op jit(solution)/shard_map/ppermute | solution.py:885
  30.4 2.7 %collective-permute-start.8 = (f32[1024,128]{1,0:T(8,128)S(1)}, f32[1024,128]{1,0:T(8,128)S(1)}, u32[]{:S(2)}, u32[]{:S(2)}) collective-permute-start(f32[1024,128]{1,0:T(8,128)S(1)} %collective-permute-done.4.refs_4_), channel_id=1, source_target_pairs={{0,2},{1,3},{2,0},{3,1},{4,6},{5,7},{6,4},{7,5},{8,10},{9,11},{10,... | collective-permute-start | bytes 1572872 | tf_op jit(solution)/shard_map/ppermute | solution.py:885
  33.2 0.1 fusion.12
  33.3 4.6 %collective-permute-done.7.refs_8_ = f32[1024,128]{1,0:T(8,128)S(1)} collective-permute-done((f32[1024,128]{1,0:T(8,128)}, f32[1024,128]{1,0:T(8,128)S(1)}, u32[]{:S(2)}, u32[]{:S(2)}) %collective-permute-start.7) | collective-permute-done | bytes 524320 | tf_op jit(solution)/shard_map/ppermute | solution.py:885
  37.8 0.5 collective-permute-start.20
  38.4 2.5 %collective-permute-start.6 = (f32[512,128]{1,0:T(8,128)}, f32[512,128]{1,0:T(8,128)S(1)}, u32[]{:S(2)}, u32[]{:S(2)}) collective-permute-start(f32[512,128]{1,0:T(8,128)} %get-tuple-element.39), channel_id=1, source_target_pairs={{0,12},{1,13},{2,14},{3,15},{4,8},{5,9},{6,10},{7,11},{8,4},{9,5},... | collective-permute-start | bytes 786440 | tf_op jit(solution)/shard_map/ppermute | solution.py:885
  40.8 5.1 %collective-permute-done.8.refs_6_ = f32[1024,128]{1,0:T(8,128)S(1)} collective-permute-done((f32[1024,128]{1,0:T(8,128)S(1)}, f32[1024,128]{1,0:T(8,128)S(1)}, u32[]{:S(2)}, u32[]{:S(2)}) %collective-permute-start.8) | collective-permute-done | bytes 524320 | tf_op jit(solution)/shard_map/ppermute | solution.py:885
  45.9 4.4 %select_multiply_fusion = (f32[4,8,128,128]{3,2,1,0:T(8,128)}, f32[4,8,128,128]{3,2,1,0:T(8,128)}) fusion(f32[]{:T(128)S(6)} %mul.153, f32[4,128]{1,0:T(4,128)S(1)} %fusion.12, f32[8,128]{1,0:T(8,128)S(1)} %fusion.9, f32[]{:T(128)S(6)} %mul.130), kind=kLoop, calls=%fused_computation | loop fusion | flops 13107200 | bytes 4200456 | tf_op jit(solution)/shard_map/mul | solution.py:864
  50.4 2.5 %collective-permute-start.9 = (f32[512,128]{1,0:T(8,128)S(1)}, f32[512,128]{1,0:T(8,128)S(1)}, u32[]{:S(2)}, u32[]{:S(2)}) collective-permute-start(f32[512,128]{1,0:T(8,128)S(1)} %copy-done.27), channel_id=1, source_target_pairs={{0,12},{1,13},{2,14},{3,15},{4,8},{5,9},{6,10},{7,11},{8,4},{9,5},... | collective-permute-start | bytes 786440 | tf_op jit(solution)/shard_map/ppermute | solution.py:885
  52.9 2.0 collective-permute-start.24
  54.9 1.6 collective-permute-start
  56.5 4.6 %collective-permute-done.9.refs_13_ = f32[512,128]{1,0:T(8,128)S(1)} collective-permute-done((f32[512,128]{1,0:T(8,128)S(1)}, f32[512,128]{1,0:T(8,128)S(1)}, u32[]{:S(2)}, u32[]{:S(2)}) %collective-permute-start.9) | collective-permute-done | bytes 262176 | tf_op jit(solution)/shard_map/ppermute | solution.py:885
  61.1 0.6 collective-permute-done.24.refs_16_
  61.6 1.7 collective-permute-start.25
  63.4 0.6 fusion.13
  65.4 0.1 pad.15.clone
  65.5 0.5 collective-permute-start.21
  66.0 0.1 fusion.2
  66.1 0.1 collective-permute-start.26
  66.2 0.4 collective-permute-start.23
  66.7 2.9 %collective-permute-done.25.refs_17_ = f32[512,128]{1,0:T(8,128)S(1)} collective-permute-done((f32[512,128]{1,0:T(8,128)S(1)}, f32[512,128]{1,0:T(8,128)S(1)}, u32[]{:S(2)}, u32[]{:S(2)}) %collective-permute-start.25) | collective-permute-done | bytes 262176 | tf_op jit(solution)/shard_map/ppermute | solution.py:885
  69.7 0.1 maximum_bitcast_fusion
  69.8 4.2 %collective-permute-start.1 = (f32[1,8,72,128]{3,2,1,0:T(8,128)S(1)}, f32[1,8,72,128]{3,2,1,0:T(8,128)S(1)}, u32[]{:S(2)}, u32[]{:S(2)}) collective-permute-start(f32[1,8,72,128]{3,2,1,0:T(8,128)S(1)} %maximum_bitcast_fusion), channel_id=1, source_target_pairs={{0,8},{1,9},{2,10},{3,11},{4,12},{5,13},{6,14},{7,15},{8,0},{9,1},... | collective-permute-start | bytes 884744 | tf_op jit(solution)/shard_map/ppermute | solution.py:885
  74.2 0.7 copy-done.22
  74.9 0.1 copy-done.30
  75.0 0.7 copy-done.31
  75.7 11.6 %enter_columns.1 = (f32[8,528,128]{2,1,0:T(8,128)}, f32[8,528,128]{2,1,0:T(8,128)}) custom-call(s32[4]{0:T(128)} %pad_add_fusion.ids, f32[4,8,128,128]{3,2,1,0:T(8,128)} %get-tuple-element.72.filt_re, f32[4,8,128,128]{3,2,1,0:T(8,128)} %get-tuple-element.71.filt_im, bf16[512,256]{1,0:T(8,128)(2,1)} %constant.187.clone.ahead, ...), custom_call_target="tpu_custom_call" | custom-call | flops 8000000000 | bytes 8000000 | tf_op jit(solution)/shard_map/enter_columns/pallas_call | solution.py:157
  87.3 0.3 collective-permute-start.28
  87.6 0.4 collective-permute-done.1
  88.2 1.8 collective-permute-start.3
  90.0 13.3 %collective-permute-done.2.refs_1_ = f32[2,8,72,128]{3,2,1,0:T(8,128)S(1)} collective-permute-done((f32[2,8,72,128]{3,2,1,0:T(8,128)S(1)}, f32[2,8,72,128]{3,2,1,0:T(8,128)S(1)}, u32[]{:S(2)}, u32[]{:S(2)}) %collective-permute-start.2) | collective-permute-done | bytes 589856 | tf_op jit(solution)/shard_map/ppermute | solution.py:885
  103.3 1.7 collective-permute-start.10
  105.1 0.7 pad_maximum_fusion.3
  105.8 0.7 pad_maximum_fusion.4
  106.5 0.5 collective-permute-start.12
  107.0 0.7 pad_maximum_fusion.5
  107.7 9.9 %collective-permute-done.10.refs_3_ = f32[2,8,72,128]{3,2,1,0:T(8,128)S(1)} collective-permute-done((f32[2,8,72,128]{3,2,1,0:T(8,128)S(1)}, f32[2,8,72,128]{3,2,1,0:T(8,128)S(1)}, u32[]{:S(2)}, u32[]{:S(2)}) %collective-permute-start.10) | collective-permute-done | bytes 589856 | tf_op jit(solution)/shard_map/ppermute | solution.py:885
  117.7 0.7 pad_maximum_fusion.6
  118.5 1.5 collective-permute-done.14.refs_7_
  120.0 3.8 %prepare.1 = (f32[8,8,64,128]{3,2,1,0:T(8,128)S(1)}, f32[8,8,64,128]{3,2,1,0:T(8,128)S(1)}, f32[8,8,64,128]{3,2,1,0:T(8,128)S(1)}, f32[8,16,128]{2,1,0:T(8,128)S...) custom-call(s32[4]{0:T(128)S(1)} %copy-done.2, f32[2]{0:T(128)S(1)} %pad_maximum_fusion.7.scales, ...), custom_call_target="tpu_custom_call" | custom-call | flops 4000000000 | bytes 8000000 | tf_op jit(solution)/shard_map/prepare/pallas_call | solution.py:157
  123.9 13.9 %middle.1 = (f32[8,512,128]{2,1,0:T(8,128)S(1)}, f32[8,512,128]{2,1,0:T(8,128)S(1)}, f32[2,2,64,1024]{3,2,1,0:T(8,128)S(1)}, f32[2,2,64,1024]{3,2,1,0:T(8,128)S(1)}) custom-call(s32[4]{0:T(128)S(1)} %copy-done.2, bf16[2,256,256]{2,1,0:T(8,128)(2,1)S(1)} %copy-done.4, bf16[2,256,256]{2,1,0:T(8,128)(2,1)S(1)} %copy-done.8, f32[2,8,1,128]{3,2,1,0:T(1,128)S(1)} %copy-done.9, ...), custom_call_target="tpu_custom_call" | custom-call | flops 16000000000 | bytes 10000000 | tf_op jit(solution)/shard_map/middle/pallas_call | solution.py:157
  137.9 0.2 collective-permute-start.30
  138.1 0.6 collective-permute-start.29
  138.7 3.4 %collective-permute-done.30.other = f32[8,512,128]{2,1,0:T(8,128)S(1)} collective-permute-done((f32[8,512,128]{2,1,0:T(8,128)S(1)}, f32[8,512,128]{2,1,0:T(8,128)S(1)}, u32[]{:S(2)}, u32[]{:S(2)}) %collective-permute-start.30) | collective-permute-done | bytes 2097184 | tf_op jit(solution)/shard_map/ppermute | solution.py:885
  142.1 8.7 %leave_columns.1 = (f32[2,528,128]{2,1,0:T(8,128)S(1)}, f32[2,528,128]{2,1,0:T(8,128)}, f32[2,528,128]{2,1,0:T(8,128)}, f32[2,528,128]{2,1,0:T(8,128)}) custom-call(s32[4]{0:T(128)S(1)} %copy-done.2, f32[4,8,128,128]{3,2,1,0:T(8,128)S(1)} %copy-done.1, f32[4,8,128,128]{3,2,1,0:T(8,128)S(1)} %copy-done, bf16[512,256]{1,0:T(8,128)(2,1)S(1)} %copy-done.6, ...), custom_call_target="tpu_custom_call" | custom-call | flops 8000000000 | bytes 8000000 | tf_op jit(solution)/shard_map/leave_columns/pallas_call | solution.py:157
  150.8 0.7 collective-permute-start.31
  151.5 0.2 collective-permute-start.36
  151.7 3.6 %collective-permute-start.38 = (f32[2,528,128]{2,1,0:T(8,128)}, f32[2,528,128]{2,1,0:T(8,128)}, u32[]{:S(2)}, u32[]{:S(2)}) collective-permute-start(f32[2,528,128]{2,1,0:T(8,128)} %get-tuple-element.63), channel_id=1, source_target_pairs={{0,12},{1,13},{2,14},{3,15},{4,8},{5,9},{6,10},{7,11},{8,4},{9,5},... | collective-permute-start | bytes 1622024 | tf_op jit(solution)/shard_map/ppermute | solution.py:885
  155.3 20.5 %collective-permute-done.29 = f32[2,2,64,1024]{3,2,1,0:T(8,128)} collective-permute-done((f32[2,2,64,1024]{3,2,1,0:T(8,128)S(1)}, f32[2,2,64,1024]{3,2,1,0:T(8,128)}, u32[]{:S(2)}, u32[]{:S(2)}) %collective-permute-start.29) | collective-permute-done | bytes 1048608 | tf_op jit(solution)/shard_map/ppermute | solution.py:885
  175.8 11.4 %collective-permute-done.31.refs_2_ = f32[2,528,128]{2,1,0:T(8,128)} collective-permute-done((f32[2,528,128]{2,1,0:T(8,128)}, f32[2,528,128]{2,1,0:T(8,128)}, u32[]{:S(2)}, u32[]{:S(2)}) %collective-permute-start.31) | collective-permute-done | bytes 540704 | tf_op jit(solution)/shard_map/ppermute | solution.py:885
  187.2 1.4 multiply_add_fusion
  188.6 1.6 collective-permute-start.32
  190.2 0.5 collective-permute-start.35
  190.7 7.8 %collective-permute-done.38.refs_6_ = f32[2,528,128]{2,1,0:T(8,128)} collective-permute-done((f32[2,528,128]{2,1,0:T(8,128)}, f32[2,528,128]{2,1,0:T(8,128)}, u32[]{:S(2)}, u32[]{:S(2)}) %collective-permute-start.38) | collective-permute-done | bytes 540704 | tf_op jit(solution)/shard_map/ppermute | solution.py:885
  198.6 3.7 %collective-permute-start.33 = (f32[64,512]{1,0:T(8,128)S(1)}, f32[64,512]{1,0:T(8,128)S(1)}, u32[]{:S(2)}, u32[]{:S(2)}) collective-permute-start(f32[64,512]{1,0:T(8,128)S(1)} %dynamic-slice_bitcast_fusion.1), channel_id=1, source_target_pairs={{0,8},{1,9},{2,10},{3,11},{4,12},{5,13},{6,14},{7,15},{8,0},{9,1},... | collective-permute-start | bytes 393224 | tf_op jit(solution)/shard_map/ppermute | solution.py:885
  202.3 6.4 %last.1 = (f32[2,2,64,1024]{3,2,1,0:T(8,128)}, f32[2,2,64,1024]{3,2,1,0:T(8,128)}, f32[64,1024]{1,0:T(8,128)S(1)}) custom-call(s32[4]{0:T(128)S(1)} %copy-done.2, f32[2]{0:T(128)S(1)} %convert_multiply_fusion.angulars, bf16[2,256,256]{2,1,0:T(8,128)(2,1)S(1)} %copy-done.5, f32[2,8,1,128]{3,2,1,0:T(1,128)S(1)} %copy-done.9, f32[64,1024]{1,0:T(8,128)S(1)} %bitcast.38, ...), custom_call_target="tpu_custom_call" | custom-call | flops 8000000000 | bytes 8000000 | tf_op jit(solution)/shard_map/last/pallas_call | solution.py:157
  208.8 1.5 collective-permute-start.40
  210.4 4.1 %collective-permute-done.40 = f32[64,512]{1,0:T(8,128)S(1)} collective-permute-done((f32[64,512]{1,0:T(8,128)S(1)}, f32[64,512]{1,0:T(8,128)S(1)}, u32[]{:S(2)}, u32[]{:S(2)}) %collective-permute-start.40) | collective-permute-done | bytes 131104 | tf_op jit(solution)/shard_map/ppermute | solution.py:897
  214.5 0.7 pad_maximum_fusion.2
  (125 shorter events, 0.9 us)
Async XLA Ops:
  6.5 23.9 %collective-permute-start.4 = (f32[1024,128]{1,0:T(8,128)}, f32[1024,128]{1,0:T(8,128)S(1)}, u32[]{:S(2)}, u32[]{:S(2)}) collective-permute-start(f32[1024,128]{1,0:T(8,128)} %get-tuple-element.36), channel_id=1, source_target_pairs={{0,4},{1,5},{2,6},{3,7},{4,0},{5,1},{6,2},{7,3},{8,12},{9,13},{10,... | collective-permute-start | bytes 1572872 | tf_op jit(solution)/shard_map/ppermute | solution.py:885
  9.6 23.5 %collective-permute-start.5 = (f32[1024,128]{1,0:T(8,128)}, f32[1024,128]{1,0:T(8,128)S(1)}, u32[]{:S(2)}, u32[]{:S(2)}) collective-permute-start(f32[1024,128]{1,0:T(8,128)} %get-tuple-element.38.refs_0_), channel_id=1, source_target_pairs={{0,2},{1,3},{2,0},{3,1},{4,6},{5,7},{6,4},{7,5},{8,10},{9,11},{10,... | collective-permute-start | bytes 1572872 | tf_op jit(solution)/shard_map/ppermute | solution.py:885
  11.1 29.7 %collective-permute-start.15 = (f32[1024,128]{1,0:T(8,128)}, f32[1024,128]{1,0:T(8,128)S(1)}, u32[]{:S(2)}, u32[]{:S(2)}) collective-permute-start(f32[1024,128]{1,0:T(8,128)} %get-tuple-element.38.refs_0_), channel_id=1, source_target_pairs={{0,1},{1,0},{2,3},{3,2},{4,5},{5,4},{6,7},{7,6},{8,9},{9,8},{10,11... | collective-permute-start | bytes 1572872 | tf_op jit(solution)/shard_map/ppermute | solution.py:885
  11.1 26.7 %collective-permute-start.7 = (f32[1024,128]{1,0:T(8,128)}, f32[1024,128]{1,0:T(8,128)S(1)}, u32[]{:S(2)}, u32[]{:S(2)}) collective-permute-start(f32[1024,128]{1,0:T(8,128)} %get-tuple-element.41), channel_id=1, source_target_pairs={{0,8},{1,9},{2,10},{3,11},{4,12},{5,13},{6,14},{7,15},{8,0},{9,1},... | collective-permute-start | bytes 1572872 | tf_op jit(solution)/shard_map/ppermute | solution.py:885
  30.4 19.9 %copy-start.13 = (f32[1024,128]{1,0:T(8,128)}, f32[1024,128]{1,0:T(8,128)S(1)}, u32[]{:S(2)}) copy-start(f32[1024,128]{1,0:T(8,128)S(1)} %collective-permute-done.4.refs_4_) | copy-start | bytes 1572868
  30.4 15.5 %collective-permute-start.8 = (f32[1024,128]{1,0:T(8,128)S(1)}, f32[1024,128]{1,0:T(8,128)S(1)}, u32[]{:S(2)}, u32[]{:S(2)}) collective-permute-start(f32[1024,128]{1,0:T(8,128)S(1)} %collective-permute-done.4.refs_4_), channel_id=1, source_target_pairs={{0,2},{1,3},{2,0},{3,1},{4,6},{5,7},{6,4},{7,5},{8,10},{9,11},{10,... | collective-permute-start | bytes 1572872 | tf_op jit(solution)/shard_map/ppermute | solution.py:885
  33.1 17.2 %copy-start.14 = (f32[1024,128]{1,0:T(8,128)}, f32[1024,128]{1,0:T(8,128)S(1)}, u32[]{:S(2)}) copy-start(f32[1024,128]{1,0:T(8,128)S(1)} %collective-permute-done.5.refs_2_) | copy-start | bytes 1572868
  33.1 19.8 %collective-permute-start.16 = (f32[1024,128]{1,0:T(8,128)S(1)}, f32[1024,128]{1,0:T(8,128)}, u32[]{:S(2)}, u32[]{:S(2)}) collective-permute-start(f32[1024,128]{1,0:T(8,128)S(1)} %collective-permute-done.5.refs_2_), channel_id=1, source_target_pairs={{0,1},{1,0},{2,3},{3,2},{4,5},{5,4},{6,7},{7,6},{8,9},{9,8},{10,11... | collective-permute-start | bytes 1572872 | tf_op jit(solution)/shard_map/ppermute | solution.py:885
  37.8 27.6 %copy-start.16 = (f32[1024,128]{1,0:T(8,128)}, f32[1024,128]{1,0:T(8,128)S(1)}, u32[]{:S(2)}) copy-start(f32[1024,128]{1,0:T(8,128)S(1)} %collective-permute-done.7.refs_8_) | copy-start | bytes 1572868
  37.8 18.6 %collective-permute-start.20 = (f32[1024,128]{1,0:T(8,128)S(1)}, f32[1024,128]{1,0:T(8,128)S(1)}, u32[]{:S(2)}, u32[]{:S(2)}) collective-permute-start(f32[1024,128]{1,0:T(8,128)S(1)} %collective-permute-done.7.refs_8_), channel_id=1, source_target_pairs={{0,2},{1,3},{2,0},{3,1},{4,6},{5,7},{6,4},{7,5},{8,10},{9,11},{10,... | collective-permute-start | bytes 1572872 | tf_op jit(solution)/shard_map/ppermute | solution.py:885
  38.3 12.0 %copy-start.27 = (f32[512,128]{1,0:T(8,128)S(1)}, f32[512,128]{1,0:T(8,128)}, u32[]{:S(2)}) copy-start(f32[512,128]{1,0:T(8,128)} %get-tuple-element.42) | copy-start | bytes 786436
  38.4 16.6 %copy-start.11 = (f32[1,64,1024]{2,1,0:T(8,128)S(1)}, f32[1,64,1024]{2,1,0:T(8,128)}, u32[]{:S(2)}) copy-start(f32[1,64,1024]{2,1,0:T(8,128)} %param.12) | copy-start | bytes 786436
  38.4 25.0 %copy-start.12 = (s32[2]{0:T(128)S(1)}, s32[2]{0:T(128)}, u32[]{:S(2)}) copy-start(s32[2]{0:T(128)} %param.13) | copy-start | bytes 28
  38.4 12.0 %collective-permute-start.6 = (f32[512,128]{1,0:T(8,128)}, f32[512,128]{1,0:T(8,128)S(1)}, u32[]{:S(2)}, u32[]{:S(2)}) collective-permute-start(f32[512,128]{1,0:T(8,128)} %get-tuple-element.39), channel_id=1, source_target_pairs={{0,12},{1,13},{2,14},{3,15},{4,8},{5,9},{6,10},{7,11},{8,4},{9,5},... | collective-permute-start | bytes 786440 | tf_op jit(solution)/shard_map/ppermute | solution.py:885
  40.8 9.5 %copy-start.15 = (f32[1024,128]{1,0:T(8,128)}, f32[1024,128]{1,0:T(8,128)S(1)}, u32[]{:S(2)}) copy-start(f32[1024,128]{1,0:T(8,128)S(1)} %collective-permute-done.15.refs_1_) | copy-start | bytes 1572868
  40.8 14.1 %collective-permute-start.17 = (f32[1024,128]{1,0:T(8,128)S(1)}, f32[1024,128]{1,0:T(8,128)S(1)}, u32[]{:S(2)}, u32[]{:S(2)}) collective-permute-start(f32[1024,128]{1,0:T(8,128)S(1)} %collective-permute-done.4.refs_4_), channel_id=1, source_target_pairs={{0,1},{1,0},{2,3},{3,2},{4,5},{5,4},{6,7},{7,6},{8,9},{9,8},{10,11... | collective-permute-start | bytes 1572872 | tf_op jit(solution)/shard_map/ppermute | solution.py:885
  45.9 15.1 %collective-permute-start.18 = (f32[1024,128]{1,0:T(8,128)S(1)}, f32[1024,128]{1,0:T(8,128)S(1)}, u32[]{:S(2)}, u32[]{:S(2)}) collective-permute-start(f32[1024,128]{1,0:T(8,128)S(1)} %collective-permute-done.8.refs_6_), channel_id=1, source_target_pairs={{0,1},{1,0},{2,3},{3,2},{4,5},{5,4},{6,7},{7,6},{8,9},{9,8},{10,11... | collective-permute-start | bytes 1572872 | tf_op jit(solution)/shard_map/ppermute | solution.py:885
  50.3 23.8 %copy-start.23 = (f32[512,128]{1,0:T(8,128)}, f32[512,128]{1,0:T(8,128)S(1)}, u32[]{:S(2)}) copy-start(f32[512,128]{1,0:T(8,128)S(1)} %collective-permute-done.6.refs_12_) | copy-start | bytes 786436
  50.4 10.7 %collective-permute-start.9 = (f32[512,128]{1,0:T(8,128)S(1)}, f32[512,128]{1,0:T(8,128)S(1)}, u32[]{:S(2)}, u32[]{:S(2)}) collective-permute-start(f32[512,128]{1,0:T(8,128)S(1)} %copy-done.27), channel_id=1, source_target_pairs={{0,12},{1,13},{2,14},{3,15},{4,8},{5,9},{6,10},{7,11},{8,4},{9,5},... | collective-permute-start | bytes 786440 | tf_op jit(solution)/shard_map/ppermute | solution.py:885
  52.9 8.7 %collective-permute-start.24 = (f32[512,128]{1,0:T(8,128)S(1)}, f32[512,128]{1,0:T(8,128)S(1)}, u32[]{:S(2)}, u32[]{:S(2)}) collective-permute-start(f32[512,128]{1,0:T(8,128)S(1)} %collective-permute-done.6.refs_12_), channel_id=1, source_target_pairs={{0,2},{1,3},{2,0},{3,1},{4,6},{5,7},{6,4},{7,5},{8,10},{9,11},{10,... | collective-permute-start | bytes 786440 | tf_op jit(solution)/shard_map/ppermute | solution.py:885
  54.9 9.1 %copy-start.19 = (f32[1024,128]{1,0:T(8,128)}, f32[1024,128]{1,0:T(8,128)S(1)}, u32[]{:S(2)}) copy-start(f32[1024,128]{1,0:T(8,128)S(1)} %collective-permute-done.17.refs_5_) | copy-start | bytes 1572868
  54.9 11.0 %collective-permute-start = (f32[1,64,1024]{2,1,0:T(8,128)S(1)}, f32[1,64,1024]{2,1,0:T(8,128)S(1)}, u32[]{:S(2)}, u32[]{:S(2)}) collective-permute-start(f32[1,64,1024]{2,1,0:T(8,128)S(1)} %copy-done.11), channel_id=1, source_target_pairs={{0,16},{16,0},{1,17},{17,1},{2,18},{18,2},{3,19},{19,3},{4,20},{20... | collective-permute-start | bytes 786440 | tf_op jit(solution)/shard_map/ppermute | solution.py:897
  56.5 7.5 %copy-start.18 = (f32[1024,128]{1,0:T(8,128)}, f32[1024,128]{1,0:T(8,128)S(1)}, u32[]{:S(2)}) copy-start(f32[1024,128]{1,0:T(8,128)S(1)} %collective-permute-done.20.refs_10_) | copy-start | bytes 1572868
  56.5 9.7 %collective-permute-start.22 = (f32[512,128]{1,0:T(8,128)S(1)}, f32[512,128]{1,0:T(8,128)S(1)}, u32[]{:S(2)}, u32[]{:S(2)}) collective-permute-start(f32[512,128]{1,0:T(8,128)S(1)} %collective-permute-done.6.refs_12_), channel_id=1, source_target_pairs={{0,1},{1,0},{2,3},{3,2},{4,5},{5,4},{6,7},{7,6},{8,9},{9,8},{10,11... | collective-permute-start | bytes 786440 | tf_op jit(solution)/shard_map/ppermute | solution.py:885
  61.1 13.1 %copy-start.24 = (f32[512,128]{1,0:T(8,128)}, f32[512,128]{1,0:T(8,128)S(1)}, u32[]{:S(2)}) copy-start(f32[512,128]{1,0:T(8,128)S(1)} %collective-permute-done.9.refs_13_) | copy-start | bytes 786436
  61.6 12.5 %copy-start.25 = (f32[512,128]{1,0:T(8,128)}, f32[512,128]{1,0:T(8,128)S(1)}, u32[]{:S(2)}) copy-start(f32[512,128]{1,0:T(8,128)S(1)} %collective-permute-done.24.refs_16_) | copy-start | bytes 786436
  61.6 7.9 %collective-permute-start.25 = (f32[512,128]{1,0:T(8,128)S(1)}, f32[512,128]{1,0:T(8,128)S(1)}, u32[]{:S(2)}, u32[]{:S(2)}) collective-permute-start(f32[512,128]{1,0:T(8,128)S(1)} %collective-permute-done.9.refs_13_), channel_id=1, source_target_pairs={{0,2},{1,3},{2,0},{3,1},{4,6},{5,7},{6,4},{7,5},{8,10},{9,11},{10,... | collective-permute-start | bytes 786440 | tf_op jit(solution)/shard_map/ppermute | solution.py:885
  65.4 4.3 %collective-permute-start.19 = (f32[1024,128]{1,0:T(8,128)S(1)}, f32[1024,128]{1,0:T(8,128)S(1)}, u32[]{:S(2)}, u32[]{:S(2)}) collective-permute-start(f32[1024,128]{1,0:T(8,128)S(1)} %collective-permute-done.7.refs_8_), channel_id=1, source_target_pairs={{0,1},{1,0},{2,3},{3,2},{4,5},{5,4},{6,7},{7,6},{8,9},{9,8},{10,11... | collective-permute-start | bytes 1572872 | tf_op jit(solution)/shard_map/ppermute | solution.py:885
  65.5 8.6 %collective-permute-start.21 = (f32[1024,128]{1,0:T(8,128)}, f32[1024,128]{1,0:T(8,128)S(1)}, u32[]{:S(2)}, u32[]{:S(2)}) collective-permute-start(f32[1024,128]{1,0:T(8,128)} %copy-done.18), channel_id=1, source_target_pairs={{0,1},{1,0},{2,3},{3,2},{4,5},{5,4},{6,7},{7,6},{8,9},{9,8},{10,11... | collective-permute-start | bytes 1572872 | tf_op jit(solution)/shard_map/ppermute | solution.py:885
  66.1 8.0 %collective-permute-start.26 = (f32[512,128]{1,0:T(8,128)S(1)}, f32[512,128]{1,0:T(8,128)S(1)}, u32[]{:S(2)}, u32[]{:S(2)}) collective-permute-start(f32[512,128]{1,0:T(8,128)S(1)} %collective-permute-done.24.refs_16_), channel_id=1, source_target_pairs={{0,1},{1,0},{2,3},{3,2},{4,5},{5,4},{6,7},{7,6},{8,9},{9,8},{10,11... | collective-permute-start | bytes 786440 | tf_op jit(solution)/shard_map/ppermute | solution.py:885
  66.2 7.9 %copy-start.26 = (f32[512,128]{1,0:T(8,128)}, f32[512,128]{1,0:T(8,128)S(1)}, u32[]{:S(2)}) copy-start(f32[512,128]{1,0:T(8,128)S(1)} %collective-permute-done.22.refs_14_) | copy-start | bytes 786436
  66.2 7.8 %collective-permute-start.23 = (f32[512,128]{1,0:T(8,128)S(1)}, f32[512,128]{1,0:T(8,128)S(1)}, u32[]{:S(2)}, u32[]{:S(2)}) collective-permute-start(f32[512,128]{1,0:T(8,128)S(1)} %collective-permute-done.9.refs_13_), channel_id=1, source_target_pairs={{0,1},{1,0},{2,3},{3,2},{4,5},{5,4},{6,7},{7,6},{8,9},{9,8},{10,11... | collective-permute-start | bytes 786440 | tf_op jit(solution)/shard_map/ppermute | solution.py:885
  69.6 4.5 %collective-permute-start.27 = (f32[512,128]{1,0:T(8,128)S(1)}, f32[512,128]{1,0:T(8,128)S(1)}, u32[]{:S(2)}, u32[]{:S(2)}) collective-permute-start(f32[512,128]{1,0:T(8,128)S(1)} %collective-permute-done.25.refs_17_), channel_id=1, source_target_pairs={{0,1},{1,0},{2,3},{3,2},{4,5},{5,4},{6,7},{7,6},{8,9},{9,8},{10,11... | collective-permute-start | bytes 786440 | tf_op jit(solution)/shard_map/ppermute | solution.py:885
  69.8 18.2 %collective-permute-start.1 = (f32[1,8,72,128]{3,2,1,0:T(8,128)S(1)}, f32[1,8,72,128]{3,2,1,0:T(8,128)S(1)}, u32[]{:S(2)}, u32[]{:S(2)}) collective-permute-start(f32[1,8,72,128]{3,2,1,0:T(8,128)S(1)} %maximum_bitcast_fusion), channel_id=1, source_target_pairs={{0,8},{1,9},{2,10},{3,11},{4,12},{5,13},{6,14},{7,15},{8,0},{9,1},... | collective-permute-start | bytes 884744 | tf_op jit(solution)/shard_map/ppermute | solution.py:885
  87.3 36.5 %collective-permute-start.28 = (f32[8,528,128]{2,1,0:T(8,128)}, f32[8,528,128]{2,1,0:T(8,128)}, u32[]{:S(2)}, u32[]{:S(2)}) collective-permute-start(f32[8,528,128]{2,1,0:T(8,128)} %get-tuple-element.53), channel_id=1, source_target_pairs={{0,1},{1,0},{2,3},{3,2},{4,5},{5,4},{6,7},{7,6},{8,9},{9,8},{10,11... | collective-permute-start | bytes 6488072 | tf_op jit(solution)/shard_map/ppermute | solution.py:885
  88.1 31.9 %copy-start.2 = (s32[4]{0:T(128)S(1)}, s32[4]{0:T(128)}, u32[]{:S(2)}) copy-start(s32[4]{0:T(128)} %pad_add_fusion.ids) | copy-start | bytes 52
  88.1 15.2 %collective-permute-start.2 = (f32[2,8,72,128]{3,2,1,0:T(8,128)S(1)}, f32[2,8,72,128]{3,2,1,0:T(8,128)S(1)}, u32[]{:S(2)}, u32[]{:S(2)}) collective-permute-start(f32[2,8,72,128]{3,2,1,0:T(8,128)S(1)} %pad_maximum_fusion.refs_0_), channel_id=1, source_target_pairs={{0,4},{1,5},{2,6},{3,7},{4,0},{5,1},{6,2},{7,3},{8,12},{9,13},{10,... | collective-permute-start | bytes 1769480 | tf_op jit(solution)/shard_map/ppermute | solution.py:885
  88.2 18.8 %collective-permute-start.3 = (f32[2,8,72,128]{3,2,1,0:T(8,128)S(1)}, f32[2,8,72,128]{3,2,1,0:T(8,128)S(1)}, u32[]{:S(2)}, u32[]{:S(2)}) collective-permute-start(f32[2,8,72,128]{3,2,1,0:T(8,128)S(1)} %pad_maximum_fusion.refs_0_), channel_id=1, source_target_pairs={{0,2},{1,3},{2,0},{3,1},{4,6},{5,7},{6,4},{7,5},{8,10},{9,11},{10,... | collective-permute-start | bytes 1769480 | tf_op jit(solution)/shard_map/ppermute | solution.py:885
  103.3 14.3 %collective-permute-start.10 = (f32[2,8,72,128]{3,2,1,0:T(8,128)S(1)}, f32[2,8,72,128]{3,2,1,0:T(8,128)S(1)}, u32[]{:S(2)}, u32[]{:S(2)}) collective-permute-start(f32[2,8,72,128]{3,2,1,0:T(8,128)S(1)} %collective-permute-done.2.refs_1_), channel_id=1, source_target_pairs={{0,2},{1,3},{2,0},{3,1},{4,6},{5,7},{6,4},{7,5},{8,10},{9,11},{10,... | collective-permute-start | bytes 1769480 | tf_op jit(solution)/shard_map/ppermute | solution.py:885
  105.8 12.7 %collective-permute-start.11 = (f32[2,8,24,128]{3,2,1,0:T(8,128)}, f32[2,8,24,128]{3,2,1,0:T(8,128)S(1)}, u32[]{:S(2)}, u32[]{:S(2)}) collective-permute-start(f32[2,8,24,128]{3,2,1,0:T(8,128)} %pad_maximum_fusion.3), channel_id=1, source_target_pairs={{0,1},{1,0},{2,3},{3,2},{4,5},{5,4},{6,7},{7,6},{8,9},{9,8},{10,11... | collective-permute-start | bytes 589832 | tf_op jit(solution)/shard_map/ppermute | solution.py:885
  106.5 12.0 %collective-permute-start.12 = (f32[2,8,24,128]{3,2,1,0:T(8,128)}, f32[2,8,24,128]{3,2,1,0:T(8,128)S(1)}, u32[]{:S(2)}, u32[]{:S(2)}) collective-permute-start(f32[2,8,24,128]{3,2,1,0:T(8,128)} %pad_maximum_fusion.4), channel_id=1, source_target_pairs={{0,1},{1,0},{2,3},{3,2},{4,5},{5,4},{6,7},{7,6},{8,9},{9,8},{10,11... | collective-permute-start | bytes 589832 | tf_op jit(solution)/shard_map/ppermute | solution.py:885
  107.7 10.8 %collective-permute-start.13 = (f32[2,8,24,128]{3,2,1,0:T(8,128)}, f32[2,8,24,128]{3,2,1,0:T(8,128)S(1)}, u32[]{:S(2)}, u32[]{:S(2)}) collective-permute-start(f32[2,8,24,128]{3,2,1,0:T(8,128)} %pad_maximum_fusion.5), channel_id=1, source_target_pairs={{0,1},{1,0},{2,3},{3,2},{4,5},{5,4},{6,7},{7,6},{8,9},{9,8},{10,11... | collective-permute-start | bytes 589832 | tf_op jit(solution)/shard_map/ppermute | solution.py:885
  118.4 1.7 collective-permute-start.14
  118.4 5.4 %copy-start.8 = (bf16[2,256,256]{2,1,0:T(8,128)(2,1)S(1)}, bf16[2,256,256]{2,1,0:T(8,128)(2,1)}, u32[]{:S(2)}) copy-start(bf16[2,256,256]{2,1,0:T(8,128)(2,1)} %constant.185.clone.table.ahead) | copy-start | bytes 786436
  118.4 5.4 %copy-start.9 = (f32[2,8,1,128]{3,2,1,0:T(1,128)S(1)}, f32[2,8,1,128]{3,2,1,0:T(1,128)}, u32[]{:S(2)}) copy-start(f32[2,8,1,128]{3,2,1,0:T(1,128)} %constant.189.clone.twist) | copy-start | bytes 24580
  118.5 5.4 %copy-start.10 = (f32[8,528,128]{2,1,0:T(8,128)S(1)}, f32[8,528,128]{2,1,0:T(8,128)}, u32[]{:S(2)}) copy-start(f32[8,528,128]{2,1,0:T(8,128)} %get-tuple-element.52.mine) | copy-start | bytes 6488068
  123.9 18.2 %copy-start = (f32[4,8,128,128]{3,2,1,0:T(8,128)S(1)}, f32[4,8,128,128]{3,2,1,0:T(8,128)}, u32[]{:S(2)}) copy-start(f32[4,8,128,128]{3,2,1,0:T(8,128)} %get-tuple-element.71.filt_im) | copy-start | bytes 6291460
  123.9 18.2 %copy-start.1 = (f32[4,8,128,128]{3,2,1,0:T(8,128)S(1)}, f32[4,8,128,128]{3,2,1,0:T(8,128)}, u32[]{:S(2)}) copy-start(f32[4,8,128,128]{3,2,1,0:T(8,128)} %get-tuple-element.72.filt_re) | copy-start | bytes 6291460
  123.9 18.2 %copy-start.3 = (f32[2,8,128,128]{3,2,1,0:T(8,128)S(1)}, f32[2,8,128,128]{3,2,1,0:T(8,128)}, u32[]{:S(2)}) copy-start(f32[2,8,128,128]{3,2,1,0:T(8,128)} %constant.190.clone.twist) | copy-start | bytes 3145732
  123.9 18.2 %copy-start.6 = (bf16[512,256]{1,0:T(8,128)(2,1)S(1)}, bf16[512,256]{1,0:T(8,128)(2,1)}, u32[]{:S(2)}) copy-start(bf16[512,256]{1,0:T(8,128)(2,1)} %constant.187.clone.ahead) | copy-start | bytes 786436
  123.9 18.2 %copy-start.7 = (bf16[512,256]{1,0:T(8,128)(2,1)S(1)}, bf16[512,256]{1,0:T(8,128)(2,1)}, u32[]{:S(2)}) copy-start(bf16[512,256]{1,0:T(8,128)(2,1)} %constant.188.clone.back) | copy-start | bytes 786436
  137.9 4.2 %collective-permute-start.30 = (f32[8,512,128]{2,1,0:T(8,128)S(1)}, f32[8,512,128]{2,1,0:T(8,128)S(1)}, u32[]{:S(2)}, u32[]{:S(2)}) collective-permute-start(f32[8,512,128]{2,1,0:T(8,128)S(1)} %get-tuple-element.57), channel_id=1, source_target_pairs={{0,1},{1,0},{2,3},{3,2},{4,5},{5,4},{6,7},{7,6},{8,9},{9,8},{10,11... | collective-permute-start | bytes 6291464 | tf_op jit(solution)/shard_map/ppermute | solution.py:885
  138.1 37.7 %collective-permute-start.29 = (f32[2,2,64,1024]{3,2,1,0:T(8,128)S(1)}, f32[2,2,64,1024]{3,2,1,0:T(8,128)}, u32[]{:S(2)}, u32[]{:S(2)}) collective-permute-start(f32[2,2,64,1024]{3,2,1,0:T(8,128)S(1)} %get-tuple-element.55), channel_id=1, source_target_pairs={{0,4},{1,5},{2,6},{3,7},{4,0},{5,1},{6,2},{7,3},{8,12},{9,13},{10,... | collective-permute-start | bytes 3145736 | tf_op jit(solution)/shard_map/ppermute | solution.py:885
  150.8 36.4 %collective-permute-start.31 = (f32[2,528,128]{2,1,0:T(8,128)}, f32[2,528,128]{2,1,0:T(8,128)}, u32[]{:S(2)}, u32[]{:S(2)}) collective-permute-start(f32[2,528,128]{2,1,0:T(8,128)} %get-tuple-element.58), channel_id=1, source_target_pairs={{0,4},{1,5},{2,6},{3,7},{4,0},{5,1},{6,2},{7,3},{8,12},{9,13},{10,... | collective-permute-start | bytes 1622024 | tf_op jit(solution)/shard_map/ppermute | solution.py:885
  151.5 39.2 %collective-permute-start.36 = (f32[2,528,128]{2,1,0:T(8,128)}, f32[2,528,128]{2,1,0:T(8,128)}, u32[]{:S(2)}, u32[]{:S(2)}) collective-permute-start(f32[2,528,128]{2,1,0:T(8,128)} %get-tuple-element.62), channel_id=1, source_target_pairs={{0,8},{1,9},{2,10},{3,11},{4,12},{5,13},{6,14},{7,15},{8,0},{9,1},... | collective-permute-start | bytes 1622024 | tf_op jit(solution)/shard_map/ppermute | solution.py:885
  151.7 46.9 %collective-permute-start.38 = (f32[2,528,128]{2,1,0:T(8,128)}, f32[2,528,128]{2,1,0:T(8,128)}, u32[]{:S(2)}, u32[]{:S(2)}) collective-permute-start(f32[2,528,128]{2,1,0:T(8,128)} %get-tuple-element.63), channel_id=1, source_target_pairs={{0,12},{1,13},{2,14},{3,15},{4,8},{5,9},{6,10},{7,11},{8,4},{9,5},... | collective-permute-start | bytes 1622024 | tf_op jit(solution)/shard_map/ppermute | solution.py:885
  187.2 15.2 %copy-start.5 = (bf16[2,256,256]{2,1,0:T(8,128)(2,1)S(1)}, bf16[2,256,256]{2,1,0:T(8,128)(2,1)}, u32[]{:S(2)}) copy-start(bf16[2,256,256]{2,1,0:T(8,128)(2,1)} %constant.186.clone.back) | copy-start | bytes 786436
  188.6 9.9 %collective-permute-start.32 = (f32[2,64,512]{2,1,0:T(8,128)S(1)}, f32[2,64,512]{2,1,0:T(8,128)S(1)}, u32[]{:S(2)}, u32[]{:S(2)}) collective-permute-start(f32[2,64,512]{2,1,0:T(8,128)S(1)} %dynamic-slice_bitcast_fusion), channel_id=1, source_target_pairs={{0,16},{16,0},{1,17},{17,1},{2,18},{18,2},{3,19},{19,3},{4,20},{20... | collective-permute-start | bytes 786440 | tf_op jit(solution)/shard_map/ppermute | solution.py:897
  190.2 12.1 %collective-permute-start.34 = (f32[2,528,128]{2,1,0:T(8,128)S(1)}, f32[2,528,128]{2,1,0:T(8,128)S(1)}, u32[]{:S(2)}, u32[]{:S(2)}) collective-permute-start(f32[2,528,128]{2,1,0:T(8,128)S(1)} %get-tuple-element.61.refs_0_), channel_id=1, source_target_pairs={{0,1},{1,0},{2,3},{3,2},{4,5},{5,4},{6,7},{7,6},{8,9},{9,8},{10,11... | collective-permute-start | bytes 1622024 | tf_op jit(solution)/shard_map/ppermute | solution.py:885
  190.2 12.1 %collective-permute-start.35 = (f32[2,528,128]{2,1,0:T(8,128)}, f32[2,528,128]{2,1,0:T(8,128)S(1)}, u32[]{:S(2)}, u32[]{:S(2)}) collective-permute-start(f32[2,528,128]{2,1,0:T(8,128)} %collective-permute-done.31.refs_2_), channel_id=1, source_target_pairs={{0,1},{1,0},{2,3},{3,2},{4,5},{5,4},{6,7},{7,6},{8,9},{9,8},{10,11... | collective-permute-start | bytes 1622024 | tf_op jit(solution)/shard_map/ppermute | solution.py:885
  190.7 11.6 %collective-permute-start.37 = (f32[2,528,128]{2,1,0:T(8,128)}, f32[2,528,128]{2,1,0:T(8,128)}, u32[]{:S(2)}, u32[]{:S(2)}) collective-permute-start(f32[2,528,128]{2,1,0:T(8,128)} %collective-permute-done.36.refs_4_), channel_id=1, source_target_pairs={{0,1},{1,0},{2,3},{3,2},{4,5},{5,4},{6,7},{7,6},{8,9},{9,8},{10,11... | collective-permute-start | bytes 1622024 | tf_op jit(solution)/shard_map/ppermute | solution.py:885
  198.5 3.8 %collective-permute-start.39 = (f32[2,528,128]{2,1,0:T(8,128)}, f32[2,528,128]{2,1,0:T(8,128)}, u32[]{:S(2)}, u32[]{:S(2)}) collective-permute-start(f32[2,528,128]{2,1,0:T(8,128)} %collective-permute-done.38.refs_6_), channel_id=1, source_target_pairs={{0,1},{1,0},{2,3},{3,2},{4,5},{5,4},{6,7},{7,6},{8,9},{9,8},{10,11... | collective-permute-start | bytes 1622024 | tf_op jit(solution)/shard_map/ppermute | solution.py:885
  198.6 11.7 %collective-permute-start.33 = (f32[64,512]{1,0:T(8,128)S(1)}, f32[64,512]{1,0:T(8,128)S(1)}, u32[]{:S(2)}, u32[]{:S(2)}) collective-permute-start(f32[64,512]{1,0:T(8,128)S(1)} %dynamic-slice_bitcast_fusion.1), channel_id=1, source_target_pairs={{0,8},{1,9},{2,10},{3,11},{4,12},{5,13},{6,14},{7,15},{8,0},{9,1},... | collective-permute-start | bytes 393224 | tf_op jit(solution)/shard_map/ppermute | solution.py:885
  208.8 5.7 %collective-permute-start.40 = (f32[64,512]{1,0:T(8,128)S(1)}, f32[64,512]{1,0:T(8,128)S(1)}, u32[]{:S(2)}, u32[]{:S(2)}) collective-permute-start(f32[64,512]{1,0:T(8,128)S(1)} %constant_dynamic-slice_fusion), channel_id=1, source_target_pairs={{0,16},{16,0},{1,17},{17,1},{2,18},{18,2},{3,19},{19,3},{4,20},{20... | collective-permute-start | bytes 393224 | tf_op jit(solution)/shard_map/ppermute | solution.py:897
  (9 other events, 25.0 us)

commit v4 on v3

--- a/solution.py
+++ b/solution.py
@@ -194,7 +194,7 @@
             )
             return carry
 
-        lax.fori_loop(0, rows // ROWS, chunk, 0)
+        lax.fori_loop(0, rows // ROWS, chunk, 0, unroll=True)
         for slot, start in ((0, core * half), (1, (1 - core) * half)):
             h = high[e, pl.ds(start, half)].reshape(half * rows, 2 * LANES)
             l = low[e, pl.ds(start, half)].reshape(half * rows, 2 * LANES)
@@ -744,8 +744,8 @@
 
 
 def last_kernel(groups, rows, ids, angulars, back, twist, speed, beside, *refs):
-    source, receiver, image, data, field, edge, turns, sems = refs[-8:]
-    pieces = refs[:-8]
+    source_out, receiver_out, image, source, receiver, data, field, edge, turns, sems = refs[-10:]
+    pieces = refs[:-10]
     z, core = ids[0], ids[2]
     radix = twist.shape[1]
     half = radix // 2
@@ -769,10 +769,11 @@
             pair = slice(2 * g, 2 * g + 2)
             edge[0, a, pair, :] = real[a][pair] * c - imag[a][pair] * s
             edge[1, a, pair, :] = real[a][pair] * s + imag[a][pair] * c
+    leaving = []
     for number in range(groups // 2):
         for a in range(radix):
             turns[0, a], turns[1, a], turns[2, a] = correction(speed[:, lanes(a)], angulars[number], 1.0)
-        for which, out in ((0, source), (1, receiver)):
+        for which, out, home in ((0, source, source_out), (1, receiver, receiver_out)):
             sign = 2.0 * which - 1.0
             g = 2 * number + which
             real, imag = inverse_tiles(
@@ -796,12 +797,14 @@
                 sign,
                 store,
             )
+            leaving += copies((out.at[:, number], home.at[:, number]))
     for a in range(radix):
         total = jnp.zeros((rows, LANES), F32)
         for number in range(groups // 2):
             for part in (0, 1):
                 total = total + source[part, number, :, lanes(a)] * receiver[part, number, :, lanes(a)]
         image[:, lanes(a)] = total
+    done(leaving)
 
 
 def last(ids, angulars, speed, beside, pieces, tab, groups):
@@ -813,13 +816,15 @@
         "last",
         (out, out, jax.ShapeDtypeStruct((rows, width), F32)),
         [SMEM] * 2 + [VMEM] * 4 + [ANY] * (2 * groups),
-        (VMEM,) * 3,
+        (ANY, ANY, VMEM),
         [
+            pltpu.VMEM(out.shape, F32),
+            pltpu.VMEM(out.shape, F32),
             pltpu.VMEM((groups, 2, radix * rows + 2 * radix, LANES), F32),
             pltpu.VMEM((2, radix, rows, LANES), F32),
             pltpu.VMEM((2, radix, 2 * groups, LANES), F32),
             pltpu.VMEM((3, radix, rows, LANES), F32),
-            pltpu.SemaphoreType.DMA((2 * groups,)),
+            pltpu.SemaphoreType.DMA((3 * groups,)),
         ],
         12,
         8000000000,

time: 215 us -> 215 us (level)
  no operation moved by 1% of the time
where the time goes in v4:
time: 215 us
  waiting for transfers between devices  107 us (50%)
  Pallas kernels  49.2 us (23%)
  starting transfers between devices  43.3 us (20%)
  other arithmetic  10.4 us (5%)
  local copies, waits for them, and re-layouts  2.61 us (1%)
  between operations  2.57 us (1%)
    ppermute x38, waiting for transfers between devices, swap(): return lax.ppermute(value, 'strip', [(i, i ^ bit) for i in range(strips)])  103 us
    pallas_call x6, Pallas kernels, call(): pl.pallas_call(kernel, out_shape=out_shape, in_specs=in_specs, out_specs=...  49.2 us
    ppermute x38, starting transfers between devices, swap(): return lax.ppermute(value, 'strip', [(i, i ^ bit) for i in range(strips)])  38.6 us
    ppermute x3, starting transfers between devices, ahead_plane(): lax.ppermute(value, 'freq', [(i, (i + k) % planes) for i in range(planes)])  4.69 us
    mul x1, other arithmetic, column_filter(): imag = jnp.where(travel, ratio * radius, 0.0) * (sign * scale)  4.39 us
  transfers between devices with their start and end apart: 41, of which 15 were waited for; matrix products, arithmetic and copies ran while one was open for 5% of the time, Pallas kernels for 14%

profile of v4, /device:TPU:0, one launch (start us, length us, event | category | flops | bytes accessed | tf_op | source)
XLA Modules:
  0.0 214.9 jit_solution(9943159640987314039)
XLA Ops:
  0.7 0.6 pad_add_fusion.ids
  1.3 5.1 %first_transform.1 = (f32[1024,128]{1,0:T(8,128)}, f32[1024,128]{1,0:T(8,128)}, f32[1024,128]{1,0:T(8,128)}, f32[512,128]{1,0:T(8,128)}, f32[512,128]{1,0:T(8,128)}) custom-call(s32[4]{0:T(128)} %pad_add_fusion.ids, f32[2,2,64,1024]{3,2,1,0:T(8,128)} %source.1, f32[2,2,64,1024]{3,2,1,0:T(8,128)} %receiver.1, ...), custom_call_target="tpu_custom_call" | custom-call | flops 4000000000 | bytes 4000000 | tf_op jit(solution)/shard_map/first_transform/pallas_call | solution.py:157
  6.4 3.1 %collective-permute-start.4 = (f32[1024,128]{1,0:T(8,128)}, f32[1024,128]{1,0:T(8,128)S(1)}, u32[]{:S(2)}, u32[]{:S(2)}) collective-permute-start(f32[1024,128]{1,0:T(8,128)} %get-tuple-element.36), channel_id=1, source_target_pairs={{0,4},{1,5},{2,6},{3,7},{4,0},{5,1},{6,2},{7,3},{8,12},{9,13},{10,... | collective-permute-start | bytes 1572872 | tf_op jit(solution)/shard_map/ppermute | solution.py:890
  9.5 1.5 collective-permute-start.5
  11.0 2.6 %collective-permute-start.7 = (f32[1024,128]{1,0:T(8,128)}, f32[1024,128]{1,0:T(8,128)S(1)}, u32[]{:S(2)}, u32[]{:S(2)}) collective-permute-start(f32[1024,128]{1,0:T(8,128)} %get-tuple-element.41), channel_id=1, source_target_pairs={{0,8},{1,9},{2,10},{3,11},{4,12},{5,13},{6,14},{7,15},{8,0},{9,1},... | collective-permute-start | bytes 1572872 | tf_op jit(solution)/shard_map/ppermute | solution.py:890
  13.6 16.7 %collective-permute-done.4.refs_4_ = f32[1024,128]{1,0:T(8,128)S(1)} collective-permute-done((f32[1024,128]{1,0:T(8,128)}, f32[1024,128]{1,0:T(8,128)S(1)}, u32[]{:S(2)}, u32[]{:S(2)}) %collective-permute-start.4) | collective-permute-done | bytes 524320 | tf_op jit(solution)/shard_map/ppermute | solution.py:890
  30.3 2.7 %collective-permute-start.8 = (f32[1024,128]{1,0:T(8,128)S(1)}, f32[1024,128]{1,0:T(8,128)S(1)}, u32[]{:S(2)}, u32[]{:S(2)}) collective-permute-start(f32[1024,128]{1,0:T(8,128)S(1)} %collective-permute-done.4.refs_4_), channel_id=1, source_target_pairs={{0,2},{1,3},{2,0},{3,1},{4,6},{5,7},{6,4},{7,5},{8,10},{9,11},{10,... | collective-permute-start | bytes 1572872 | tf_op jit(solution)/shard_map/ppermute | solution.py:890
  33.1 0.1 fusion.12
  33.1 4.6 %collective-permute-done.7.refs_8_ = f32[1024,128]{1,0:T(8,128)S(1)} collective-permute-done((f32[1024,128]{1,0:T(8,128)}, f32[1024,128]{1,0:T(8,128)S(1)}, u32[]{:S(2)}, u32[]{:S(2)}) %collective-permute-start.7) | collective-permute-done | bytes 524320 | tf_op jit(solution)/shard_map/ppermute | solution.py:890
  37.7 0.5 collective-permute-start.20
  38.2 2.5 %collective-permute-start.6 = (f32[512,128]{1,0:T(8,128)}, f32[512,128]{1,0:T(8,128)S(1)}, u32[]{:S(2)}, u32[]{:S(2)}) collective-permute-start(f32[512,128]{1,0:T(8,128)} %get-tuple-element.39), channel_id=1, source_target_pairs={{0,12},{1,13},{2,14},{3,15},{4,8},{5,9},{6,10},{7,11},{8,4},{9,5},... | collective-permute-start | bytes 786440 | tf_op jit(solution)/shard_map/ppermute | solution.py:890
  40.7 5.1 %collective-permute-done.8.refs_6_ = f32[1024,128]{1,0:T(8,128)S(1)} collective-permute-done((f32[1024,128]{1,0:T(8,128)S(1)}, f32[1024,128]{1,0:T(8,128)S(1)}, u32[]{:S(2)}, u32[]{:S(2)}) %collective-permute-start.8) | collective-permute-done | bytes 524320 | tf_op jit(solution)/shard_map/ppermute | solution.py:890
  45.8 4.4 %select_multiply_fusion = (f32[4,8,128,128]{3,2,1,0:T(8,128)}, f32[4,8,128,128]{3,2,1,0:T(8,128)}) fusion(f32[]{:T(128)S(6)} %mul.153, f32[4,128]{1,0:T(4,128)S(1)} %fusion.12, f32[8,128]{1,0:T(8,128)S(1)} %fusion.9, f32[]{:T(128)S(6)} %mul.130), kind=kLoop, calls=%fused_computation | loop fusion | flops 13107200 | bytes 4200456 | tf_op jit(solution)/shard_map/mul | solution.py:869
  50.2 2.5 %collective-permute-start.9 = (f32[512,128]{1,0:T(8,128)S(1)}, f32[512,128]{1,0:T(8,128)S(1)}, u32[]{:S(2)}, u32[]{:S(2)}) collective-permute-start(f32[512,128]{1,0:T(8,128)S(1)} %copy-done.27), channel_id=1, source_target_pairs={{0,12},{1,13},{2,14},{3,15},{4,8},{5,9},{6,10},{7,11},{8,4},{9,5},... | collective-permute-start | bytes 786440 | tf_op jit(solution)/shard_map/ppermute | solution.py:890
  52.8 2.0 collective-permute-start.24
  54.8 1.6 collective-permute-start
  56.4 4.5 %collective-permute-done.9.refs_13_ = f32[512,128]{1,0:T(8,128)S(1)} collective-permute-done((f32[512,128]{1,0:T(8,128)S(1)}, f32[512,128]{1,0:T(8,128)S(1)}, u32[]{:S(2)}, u32[]{:S(2)}) %collective-permute-start.9) | collective-permute-done | bytes 262176 | tf_op jit(solution)/shard_map/ppermute | solution.py:890
  60.9 0.6 collective-permute-done.24.refs_16_
  61.5 1.7 collective-permute-start.25
  63.3 0.6 fusion.13
  65.3 0.1 pad.15.clone
  65.4 0.5 collective-permute-start.21
  65.9 0.1 fusion.2
  66.0 0.1 collective-permute-start.26
  66.1 0.4 collective-permute-start.23
  66.5 2.9 %collective-permute-done.25.refs_17_ = f32[512,128]{1,0:T(8,128)S(1)} collective-permute-done((f32[512,128]{1,0:T(8,128)S(1)}, f32[512,128]{1,0:T(8,128)S(1)}, u32[]{:S(2)}, u32[]{:S(2)}) %collective-permute-start.25) | collective-permute-done | bytes 262176 | tf_op jit(solution)/shard_map/ppermute | solution.py:890
  69.6 0.1 maximum_bitcast_fusion
  69.7 4.2 %collective-permute-start.1 = (f32[1,8,72,128]{3,2,1,0:T(8,128)S(1)}, f32[1,8,72,128]{3,2,1,0:T(8,128)S(1)}, u32[]{:S(2)}, u32[]{:S(2)}) collective-permute-start(f32[1,8,72,128]{3,2,1,0:T(8,128)S(1)} %maximum_bitcast_fusion), channel_id=1, source_target_pairs={{0,8},{1,9},{2,10},{3,11},{4,12},{5,13},{6,14},{7,15},{8,0},{9,1},... | collective-permute-start | bytes 884744 | tf_op jit(solution)/shard_map/ppermute | solution.py:890
  74.0 0.7 copy-done.22
  74.8 0.1 copy-done.30
  74.9 0.7 copy-done.31
  75.6 11.6 %enter_columns.1 = (f32[8,528,128]{2,1,0:T(8,128)}, f32[8,528,128]{2,1,0:T(8,128)}) custom-call(s32[4]{0:T(128)} %pad_add_fusion.ids, f32[4,8,128,128]{3,2,1,0:T(8,128)} %get-tuple-element.72.filt_re, f32[4,8,128,128]{3,2,1,0:T(8,128)} %get-tuple-element.71.filt_im, bf16[512,256]{1,0:T(8,128)(2,1)} %constant.187.clone.ahead, ...), custom_call_target="tpu_custom_call" | custom-call | flops 8000000000 | bytes 8000000 | tf_op jit(solution)/shard_map/enter_columns/pallas_call | solution.py:157
  87.2 0.5 collective-permute-start.28
  87.7 0.3 collective-permute-done.1
  88.1 1.8 collective-permute-start.3
  89.9 13.5 %collective-permute-done.2.refs_1_ = f32[2,8,72,128]{3,2,1,0:T(8,128)S(1)} collective-permute-done((f32[2,8,72,128]{3,2,1,0:T(8,128)S(1)}, f32[2,8,72,128]{3,2,1,0:T(8,128)S(1)}, u32[]{:S(2)}, u32[]{:S(2)}) %collective-permute-start.2) | collective-permute-done | bytes 589856 | tf_op jit(solution)/shard_map/ppermute | solution.py:890
  103.3 1.7 collective-permute-start.10
  105.1 0.7 pad_maximum_fusion.3
  105.8 0.7 pad_maximum_fusion.4
  106.5 0.5 collective-permute-start.12
  107.0 0.7 pad_maximum_fusion.5
  107.7 10.0 %collective-permute-done.10.refs_3_ = f32[2,8,72,128]{3,2,1,0:T(8,128)S(1)} collective-permute-done((f32[2,8,72,128]{3,2,1,0:T(8,128)S(1)}, f32[2,8,72,128]{3,2,1,0:T(8,128)S(1)}, u32[]{:S(2)}, u32[]{:S(2)}) %collective-permute-start.10) | collective-permute-done | bytes 589856 | tf_op jit(solution)/shard_map/ppermute | solution.py:890
  117.8 0.7 pad_maximum_fusion.6
  118.6 1.5 collective-permute-done.14.refs_7_
  120.1 3.6 %prepare.1 = (f32[8,8,64,128]{3,2,1,0:T(8,128)S(1)}, f32[8,8,64,128]{3,2,1,0:T(8,128)S(1)}, f32[8,8,64,128]{3,2,1,0:T(8,128)S(1)}, f32[8,16,128]{2,1,0:T(8,128)S...) custom-call(s32[4]{0:T(128)S(1)} %copy-done.2, f32[2]{0:T(128)S(1)} %pad_maximum_fusion.7.scales, ...), custom_call_target="tpu_custom_call" | custom-call | flops 4000000000 | bytes 8000000 | tf_op jit(solution)/shard_map/prepare/pallas_call | solution.py:157
  123.9 13.9 %middle.1 = (f32[8,512,128]{2,1,0:T(8,128)S(1)}, f32[8,512,128]{2,1,0:T(8,128)S(1)}, f32[2,2,64,1024]{3,2,1,0:T(8,128)S(1)}, f32[2,2,64,1024]{3,2,1,0:T(8,128)S(1)}) custom-call(s32[4]{0:T(128)S(1)} %copy-done.2, bf16[2,256,256]{2,1,0:T(8,128)(2,1)S(1)} %copy-done.4, bf16[2,256,256]{2,1,0:T(8,128)(2,1)S(1)} %copy-done.8, f32[2,8,1,128]{3,2,1,0:T(1,128)S(1)} %copy-done.9, ...), custom_call_target="tpu_custom_call" | custom-call | flops 16000000000 | bytes 10000000 | tf_op jit(solution)/shard_map/middle/pallas_call | solution.py:157
  137.8 0.2 collective-permute-start.30
  138.0 0.6 collective-permute-start.29
  138.6 3.4 %collective-permute-done.30.other = f32[8,512,128]{2,1,0:T(8,128)S(1)} collective-permute-done((f32[8,512,128]{2,1,0:T(8,128)S(1)}, f32[8,512,128]{2,1,0:T(8,128)S(1)}, u32[]{:S(2)}, u32[]{:S(2)}) %collective-permute-start.30) | collective-permute-done | bytes 2097184 | tf_op jit(solution)/shard_map/ppermute | solution.py:890
  142.1 8.7 %leave_columns.1 = (f32[2,528,128]{2,1,0:T(8,128)S(1)}, f32[2,528,128]{2,1,0:T(8,128)}, f32[2,528,128]{2,1,0:T(8,128)}, f32[2,528,128]{2,1,0:T(8,128)}) custom-call(s32[4]{0:T(128)S(1)} %copy-done.2, f32[4,8,128,128]{3,2,1,0:T(8,128)S(1)} %copy-done.1, f32[4,8,128,128]{3,2,1,0:T(8,128)S(1)} %copy-done, bf16[512,256]{1,0:T(8,128)(2,1)S(1)} %copy-done.6, ...), custom_call_target="tpu_custom_call" | custom-call | flops 8000000000 | bytes 8000000 | tf_op jit(solution)/shard_map/leave_columns/pallas_call | solution.py:157
  150.7 0.7 collective-permute-start.31
  151.4 0.1 collective-permute-start.36
  151.6 3.6 %collective-permute-start.38 = (f32[2,528,128]{2,1,0:T(8,128)}, f32[2,528,128]{2,1,0:T(8,128)}, u32[]{:S(2)}, u32[]{:S(2)}) collective-permute-start(f32[2,528,128]{2,1,0:T(8,128)} %get-tuple-element.63), channel_id=1, source_target_pairs={{0,12},{1,13},{2,14},{3,15},{4,8},{5,9},{6,10},{7,11},{8,4},{9,5},... | collective-permute-start | bytes 1622024 | tf_op jit(solution)/shard_map/ppermute | solution.py:890
  155.2 20.5 %collective-permute-done.29 = f32[2,2,64,1024]{3,2,1,0:T(8,128)} collective-permute-done((f32[2,2,64,1024]{3,2,1,0:T(8,128)S(1)}, f32[2,2,64,1024]{3,2,1,0:T(8,128)}, u32[]{:S(2)}, u32[]{:S(2)}) %collective-permute-start.29) | collective-permute-done | bytes 1048608 | tf_op jit(solution)/shard_map/ppermute | solution.py:890
  175.7 11.5 %collective-permute-done.31.refs_2_ = f32[2,528,128]{2,1,0:T(8,128)} collective-permute-done((f32[2,528,128]{2,1,0:T(8,128)}, f32[2,528,128]{2,1,0:T(8,128)}, u32[]{:S(2)}, u32[]{:S(2)}) %collective-permute-start.31) | collective-permute-done | bytes 540704 | tf_op jit(solution)/shard_map/ppermute | solution.py:890
  187.1 1.4 multiply_add_fusion
  188.6 1.6 collective-permute-start.32
  190.1 0.5 collective-permute-start.35
  190.7 7.8 %collective-permute-done.38.refs_6_ = f32[2,528,128]{2,1,0:T(8,128)} collective-permute-done((f32[2,528,128]{2,1,0:T(8,128)}, f32[2,528,128]{2,1,0:T(8,128)}, u32[]{:S(2)}, u32[]{:S(2)}) %collective-permute-start.38) | collective-permute-done | bytes 540704 | tf_op jit(solution)/shard_map/ppermute | solution.py:890
  198.5 3.7 %collective-permute-start.33 = (f32[64,512]{1,0:T(8,128)S(1)}, f32[64,512]{1,0:T(8,128)S(1)}, u32[]{:S(2)}, u32[]{:S(2)}) collective-permute-start(f32[64,512]{1,0:T(8,128)S(1)} %dynamic-slice_bitcast_fusion.1), channel_id=1, source_target_pairs={{0,8},{1,9},{2,10},{3,11},{4,12},{5,13},{6,14},{7,15},{8,0},{9,1},... | collective-permute-start | bytes 393224 | tf_op jit(solution)/shard_map/ppermute | solution.py:890
  202.2 6.3 %last.1 = (f32[2,2,64,1024]{3,2,1,0:T(8,128)}, f32[2,2,64,1024]{3,2,1,0:T(8,128)}, f32[64,1024]{1,0:T(8,128)S(1)}) custom-call(s32[4]{0:T(128)S(1)} %copy-done.2, f32[2]{0:T(128)S(1)} %convert_multiply_fusion.angulars, bf16[2,256,256]{2,1,0:T(8,128)(2,1)S(1)} %copy-done.5, f32[2,8,1,128]{3,2,1,0:T(1,128)S(1)} %copy-done.9, f32[64,1024]{1,0:T(8,128)S(1)} %bitcast.38, ...), custom_call_target="tpu_custom_call" | custom-call | flops 8000000000 | bytes 8000000 | tf_op jit(solution)/shard_map/last/pallas_call | solution.py:157
  208.5 1.6 collective-permute-start.40
  210.1 4.1 %collective-permute-done.40 = f32[64,512]{1,0:T(8,128)S(1)} collective-permute-done((f32[64,512]{1,0:T(8,128)S(1)}, f32[64,512]{1,0:T(8,128)S(1)}, u32[]{:S(2)}, u32[]{:S(2)}) %collective-permute-start.40) | collective-permute-done | bytes 131104 | tf_op jit(solution)/shard_map/ppermute | solution.py:902
  214.2 0.7 pad_maximum_fusion.2
  (125 shorter events, 0.9 us)
Async XLA Ops:
  6.4 23.9 %collective-permute-start.4 = (f32[1024,128]{1,0:T(8,128)}, f32[1024,128]{1,0:T(8,128)S(1)}, u32[]{:S(2)}, u32[]{:S(2)}) collective-permute-start(f32[1024,128]{1,0:T(8,128)} %get-tuple-element.36), channel_id=1, source_target_pairs={{0,4},{1,5},{2,6},{3,7},{4,0},{5,1},{6,2},{7,3},{8,12},{9,13},{10,... | collective-permute-start | bytes 1572872 | tf_op jit(solution)/shard_map/ppermute | solution.py:890
  9.5 23.5 %collective-permute-start.5 = (f32[1024,128]{1,0:T(8,128)}, f32[1024,128]{1,0:T(8,128)S(1)}, u32[]{:S(2)}, u32[]{:S(2)}) collective-permute-start(f32[1024,128]{1,0:T(8,128)} %get-tuple-element.38.refs_0_), channel_id=1, source_target_pairs={{0,2},{1,3},{2,0},{3,1},{4,6},{5,7},{6,4},{7,5},{8,10},{9,11},{10,... | collective-permute-start | bytes 1572872 | tf_op jit(solution)/shard_map/ppermute | solution.py:890
  11.0 29.7 %collective-permute-start.15 = (f32[1024,128]{1,0:T(8,128)}, f32[1024,128]{1,0:T(8,128)S(1)}, u32[]{:S(2)}, u32[]{:S(2)}) collective-permute-start(f32[1024,128]{1,0:T(8,128)} %get-tuple-element.38.refs_0_), channel_id=1, source_target_pairs={{0,1},{1,0},{2,3},{3,2},{4,5},{5,4},{6,7},{7,6},{8,9},{9,8},{10,11... | collective-permute-start | bytes 1572872 | tf_op jit(solution)/shard_map/ppermute | solution.py:890
  11.0 26.7 %collective-permute-start.7 = (f32[1024,128]{1,0:T(8,128)}, f32[1024,128]{1,0:T(8,128)S(1)}, u32[]{:S(2)}, u32[]{:S(2)}) collective-permute-start(f32[1024,128]{1,0:T(8,128)} %get-tuple-element.41), channel_id=1, source_target_pairs={{0,8},{1,9},{2,10},{3,11},{4,12},{5,13},{6,14},{7,15},{8,0},{9,1},... | collective-permute-start | bytes 1572872 | tf_op jit(solution)/shard_map/ppermute | solution.py:890
  30.2 19.9 %copy-start.13 = (f32[1024,128]{1,0:T(8,128)}, f32[1024,128]{1,0:T(8,128)S(1)}, u32[]{:S(2)}) copy-start(f32[1024,128]{1,0:T(8,128)S(1)} %collective-permute-done.4.refs_4_) | copy-start | bytes 1572868
  30.3 15.5 %collective-permute-start.8 = (f32[1024,128]{1,0:T(8,128)S(1)}, f32[1024,128]{1,0:T(8,128)S(1)}, u32[]{:S(2)}, u32[]{:S(2)}) collective-permute-start(f32[1024,128]{1,0:T(8,128)S(1)} %collective-permute-done.4.refs_4_), channel_id=1, source_target_pairs={{0,2},{1,3},{2,0},{3,1},{4,6},{5,7},{6,4},{7,5},{8,10},{9,11},{10,... | collective-permute-start | bytes 1572872 | tf_op jit(solution)/shard_map/ppermute | solution.py:890
  33.0 17.2 %copy-start.14 = (f32[1024,128]{1,0:T(8,128)}, f32[1024,128]{1,0:T(8,128)S(1)}, u32[]{:S(2)}) copy-start(f32[1024,128]{1,0:T(8,128)S(1)} %collective-permute-done.5.refs_2_) | copy-start | bytes 1572868
  33.0 19.8 %collective-permute-start.16 = (f32[1024,128]{1,0:T(8,128)S(1)}, f32[1024,128]{1,0:T(8,128)}, u32[]{:S(2)}, u32[]{:S(2)}) collective-permute-start(f32[1024,128]{1,0:T(8,128)S(1)} %collective-permute-done.5.refs_2_), channel_id=1, source_target_pairs={{0,1},{1,0},{2,3},{3,2},{4,5},{5,4},{6,7},{7,6},{8,9},{9,8},{10,11... | collective-permute-start | bytes 1572872 | tf_op jit(solution)/shard_map/ppermute | solution.py:890
  37.7 27.6 %copy-start.16 = (f32[1024,128]{1,0:T(8,128)}, f32[1024,128]{1,0:T(8,128)S(1)}, u32[]{:S(2)}) copy-start(f32[1024,128]{1,0:T(8,128)S(1)} %collective-permute-done.7.refs_8_) | copy-start | bytes 1572868
  37.7 18.6 %collective-permute-start.20 = (f32[1024,128]{1,0:T(8,128)S(1)}, f32[1024,128]{1,0:T(8,128)S(1)}, u32[]{:S(2)}, u32[]{:S(2)}) collective-permute-start(f32[1024,128]{1,0:T(8,128)S(1)} %collective-permute-done.7.refs_8_), channel_id=1, source_target_pairs={{0,2},{1,3},{2,0},{3,1},{4,6},{5,7},{6,4},{7,5},{8,10},{9,11},{10,... | collective-permute-start | bytes 1572872 | tf_op jit(solution)/shard_map/ppermute | solution.py:890
  38.2 12.0 %copy-start.27 = (f32[512,128]{1,0:T(8,128)S(1)}, f32[512,128]{1,0:T(8,128)}, u32[]{:S(2)}) copy-start(f32[512,128]{1,0:T(8,128)} %get-tuple-element.42) | copy-start | bytes 786436
  38.2 16.6 %copy-start.11 = (f32[1,64,1024]{2,1,0:T(8,128)S(1)}, f32[1,64,1024]{2,1,0:T(8,128)}, u32[]{:S(2)}) copy-start(f32[1,64,1024]{2,1,0:T(8,128)} %param.12) | copy-start | bytes 786436
  38.2 25.0 %copy-start.12 = (s32[2]{0:T(128)S(1)}, s32[2]{0:T(128)}, u32[]{:S(2)}) copy-start(s32[2]{0:T(128)} %param.13) | copy-start | bytes 28
  38.2 12.0 %collective-permute-start.6 = (f32[512,128]{1,0:T(8,128)}, f32[512,128]{1,0:T(8,128)S(1)}, u32[]{:S(2)}, u32[]{:S(2)}) collective-permute-start(f32[512,128]{1,0:T(8,128)} %get-tuple-element.39), channel_id=1, source_target_pairs={{0,12},{1,13},{2,14},{3,15},{4,8},{5,9},{6,10},{7,11},{8,4},{9,5},... | collective-permute-start | bytes 786440 | tf_op jit(solution)/shard_map/ppermute | solution.py:890
  40.7 9.5 %copy-start.15 = (f32[1024,128]{1,0:T(8,128)}, f32[1024,128]{1,0:T(8,128)S(1)}, u32[]{:S(2)}) copy-start(f32[1024,128]{1,0:T(8,128)S(1)} %collective-permute-done.15.refs_1_) | copy-start | bytes 1572868
  40.7 14.1 %collective-permute-start.17 = (f32[1024,128]{1,0:T(8,128)S(1)}, f32[1024,128]{1,0:T(8,128)S(1)}, u32[]{:S(2)}, u32[]{:S(2)}) collective-permute-start(f32[1024,128]{1,0:T(8,128)S(1)} %collective-permute-done.4.refs_4_), channel_id=1, source_target_pairs={{0,1},{1,0},{2,3},{3,2},{4,5},{5,4},{6,7},{7,6},{8,9},{9,8},{10,11... | collective-permute-start | bytes 1572872 | tf_op jit(solution)/shard_map/ppermute | solution.py:890
  45.8 15.1 %collective-permute-start.18 = (f32[1024,128]{1,0:T(8,128)S(1)}, f32[1024,128]{1,0:T(8,128)S(1)}, u32[]{:S(2)}, u32[]{:S(2)}) collective-permute-start(f32[1024,128]{1,0:T(8,128)S(1)} %collective-permute-done.8.refs_6_), channel_id=1, source_target_pairs={{0,1},{1,0},{2,3},{3,2},{4,5},{5,4},{6,7},{7,6},{8,9},{9,8},{10,11... | collective-permute-start | bytes 1572872 | tf_op jit(solution)/shard_map/ppermute | solution.py:890
  50.2 23.8 %copy-start.23 = (f32[512,128]{1,0:T(8,128)}, f32[512,128]{1,0:T(8,128)S(1)}, u32[]{:S(2)}) copy-start(f32[512,128]{1,0:T(8,128)S(1)} %collective-permute-done.6.refs_12_) | copy-start | bytes 786436
  50.2 10.7 %collective-permute-start.9 = (f32[512,128]{1,0:T(8,128)S(1)}, f32[512,128]{1,0:T(8,128)S(1)}, u32[]{:S(2)}, u32[]{:S(2)}) collective-permute-start(f32[512,128]{1,0:T(8,128)S(1)} %copy-done.27), channel_id=1, source_target_pairs={{0,12},{1,13},{2,14},{3,15},{4,8},{5,9},{6,10},{7,11},{8,4},{9,5},... | collective-permute-start | bytes 786440 | tf_op jit(solution)/shard_map/ppermute | solution.py:890
  52.8 8.7 %collective-permute-start.24 = (f32[512,128]{1,0:T(8,128)S(1)}, f32[512,128]{1,0:T(8,128)S(1)}, u32[]{:S(2)}, u32[]{:S(2)}) collective-permute-start(f32[512,128]{1,0:T(8,128)S(1)} %collective-permute-done.6.refs_12_), channel_id=1, source_target_pairs={{0,2},{1,3},{2,0},{3,1},{4,6},{5,7},{6,4},{7,5},{8,10},{9,11},{10,... | collective-permute-start | bytes 786440 | tf_op jit(solution)/shard_map/ppermute | solution.py:890
  54.8 9.1 %copy-start.19 = (f32[1024,128]{1,0:T(8,128)}, f32[1024,128]{1,0:T(8,128)S(1)}, u32[]{:S(2)}) copy-start(f32[1024,128]{1,0:T(8,128)S(1)} %collective-permute-done.17.refs_5_) | copy-start | bytes 1572868
  54.8 11.0 %collective-permute-start = (f32[1,64,1024]{2,1,0:T(8,128)S(1)}, f32[1,64,1024]{2,1,0:T(8,128)S(1)}, u32[]{:S(2)}, u32[]{:S(2)}) collective-permute-start(f32[1,64,1024]{2,1,0:T(8,128)S(1)} %copy-done.11), channel_id=1, source_target_pairs={{0,16},{16,0},{1,17},{17,1},{2,18},{18,2},{3,19},{19,3},{4,20},{20... | collective-permute-start | bytes 786440 | tf_op jit(solution)/shard_map/ppermute | solution.py:902
  56.4 7.5 %copy-start.18 = (f32[1024,128]{1,0:T(8,128)}, f32[1024,128]{1,0:T(8,128)S(1)}, u32[]{:S(2)}) copy-start(f32[1024,128]{1,0:T(8,128)S(1)} %collective-permute-done.20.refs_10_) | copy-start | bytes 1572868
  56.4 9.7 %collective-permute-start.22 = (f32[512,128]{1,0:T(8,128)S(1)}, f32[512,128]{1,0:T(8,128)S(1)}, u32[]{:S(2)}, u32[]{:S(2)}) collective-permute-start(f32[512,128]{1,0:T(8,128)S(1)} %collective-permute-done.6.refs_12_), channel_id=1, source_target_pairs={{0,1},{1,0},{2,3},{3,2},{4,5},{5,4},{6,7},{7,6},{8,9},{9,8},{10,11... | collective-permute-start | bytes 786440 | tf_op jit(solution)/shard_map/ppermute | solution.py:890
  60.9 13.1 %copy-start.24 = (f32[512,128]{1,0:T(8,128)}, f32[512,128]{1,0:T(8,128)S(1)}, u32[]{:S(2)}) copy-start(f32[512,128]{1,0:T(8,128)S(1)} %collective-permute-done.9.refs_13_) | copy-start | bytes 786436
  61.5 12.5 %copy-start.25 = (f32[512,128]{1,0:T(8,128)}, f32[512,128]{1,0:T(8,128)S(1)}, u32[]{:S(2)}) copy-start(f32[512,128]{1,0:T(8,128)S(1)} %collective-permute-done.24.refs_16_) | copy-start | bytes 786436
  61.5 7.9 %collective-permute-start.25 = (f32[512,128]{1,0:T(8,128)S(1)}, f32[512,128]{1,0:T(8,128)S(1)}, u32[]{:S(2)}, u32[]{:S(2)}) collective-permute-start(f32[512,128]{1,0:T(8,128)S(1)} %collective-permute-done.9.refs_13_), channel_id=1, source_target_pairs={{0,2},{1,3},{2,0},{3,1},{4,6},{5,7},{6,4},{7,5},{8,10},{9,11},{10,... | collective-permute-start | bytes 786440 | tf_op jit(solution)/shard_map/ppermute | solution.py:890
  65.3 4.3 %collective-permute-start.19 = (f32[1024,128]{1,0:T(8,128)S(1)}, f32[1024,128]{1,0:T(8,128)S(1)}, u32[]{:S(2)}, u32[]{:S(2)}) collective-permute-start(f32[1024,128]{1,0:T(8,128)S(1)} %collective-permute-done.7.refs_8_), channel_id=1, source_target_pairs={{0,1},{1,0},{2,3},{3,2},{4,5},{5,4},{6,7},{7,6},{8,9},{9,8},{10,11... | collective-permute-start | bytes 1572872 | tf_op jit(solution)/shard_map/ppermute | solution.py:890
  65.4 8.6 %collective-permute-start.21 = (f32[1024,128]{1,0:T(8,128)}, f32[1024,128]{1,0:T(8,128)S(1)}, u32[]{:S(2)}, u32[]{:S(2)}) collective-permute-start(f32[1024,128]{1,0:T(8,128)} %copy-done.18), channel_id=1, source_target_pairs={{0,1},{1,0},{2,3},{3,2},{4,5},{5,4},{6,7},{7,6},{8,9},{9,8},{10,11... | collective-permute-start | bytes 1572872 | tf_op jit(solution)/shard_map/ppermute | solution.py:890
  66.0 8.0 %collective-permute-start.26 = (f32[512,128]{1,0:T(8,128)S(1)}, f32[512,128]{1,0:T(8,128)S(1)}, u32[]{:S(2)}, u32[]{:S(2)}) collective-permute-start(f32[512,128]{1,0:T(8,128)S(1)} %collective-permute-done.24.refs_16_), channel_id=1, source_target_pairs={{0,1},{1,0},{2,3},{3,2},{4,5},{5,4},{6,7},{7,6},{8,9},{9,8},{10,11... | collective-permute-start | bytes 786440 | tf_op jit(solution)/shard_map/ppermute | solution.py:890
  66.1 7.9 %copy-start.26 = (f32[512,128]{1,0:T(8,128)}, f32[512,128]{1,0:T(8,128)S(1)}, u32[]{:S(2)}) copy-start(f32[512,128]{1,0:T(8,128)S(1)} %collective-permute-done.22.refs_14_) | copy-start | bytes 786436
  66.1 7.8 %collective-permute-start.23 = (f32[512,128]{1,0:T(8,128)S(1)}, f32[512,128]{1,0:T(8,128)S(1)}, u32[]{:S(2)}, u32[]{:S(2)}) collective-permute-start(f32[512,128]{1,0:T(8,128)S(1)} %collective-permute-done.9.refs_13_), channel_id=1, source_target_pairs={{0,1},{1,0},{2,3},{3,2},{4,5},{5,4},{6,7},{7,6},{8,9},{9,8},{10,11... | collective-permute-start | bytes 786440 | tf_op jit(solution)/shard_map/ppermute | solution.py:890
  69.4 4.5 %collective-permute-start.27 = (f32[512,128]{1,0:T(8,128)S(1)}, f32[512,128]{1,0:T(8,128)S(1)}, u32[]{:S(2)}, u32[]{:S(2)}) collective-permute-start(f32[512,128]{1,0:T(8,128)S(1)} %collective-permute-done.25.refs_17_), channel_id=1, source_target_pairs={{0,1},{1,0},{2,3},{3,2},{4,5},{5,4},{6,7},{7,6},{8,9},{9,8},{10,11... | collective-permute-start | bytes 786440 | tf_op jit(solution)/shard_map/ppermute | solution.py:890
  69.7 18.2 %collective-permute-start.1 = (f32[1,8,72,128]{3,2,1,0:T(8,128)S(1)}, f32[1,8,72,128]{3,2,1,0:T(8,128)S(1)}, u32[]{:S(2)}, u32[]{:S(2)}) collective-permute-start(f32[1,8,72,128]{3,2,1,0:T(8,128)S(1)} %maximum_bitcast_fusion), channel_id=1, source_target_pairs={{0,8},{1,9},{2,10},{3,11},{4,12},{5,13},{6,14},{7,15},{8,0},{9,1},... | collective-permute-start | bytes 884744 | tf_op jit(solution)/shard_map/ppermute | solution.py:890
  87.2 36.6 %collective-permute-start.28 = (f32[8,528,128]{2,1,0:T(8,128)}, f32[8,528,128]{2,1,0:T(8,128)}, u32[]{:S(2)}, u32[]{:S(2)}) collective-permute-start(f32[8,528,128]{2,1,0:T(8,128)} %get-tuple-element.53), channel_id=1, source_target_pairs={{0,1},{1,0},{2,3},{3,2},{4,5},{5,4},{6,7},{7,6},{8,9},{9,8},{10,11... | collective-permute-start | bytes 6488072 | tf_op jit(solution)/shard_map/ppermute | solution.py:890
  88.0 32.2 %copy-start.2 = (s32[4]{0:T(128)S(1)}, s32[4]{0:T(128)}, u32[]{:S(2)}) copy-start(s32[4]{0:T(128)} %pad_add_fusion.ids) | copy-start | bytes 52
  88.0 15.3 %collective-permute-start.2 = (f32[2,8,72,128]{3,2,1,0:T(8,128)S(1)}, f32[2,8,72,128]{3,2,1,0:T(8,128)S(1)}, u32[]{:S(2)}, u32[]{:S(2)}) collective-permute-start(f32[2,8,72,128]{3,2,1,0:T(8,128)S(1)} %pad_maximum_fusion.refs_0_), channel_id=1, source_target_pairs={{0,4},{1,5},{2,6},{3,7},{4,0},{5,1},{6,2},{7,3},{8,12},{9,13},{10,... | collective-permute-start | bytes 1769480 | tf_op jit(solution)/shard_map/ppermute | solution.py:890
  88.1 18.9 %collective-permute-start.3 = (f32[2,8,72,128]{3,2,1,0:T(8,128)S(1)}, f32[2,8,72,128]{3,2,1,0:T(8,128)S(1)}, u32[]{:S(2)}, u32[]{:S(2)}) collective-permute-start(f32[2,8,72,128]{3,2,1,0:T(8,128)S(1)} %pad_maximum_fusion.refs_0_), channel_id=1, source_target_pairs={{0,2},{1,3},{2,0},{3,1},{4,6},{5,7},{6,4},{7,5},{8,10},{9,11},{10,... | collective-permute-start | bytes 1769480 | tf_op jit(solution)/shard_map/ppermute | solution.py:890
  103.3 14.4 %collective-permute-start.10 = (f32[2,8,72,128]{3,2,1,0:T(8,128)S(1)}, f32[2,8,72,128]{3,2,1,0:T(8,128)S(1)}, u32[]{:S(2)}, u32[]{:S(2)}) collective-permute-start(f32[2,8,72,128]{3,2,1,0:T(8,128)S(1)} %collective-permute-done.2.refs_1_), channel_id=1, source_target_pairs={{0,2},{1,3},{2,0},{3,1},{4,6},{5,7},{6,4},{7,5},{8,10},{9,11},{10,... | collective-permute-start | bytes 1769480 | tf_op jit(solution)/shard_map/ppermute | solution.py:890
  105.8 12.8 %collective-permute-start.11 = (f32[2,8,24,128]{3,2,1,0:T(8,128)}, f32[2,8,24,128]{3,2,1,0:T(8,128)S(1)}, u32[]{:S(2)}, u32[]{:S(2)}) collective-permute-start(f32[2,8,24,128]{3,2,1,0:T(8,128)} %pad_maximum_fusion.3), channel_id=1, source_target_pairs={{0,1},{1,0},{2,3},{3,2},{4,5},{5,4},{6,7},{7,6},{8,9},{9,8},{10,11... | collective-permute-start | bytes 589832 | tf_op jit(solution)/shard_map/ppermute | solution.py:890
  106.5 12.1 %collective-permute-start.12 = (f32[2,8,24,128]{3,2,1,0:T(8,128)}, f32[2,8,24,128]{3,2,1,0:T(8,128)S(1)}, u32[]{:S(2)}, u32[]{:S(2)}) collective-permute-start(f32[2,8,24,128]{3,2,1,0:T(8,128)} %pad_maximum_fusion.4), channel_id=1, source_target_pairs={{0,1},{1,0},{2,3},{3,2},{4,5},{5,4},{6,7},{7,6},{8,9},{9,8},{10,11... | collective-permute-start | bytes 589832 | tf_op jit(solution)/shard_map/ppermute | solution.py:890
  107.7 10.9 %collective-permute-start.13 = (f32[2,8,24,128]{3,2,1,0:T(8,128)}, f32[2,8,24,128]{3,2,1,0:T(8,128)S(1)}, u32[]{:S(2)}, u32[]{:S(2)}) collective-permute-start(f32[2,8,24,128]{3,2,1,0:T(8,128)} %pad_maximum_fusion.5), channel_id=1, source_target_pairs={{0,1},{1,0},{2,3},{3,2},{4,5},{5,4},{6,7},{7,6},{8,9},{9,8},{10,11... | collective-permute-start | bytes 589832 | tf_op jit(solution)/shard_map/ppermute | solution.py:890
  118.5 1.7 collective-permute-start.14
  118.6 5.2 %copy-start.8 = (bf16[2,256,256]{2,1,0:T(8,128)(2,1)S(1)}, bf16[2,256,256]{2,1,0:T(8,128)(2,1)}, u32[]{:S(2)}) copy-start(bf16[2,256,256]{2,1,0:T(8,128)(2,1)} %constant.185.clone.table.ahead) | copy-start | bytes 786436
  118.6 5.2 %copy-start.9 = (f32[2,8,1,128]{3,2,1,0:T(1,128)S(1)}, f32[2,8,1,128]{3,2,1,0:T(1,128)}, u32[]{:S(2)}) copy-start(f32[2,8,1,128]{3,2,1,0:T(1,128)} %constant.189.clone.twist) | copy-start | bytes 24580
  118.6 5.2 %copy-start.10 = (f32[8,528,128]{2,1,0:T(8,128)S(1)}, f32[8,528,128]{2,1,0:T(8,128)}, u32[]{:S(2)}) copy-start(f32[8,528,128]{2,1,0:T(8,128)} %get-tuple-element.52.mine) | copy-start | bytes 6488068
  123.8 18.2 %copy-start = (f32[4,8,128,128]{3,2,1,0:T(8,128)S(1)}, f32[4,8,128,128]{3,2,1,0:T(8,128)}, u32[]{:S(2)}) copy-start(f32[4,8,128,128]{3,2,1,0:T(8,128)} %get-tuple-element.71.filt_im) | copy-start | bytes 6291460
  123.8 18.2 %copy-start.1 = (f32[4,8,128,128]{3,2,1,0:T(8,128)S(1)}, f32[4,8,128,128]{3,2,1,0:T(8,128)}, u32[]{:S(2)}) copy-start(f32[4,8,128,128]{3,2,1,0:T(8,128)} %get-tuple-element.72.filt_re) | copy-start | bytes 6291460
  123.8 18.2 %copy-start.3 = (f32[2,8,128,128]{3,2,1,0:T(8,128)S(1)}, f32[2,8,128,128]{3,2,1,0:T(8,128)}, u32[]{:S(2)}) copy-start(f32[2,8,128,128]{3,2,1,0:T(8,128)} %constant.190.clone.twist) | copy-start | bytes 3145732
  123.8 18.2 %copy-start.6 = (bf16[512,256]{1,0:T(8,128)(2,1)S(1)}, bf16[512,256]{1,0:T(8,128)(2,1)}, u32[]{:S(2)}) copy-start(bf16[512,256]{1,0:T(8,128)(2,1)} %constant.187.clone.ahead) | copy-start | bytes 786436
  123.9 18.2 %copy-start.7 = (bf16[512,256]{1,0:T(8,128)(2,1)S(1)}, bf16[512,256]{1,0:T(8,128)(2,1)}, u32[]{:S(2)}) copy-start(bf16[512,256]{1,0:T(8,128)(2,1)} %constant.188.clone.back) | copy-start | bytes 786436
  137.8 4.2 %collective-permute-start.30 = (f32[8,512,128]{2,1,0:T(8,128)S(1)}, f32[8,512,128]{2,1,0:T(8,128)S(1)}, u32[]{:S(2)}, u32[]{:S(2)}) collective-permute-start(f32[8,512,128]{2,1,0:T(8,128)S(1)} %get-tuple-element.57), channel_id=1, source_target_pairs={{0,1},{1,0},{2,3},{3,2},{4,5},{5,4},{6,7},{7,6},{8,9},{9,8},{10,11... | collective-permute-start | bytes 6291464 | tf_op jit(solution)/shard_map/ppermute | solution.py:890
  138.0 37.7 %collective-permute-start.29 = (f32[2,2,64,1024]{3,2,1,0:T(8,128)S(1)}, f32[2,2,64,1024]{3,2,1,0:T(8,128)}, u32[]{:S(2)}, u32[]{:S(2)}) collective-permute-start(f32[2,2,64,1024]{3,2,1,0:T(8,128)S(1)} %get-tuple-element.55), channel_id=1, source_target_pairs={{0,4},{1,5},{2,6},{3,7},{4,0},{5,1},{6,2},{7,3},{8,12},{9,13},{10,... | collective-permute-start | bytes 3145736 | tf_op jit(solution)/shard_map/ppermute | solution.py:890
  150.7 36.4 %collective-permute-start.31 = (f32[2,528,128]{2,1,0:T(8,128)}, f32[2,528,128]{2,1,0:T(8,128)}, u32[]{:S(2)}, u32[]{:S(2)}) collective-permute-start(f32[2,528,128]{2,1,0:T(8,128)} %get-tuple-element.58), channel_id=1, source_target_pairs={{0,4},{1,5},{2,6},{3,7},{4,0},{5,1},{6,2},{7,3},{8,12},{9,13},{10,... | collective-permute-start | bytes 1622024 | tf_op jit(solution)/shard_map/ppermute | solution.py:890
  151.4 39.2 %collective-permute-start.36 = (f32[2,528,128]{2,1,0:T(8,128)}, f32[2,528,128]{2,1,0:T(8,128)}, u32[]{:S(2)}, u32[]{:S(2)}) collective-permute-start(f32[2,528,128]{2,1,0:T(8,128)} %get-tuple-element.62), channel_id=1, source_target_pairs={{0,8},{1,9},{2,10},{3,11},{4,12},{5,13},{6,14},{7,15},{8,0},{9,1},... | collective-permute-start | bytes 1622024 | tf_op jit(solution)/shard_map/ppermute | solution.py:890
  151.6 46.9 %collective-permute-start.38 = (f32[2,528,128]{2,1,0:T(8,128)}, f32[2,528,128]{2,1,0:T(8,128)}, u32[]{:S(2)}, u32[]{:S(2)}) collective-permute-start(f32[2,528,128]{2,1,0:T(8,128)} %get-tuple-element.63), channel_id=1, source_target_pairs={{0,12},{1,13},{2,14},{3,15},{4,8},{5,9},{6,10},{7,11},{8,4},{9,5},... | collective-permute-start | bytes 1622024 | tf_op jit(solution)/shard_map/ppermute | solution.py:890
  187.1 15.1 %copy-start.5 = (bf16[2,256,256]{2,1,0:T(8,128)(2,1)S(1)}, bf16[2,256,256]{2,1,0:T(8,128)(2,1)}, u32[]{:S(2)}) copy-start(bf16[2,256,256]{2,1,0:T(8,128)(2,1)} %constant.186.clone.back) | copy-start | bytes 786436
  188.6 9.8 %collective-permute-start.32 = (f32[2,64,512]{2,1,0:T(8,128)S(1)}, f32[2,64,512]{2,1,0:T(8,128)S(1)}, u32[]{:S(2)}, u32[]{:S(2)}) collective-permute-start(f32[2,64,512]{2,1,0:T(8,128)S(1)} %dynamic-slice_bitcast_fusion), channel_id=1, source_target_pairs={{0,16},{16,0},{1,17},{17,1},{2,18},{18,2},{3,19},{19,3},{4,20},{20... | collective-permute-start | bytes 786440 | tf_op jit(solution)/shard_map/ppermute | solution.py:902
  190.1 12.0 %collective-permute-start.34 = (f32[2,528,128]{2,1,0:T(8,128)S(1)}, f32[2,528,128]{2,1,0:T(8,128)S(1)}, u32[]{:S(2)}, u32[]{:S(2)}) collective-permute-start(f32[2,528,128]{2,1,0:T(8,128)S(1)} %get-tuple-element.61.refs_0_), channel_id=1, source_target_pairs={{0,1},{1,0},{2,3},{3,2},{4,5},{5,4},{6,7},{7,6},{8,9},{9,8},{10,11... | collective-permute-start | bytes 1622024 | tf_op jit(solution)/shard_map/ppermute | solution.py:890
  190.1 12.0 %collective-permute-start.35 = (f32[2,528,128]{2,1,0:T(8,128)}, f32[2,528,128]{2,1,0:T(8,128)S(1)}, u32[]{:S(2)}, u32[]{:S(2)}) collective-permute-start(f32[2,528,128]{2,1,0:T(8,128)} %collective-permute-done.31.refs_2_), channel_id=1, source_target_pairs={{0,1},{1,0},{2,3},{3,2},{4,5},{5,4},{6,7},{7,6},{8,9},{9,8},{10,11... | collective-permute-start | bytes 1622024 | tf_op jit(solution)/shard_map/ppermute | solution.py:890
  190.7 11.5 %collective-permute-start.37 = (f32[2,528,128]{2,1,0:T(8,128)}, f32[2,528,128]{2,1,0:T(8,128)}, u32[]{:S(2)}, u32[]{:S(2)}) collective-permute-start(f32[2,528,128]{2,1,0:T(8,128)} %collective-permute-done.36.refs_4_), channel_id=1, source_target_pairs={{0,1},{1,0},{2,3},{3,2},{4,5},{5,4},{6,7},{7,6},{8,9},{9,8},{10,11... | collective-permute-start | bytes 1622024 | tf_op jit(solution)/shard_map/ppermute | solution.py:890
  198.4 3.8 %collective-permute-start.39 = (f32[2,528,128]{2,1,0:T(8,128)}, f32[2,528,128]{2,1,0:T(8,128)}, u32[]{:S(2)}, u32[]{:S(2)}) collective-permute-start(f32[2,528,128]{2,1,0:T(8,128)} %collective-permute-done.38.refs_6_), channel_id=1, source_target_pairs={{0,1},{1,0},{2,3},{3,2},{4,5},{5,4},{6,7},{7,6},{8,9},{9,8},{10,11... | collective-permute-start | bytes 1622024 | tf_op jit(solution)/shard_map/ppermute | solution.py:890
  198.5 11.6 %collective-permute-start.33 = (f32[64,512]{1,0:T(8,128)S(1)}, f32[64,512]{1,0:T(8,128)S(1)}, u32[]{:S(2)}, u32[]{:S(2)}) collective-permute-start(f32[64,512]{1,0:T(8,128)S(1)} %dynamic-slice_bitcast_fusion.1), channel_id=1, source_target_pairs={{0,8},{1,9},{2,10},{3,11},{4,12},{5,13},{6,14},{7,15},{8,0},{9,1},... | collective-permute-start | bytes 393224 | tf_op jit(solution)/shard_map/ppermute | solution.py:890
  208.5 5.7 %collective-permute-start.40 = (f32[64,512]{1,0:T(8,128)S(1)}, f32[64,512]{1,0:T(8,128)S(1)}, u32[]{:S(2)}, u32[]{:S(2)}) collective-permute-start(f32[64,512]{1,0:T(8,128)S(1)} %constant_dynamic-slice_fusion), channel_id=1, source_target_pairs={{0,16},{16,0},{1,17},{17,1},{2,18},{18,2},{3,19},{19,3},{4,20},{20... | collective-permute-start | bytes 393224 | tf_op jit(solution)/shard_map/ppermute | solution.py:902
  (9 other events, 24.8 us)
